TPU v7x, 256 devices: a whole 4x4x8 slice. The times are simulated.
256 devices in a mesh: kz: 4 (over y_hi, core), pw: 64 (over x, y_lo, z).
Axes of the slice: x: 4, y: 4 (y_hi: 2, y_lo: 2; y = y_hi * 2 + y_lo), z: 8, core: 2. Of those that a mesh axis runs over, the one named last changes fastest.
Arguments:
- waves: bfloat16 [16, 1, 16384, 2, 256], P('kz', None, 'pw'), may hold values from -1.25 to 1.25
- pw_map: int32 [1, 16384], P(None, 'pw'), may hold values from 0 to 16383, each once within a row
Outputs:
- correlation_plus: float32 [16, 1, 2, 256, 256], P('kz', None, None, 'pw')
- correlation_minus: float32 [16, 1, 2, 256, 256], P('kz', None, None, 'pw')
Inputs may be any that keep to these rules, and one draw needn't show every extreme that they name: Each row of pw_map is a permutation of the 16384 plane waves.
All inputs are finite; a program needn't handle non-finite values.
Results may differ from a plain program's by a relative error of at most 0.0003.
Values may be sent and summed in bfloat16 or wider, within the bound.
No kernel may reach another device: no remote copies, remote signals or barrier semaphores. Data moves between devices by JAX's collectives and lax.ppermute only.
A program may use at most 128 MiB of HBM per device.

v0:
```python
import jax
import jax.numpy as jnp
from jax import lax
from jax.sharding import PartitionSpec as P


def shifted(block, axis, distance):
    devices = range(lax.axis_size(axis))
    route = [((i - distance) % len(devices), i) for i in devices]
    return lax.ppermute(block, axis, route)


def make_term(left, right, count):
    prods = jnp.einsum("kcgpn,kcgqm->nkcpqm", left, right, preferred_element_type=jnp.float32)
    real_part = prods[:, :, :, 0, 0] + prods[:, :, :, 1, 1]
    imag_part = prods[:, :, :, 0, 1] - prods[:, :, :, 1, 0]
    return jnp.stack([real_part, imag_part], axis=3).reshape(count, -1)


def body(waves, pw_map):
    kz_dev, cols, rows, _, bands = waves.shape
    band_rows = bands // lax.axis_size("pw")
    kz_pos = lax.axis_index("kz")
    last_pos = lax.axis_size("kz") - 1
    arriving = shifted(waves[0], "kz", -1)
    source = jnp.where(kz_pos == last_pos, arriving, waves[0])
    piece = lax.all_gather(source, "pw", axis=1, tiled=True)
    count = piece.shape[1]
    inside = (pw_map >= 0) & (pw_map < count)
    index = jnp.clip(pw_map, 0, count - 1)
    values = jnp.take_along_axis(piece.reshape(cols, count, 2 * bands), index[:, :, None], axis=1)
    moved = jnp.where(inside[:, :, None], values, jnp.zeros_like(values))
    moved = moved.reshape(cols, rows, 2, bands)
    boundary = jnp.where(kz_pos == last_pos, moved, arriving)
    upper = jnp.concatenate([waves[1:], boundary[None]], axis=0)
    summed = lax.psum_scatter(
        make_term(waves, upper, band_rows * lax.axis_size("pw")),
        "pw",
        scatter_dimension=0,
        tiled=True,
    )
    correlation_plus = summed.reshape(band_rows, kz_dev, cols, 2, bands).transpose(1, 2, 3, 0, 4)
    leaving = shifted(waves[kz_dev - 1], "kz", 1)
    opening = jnp.where(kz_pos == 0, moved, waves[0])
    left_side = jnp.concatenate([opening[None], waves[1:]], axis=0)
    lower = jnp.concatenate([leaving[None], waves[:-1]], axis=0)
    summed_back = lax.psum_scatter(
        make_term(left_side, lower, band_rows * lax.axis_size("pw")),
        "pw",
        scatter_dimension=0,
        tiled=True,
    )
    correlation_minus = summed_back.reshape(band_rows, kz_dev, cols, 2, bands).transpose(
        1, 2, 3, 0, 4
    )
    return (correlation_plus, correlation_minus)


def solution(mesh):
    placed = (P("kz", None, "pw", None, None), P(None, "pw"))
    return jax.shard_map(
        body,
        mesh=mesh,
        in_specs=placed,
        out_specs=(P("kz", None, None, "pw", None), P("kz", None, None, "pw", None)),
        check_vma=False,
    )
```

profile of v0, /device:TPU:16, one launch (start us, length us, event | category | flops | bytes accessed | tf_op | source)
XLA Modules:
  0.0 1021.0 jit_solution(3574576932487633641)
XLA Ops:
  7.2 0.0 copy-start
  7.2 0.0 copy-start.5
  7.2 0.0 all-gather.2.cloned.1.call-start
  7.2 1.5 fusion.15
  8.7 0.2 copy.67
  8.9 0.0 copy-start.1
  8.9 0.1 collective-permute-start
  9.0 3.9 collective-permute-done
  12.9 0.0 copy-start.3
  12.9 0.8 broadcast_select_fusion
  13.6 0.0 all-gather.2.cloned.1.call-update
  13.7 0.0 all-reduce.5.cloned.1.call-start
  13.7 0.9 copy.70
  14.6 3.2 collective-permute-start.1
  17.9 0.0 copy-done.5
  17.9 0.0 copy-done
  17.9 0.9 fusion.16
  18.8 0.0 copy-done.1
  18.9 0.0 copy-done.3
  18.9 0.6 copy.66
  19.5 0.6 copy.71
  20.1 334.8 %all-gather.2.cloned.1.call-done = bf16[1,16384,2,256]{1,3,2,0:T(8,128)(2,1)} async-done(((bf16[1,256,2,256]{1,3,2,0:T(8,128)(2,1)}), bf16[1,16384,2,256]{1,3,2,0:T(8,128)(2,1)}) %all-gather.2.cloned.1.call-update) | async-done | bytes 16777232 | tf_op jit(solution)/shard_map/all_gather | solution.py:27
  354.9 22.4 %copy.38 = bf16[16384,512]{1,0:T(8,128)(2,1)} copy(bf16[16384,512]{0,1:T(8,128)(2,1)} %bitcast.84) | data formatting | bytes 33554432 | tf_op jit(solution)/shard_map/reshape | solution.py:31
  377.2 0.0 copy-start.2
  377.2 9.2 gather_fusion
  386.4 0.1 copy.39
  386.6 0.0 copy-done.2
  386.6 0.0 collective-permute-done.1
  386.6 1.7 convolution_bitcast_fusion
  388.3 0.1 fusion
  388.5 0.0 copy-start.4
  388.5 0.1 fusion.2
  388.6 0.8 copy-done.4
  389.5 0.7 convolution_bitcast_fusion.1
  390.2 0.1 fusion.3
  390.3 0.1 fusion.5
  390.5 0.1 pad_maximum_fusion.1
  390.6 1.5 copy.52
  392.1 0.1 pad_maximum_fusion
  392.2 1.5 copy.43
  393.7 0.0 copy-start.6
  393.7 0.0 all-reduce.5.cloned.1.call-update
  393.8 0.6 copy-done.6
  394.4 0.6 dynamic-slice
  395.6 614.5 %all-reduce.5.cloned.1.call-done = (f32[256,2048]{0,1:T(8,128)}, f32[256,2048]{0,1:T(8,128)}) async-done(((f32[256,2048]{0,1:T(8,128)}, f32[256,2048]{0,1:T(8,128)}), (f32[256,2048]{0,1:T(8,128)}, f32[256,2048]{0,1:T(8,128)})) %all-reduce.5.cloned.1.call-update) | async-done | bytes 4194320
  1010.1 2.1 constant_dynamic-slice_fusion
  1012.2 0.9 copy.44
  1013.2 0.9 copy.53
  (7 shorter events, 0.1 us)
Async XLA Ops:
  7.2 10.8 %copy-start = (bf16[4,1,256,2,256]{4,3,2,1,0:T(2,128)(2,1)S(1)}, bf16[4,1,256,2,256]{4,3,2,1,0:T(2,128)(2,1)}, u32[]{:S(2)}) copy-start(bf16[4,1,256,2,256]{4,3,2,1,0:T(2,128)(2,1)} %param.2) | copy-start | bytes 3145732
  7.2 10.7 %copy-start.5 = (s32[1,256]{1,0:T(1,128)S(1)}, s32[1,256]{1,0:T(1,128)}, u32[]{:S(2)}) copy-start(s32[1,256]{1,0:T(1,128)} %param.3) | copy-start | bytes 3076
  7.2 347.7 %all-gather.2.cloned.1.call-start = ((), (), s32[]{:S(2)}) async-start(), calls=%async_computation | async-start | bytes 17039360 | tf_op jit(solution)/shard_map/all_gather | solution.py:27
  8.9 10.0 copy-start.1
  8.9 4.0 collective-permute-start
  12.9 6.0 copy-start.3
  13.7 996.4 %all-reduce.5.cloned.1.call-start = ((), (), s32[]{:S(2)}) async-start(), calls=%async_computation.1 | async-start | bytes 8388608
  14.6 372.0 %collective-permute-start.1 = (bf16[1,256,2,256]{1,3,2,0:T(8,128)(2,1)}, bf16[1,256,2,256]{1,3,2,0:T(8,128)(2,1)}, u32[]{:S(2)}, u32[]{:S(2)}) collective-permute-start(bf16[1,256,2,256]{1,3,2,0:T(8,128)(2,1)} %bitcast.20), channel_id=1, source_target_pairs={{192,0},{0,64},{64,128},{128,192},{193,1},{1,65},{65,129},{129,193... | collective-permute-start | bytes 786440 | tf_op jit(solution)/shard_map/ppermute | solution.py:10
  377.2 9.3 copy-start.2
  388.5 1.0 copy-start.4
  393.7 0.7 copy-start.6
Sparse Core Ops, SparseCore 0:
  13.8 341.0 all-gather.1
  393.9 616.1 all-reduce.4
where the time goes:
time: 1020 us
  waiting for transfers between devices  953 us (93%)
  local copies, waits for them, and re-layouts  45.3 us (4%)
  between operations  14.9 us (1%)
    unnamed x3, waiting for transfers between devices  614 us
    all_gather x1, waiting for transfers between devices, body(): piece = lax.all_gather(source, 'pw', axis=1, tiled=True)  335 us
    reshape x1, local copies, waits for them, and re-layouts, body(): piece.reshape(cols, count, 2 * bands)  22.4 us
  transfers between devices with their start and end apart: 4, of which 3 were waited for; matrix products, arithmetic and copies ran while one was open for 3% of the time, Pallas kernels for 0%

commit v1 on v0

v1 whole, which is shorter than its diff:
```python
import jax
import jax.numpy as jnp
import numpy as np
from jax import lax
from jax.experimental import pallas as pl
from jax.experimental.pallas import tpu as pltpu
from jax.sharding import PartitionSpec as P


def pick_kernel(table_ref, hi_ref, lo_ref, out_ref):
    blocks, width = hi_ref.shape
    parts = table_ref.shape[0] // 2
    table = table_ref[...]
    rows = lax.broadcasted_iota(jnp.int32, (table.shape[1], width), 0)
    owners = lax.broadcasted_iota(jnp.int32, (parts, width), 0)

    def step(t, carry):
        base = pl.multiple_of(t * 8, 8)
        his = hi_ref[pl.ds(base, 8), :]
        los = lo_ref[pl.ds(base, 8), :]
        real_rows, imag_rows = [], []
        for r in range(8):
            hot = jnp.where(rows == los[r : r + 1, :], 1.0, 0.0).astype(jnp.bfloat16)
            found = jnp.dot(table, hot, preferred_element_type=jnp.float32)
            mine = owners == his[r : r + 1, :]
            real_rows.append(jnp.sum(jnp.where(mine, found[:parts], 0.0), axis=0, keepdims=True))
            imag_rows.append(jnp.sum(jnp.where(mine, found[parts:], 0.0), axis=0, keepdims=True))
        out_ref[0, pl.ds(base, 8), :] = jnp.concatenate(real_rows, axis=0)
        out_ref[1, pl.ds(base, 8), :] = jnp.concatenate(imag_rows, axis=0)
        return carry

    lax.fori_loop(0, blocks // 8, step, 0)


def pick(table, hi, lo):
    blocks, width = hi.shape
    vmem = pl.BlockSpec(memory_space=pltpu.VMEM)
    return pl.pallas_call(
        pick_kernel,
        out_shape=jax.ShapeDtypeStruct((2, blocks, width), jnp.float32),
        in_specs=[vmem] * 3,
        out_specs=vmem,
        cost_estimate=pl.CostEstimate(
            flops=2 * table.size * blocks * width, bytes_accessed=table.size * 6, transcendentals=0
        ),
        name="pick",
    )(table, hi, lo)


def turned(planes, axis):
    real, imag = jnp.split(planes, 2, axis=axis)
    return jnp.concatenate([imag, -real], axis=axis)


def body(waves, pw_map):
    kz_dev, cols, rows, _, bands = waves.shape
    n_kz, n_pw = lax.axis_size("kz"), lax.axis_size("pw")
    share = bands // n_pw
    kz_pos = lax.axis_index("kz")
    last = n_kz - 1
    planes = waves[:, 0]
    f32, bf16 = jnp.float32, jnp.bfloat16

    def swap(x):
        return lax.all_to_all(x, "pw", 0, 0, tiled=True)

    def sent(x, pairs):
        return lax.ppermute(x, "kz", pairs)

    with jax.named_scope("deal"):
        order = np.arange(bands).reshape(n_pw, share).T.reshape(-1)
        deal = jnp.asarray(np.eye(bands)[order], dtype=bf16)
        dealt = jnp.einsum("qb,gpb->qpg", deal, planes[0], preferred_element_type=f32)
        dealt = dealt.astype(bf16).reshape(share, n_pw, 2, rows)
        mine = jnp.where(kz_pos == 0, dealt[0], jnp.zeros_like(dealt[0]))
        for j in range(1, n_kz):
            mine = mine + sent(dealt[j], [(0, j)])
        digits = jnp.stack([pw_map[0] // rows, pw_map[0] % rows]).astype(bf16)
        load = jnp.concatenate(
            [mine, jnp.broadcast_to(digits[None], (n_pw, 2, rows))], axis=1
        )
        spread = swap(load)
    with jax.named_scope("pick"):
        table = spread[:, :2].transpose(1, 0, 2).reshape(2 * n_pw, rows)
        hi = spread[:, 2].astype(jnp.int32)
        lo = spread[:, 3].astype(jnp.int32)
        picked = pick(table, hi, lo).astype(bf16)
        moved = swap(picked.transpose(1, 0, 2))

    with jax.named_scope("inner"):
        arriving = sent(planes[0], [((i + 1) % n_kz, i) for i in range(n_kz)])
        right = jnp.concatenate([planes[1:], arriving[None]], axis=0)
        both = jnp.stack([right, turned(right, 2)], axis=1)
        terms = jnp.einsum("kgpn,kogpm->nkom", planes, both, preferred_element_type=f32)
        terms = terms.reshape(n_pw, share * kz_dev * 2, bands)
        total = jnp.sum(swap(terms), axis=0).reshape(share, kz_dev, 2, bands)
        plus = total.transpose(1, 2, 0, 3)

    with jax.named_scope("mirror"):
        signs = jnp.array([1.0, -1.0], f32)[None, :, None, None]
        tiles = (plus * signs).reshape(kz_dev, 2, share, n_pw, share)
        tiles = tiles.transpose(3, 0, 1, 4, 2).reshape(n_pw, -1)
        tiles = swap(tiles).reshape(n_pw, kz_dev, 2, share, share)
        minus = tiles.transpose(1, 2, 3, 0, 4).reshape(kz_dev, 2, share, bands)

    with jax.named_scope("edge"):
        final = planes[kz_dev - 1]
        for j in range(last):
            got = sent(planes[kz_dev - 1], [(last, j)])
            final = jnp.where(kz_pos == j, got, final)
        moved_both = jnp.stack([moved, turned(moved, 1)], axis=1)
        rows_n = jnp.einsum("gpn,iopg->noi", final, moved_both, preferred_element_type=f32)
        final_both = jnp.stack([final, turned(final, 1)], axis=0)
        rows_m = jnp.einsum("ipg,ogpn->ion", moved, final_both, preferred_element_type=f32)
        out = jnp.concatenate([rows_n.reshape(n_pw, -1), rows_m.reshape(n_pw, -1)], axis=1)
        edge = jnp.sum(swap(out), axis=0)
        half = edge.shape[0] // 2
        edge_n, edge_m = edge[:half], edge[half:]

    with jax.named_scope("close"):
        edge_ns, edge_ms = [], []
        for j in range(n_kz):
            edge_ns.append(edge_n if j == last else sent(edge_n, [(j, last)]))
            edge_ms.append(edge_m if j == 0 else sent(edge_m, [(j, 0)]))
        last_plus = jnp.stack(edge_ns).reshape(share, share, 2, n_pw)
        last_plus = last_plus.transpose(2, 1, 3, 0).reshape(2, share, bands)
        first_minus = jnp.stack(edge_ms).reshape(share, 2, bands).transpose(1, 0, 2)
        before = sent(minus[kz_dev - 1], [(i, i + 1) for i in range(last)])
        first = jnp.where(kz_pos == 0, first_minus, before)
        plus_end = jnp.where(kz_pos == last, last_plus, plus[kz_dev - 1])
        plus = jnp.concatenate([plus[:-1], plus_end[None]], axis=0)
        minus = jnp.concatenate([first[None], minus[:-1]], axis=0)
    return plus[:, None], minus[:, None]


def solution(mesh):
    return jax.shard_map(
        body,
        mesh=mesh,
        in_specs=(P("kz", None, "pw", None, None), P(None, "pw")),
        out_specs=(P("kz", None, None, "pw", None), P("kz", None, None, "pw", None)),
        check_vma=False,
    )
```

time: 1020 us -> 166 us (0.16)
  the two profiles are of different devices: /device:TPU:16 before, /device:TPU:1 now
where the time goes in v1:
time: 166 us; the launch traced here: 165 us
  starting transfers between devices  83.7 us (50%)
  waiting for transfers between devices  55.3 us (33%)
  local copies, waits for them, and re-layouts  14.4 us (9%)
  Pallas kernels  4.23 us (3%)
  other arithmetic  3.77 us (2%)
  matrix products  2.39 us (1%)
    all_to_all x5, waiting for transfers between devices, swap(): return lax.all_to_all(x, 'pw', 0, 0, tiled=True)  53.3 us
    ppermute x14, starting transfers between devices, sent(): return lax.ppermute(x, 'kz', pairs)  44.9 us
    all_to_all x5, starting transfers between devices, swap(): return lax.all_to_all(x, 'pw', 0, 0, tiled=True)  38.8 us
    pallas_call x1, Pallas kernels, pick(): pl.pallas_call(pick_kernel, out_shape=jax.ShapeDtypeStruct((2, blocks, wi...  4.23 us
  transfers between devices with their start and end apart: 19, of which 6 were waited for; matrix products, arithmetic and copies ran while one was open for 11% of the time, Pallas kernels for 3%

profile of v1, /device:TPU:1, one launch (start us, length us, event | category | flops | bytes accessed | tf_op | source)
XLA Modules:
  0.0 165.0 jit_solution(13142555335234127457)
XLA Ops:
  0.6 1.4 fusion.34
  2.1 0.7 collective-permute-start.4
  2.8 1.3 collective-permute-start.5
  4.1 1.2 fusion.7
  5.3 1.3 collective-permute-start.1
  6.6 0.7 collective-permute-start.2
  7.3 0.7 collective-permute-start.3
  8.1 1.9 %collective-permute-done.1 = bf16[64,2,256]{2,0,1:T(8,128)(2,1)S(1)} collective-permute-done((bf16[64,2,256]{2,0,1:T(8,128)(2,1)S(1)}, bf16[64,2,256]{2,0,1:T(8,128)(2,1)S(1)}, u32[]{:S(2)}, u32[]{:S(2)}) %collective-permute-start.1) | collective-permute-done | bytes 65568 | tf_op jit(solution)/shard_map/deal/ppermute | solution.py:68
  10.0 1.3 collective-permute-start.6
  11.4 0.8 copy.61
  12.2 12.0 %all-to-all-start.1 = ((bf16[64,4,256]{2,1,0:T(4,128)(2,1)}), bf16[64,4,256]{2,1,0:T(4,128)(2,1)S(1)}, u32[]{:S(2)}, u32[]{:S(2)}) async-start(bf16[64,4,256]{2,1,0:T(4,128)(2,1)} %copy.61), calls=%async_computation.1 | async-start | bytes 262144 | tf_op jit(solution)/shard_map/deal/all_to_all | solution.py:65
  24.2 5.3 %collective-permute-start = (bf16[256,2,256]{2,0,1:T(8,128)(2,1)S(1)}, bf16[256,2,256]{2,0,1:T(8,128)(2,1)S(1)}, u32[]{:S(2)}, u32[]{:S(2)}) collective-permute-start(bf16[256,2,256]{2,0,1:T(8,128)(2,1)S(1)} %bitcast.122), channel_id=1, source_target_pairs={{64,0},{128,64},{192,128},{0,192},{65,1},{129,65},{193,129},{1,193... | collective-permute-start | bytes 786440 | tf_op jit(solution)/shard_map/inner/ppermute | solution.py:68
  29.8 4.4 %all-to-all-done.1 = bf16[64,4,256]{2,1,0:T(4,128)(2,1)S(1)} async-done(((bf16[64,4,256]{2,1,0:T(4,128)(2,1)}), bf16[64,4,256]{2,1,0:T(4,128)(2,1)S(1)}, u32[]{:S(2)}, u32[]{:S(2)}) %all-to-all-start.1) | async-done | bytes 131104 | tf_op jit(solution)/shard_map/deal/all_to_all | solution.py:65
  34.2 0.6 copy.62
  35.0 0.7 fusion.24
  35.6 4.2 %pick.1 = f32[2,64,256]{2,1,0:T(8,128)} custom-call(bf16[128,256]{1,0:T(8,128)(2,1)} %bitcast.128, s32[64,256]{1,0:T(8,128)} %get-tuple-element.28.hi_ref, s32[64,256]{1,0:T(8,128)} %get-tuple-element.27.lo_ref), custom_call_target="tpu_custom_call" | custom-call | flops 1073741824 | bytes 196608 | tf_op jit(solution)/shard_map/pick/pick/pallas_call | solution.py:38
  39.9 0.9 convert_bitcast_fusion
  40.8 0.7 copy.65
  41.5 6.6 %all-to-all-start.2 = ((bf16[64,2,256]{2,1,0:T(2,128)(2,1)}), bf16[64,2,256]{2,1,0:T(2,128)(2,1)S(1)}, u32[]{:S(2)}, u32[]{:S(2)}) async-start(bf16[64,2,256]{2,1,0:T(2,128)(2,1)} %copy.65), calls=%async_computation.2 | async-start | bytes 131072 | tf_op jit(solution)/shard_map/pick/all_to_all | solution.py:65
  48.1 9.4 %all-to-all-done.2 = bf16[64,2,256]{2,1,0:T(2,128)(2,1)S(1)} async-done(((bf16[64,2,256]{2,1,0:T(2,128)(2,1)}), bf16[64,2,256]{2,1,0:T(2,128)(2,1)S(1)}, u32[]{:S(2)}, u32[]{:S(2)}) %all-to-all-start.2) | async-done | bytes 65568 | tf_op jit(solution)/shard_map/pick/all_to_all | solution.py:65
  57.6 0.2 convolution_bitcast_fusion.1
  58.0 0.3 reshape.107
  58.2 0.2 convolution_bitcast_fusion
  58.5 1.0 copy.73
  59.5 4.6 %all-to-all-start.3 = ((f32[64,1,1024]{2,1,0:T(1,128)}), f32[64,1,1024]{2,1,0:T(1,128)S(1)}, u32[]{:S(2)}, u32[]{:S(2)}) async-start(f32[64,1,1024]{2,1,0:T(1,128)} %copy.73), calls=%async_computation.3 | async-start | bytes 524288 | tf_op jit(solution)/shard_map/edge/all_to_all | solution.py:65
  64.4 1.0 copy-done
  65.4 0.8 fusion.4
  66.2 1.6 copy.59
  67.8 2.4 %reshape.104 = f32[64,32,256]{2,1,0:T(8,128)} reshape(f32[256,4,2,256]{3,2,1,0:T(2,128)S(1)} %copy.59) | data formatting | bytes 4194304 | tf_op jit(solution)/shard_map/inner/reshape | solution.py:95
  70.3 4.8 %all-to-all-done.3 = f32[64,1,1024]{2,1,0:T(1,128)S(1)} async-done(((f32[64,1,1024]{2,1,0:T(1,128)}), f32[64,1,1024]{2,1,0:T(1,128)S(1)}, u32[]{:S(2)}, u32[]{:S(2)}) %all-to-all-start.3) | async-done | bytes 262176 | tf_op jit(solution)/shard_map/edge/all_to_all | solution.py:65
  75.1 5.9 %all-to-all-start = ((f32[64,32,256]{2,1,0:T(8,128)}), f32[64,32,256]{2,1,0:T(8,128)S(1)}, u32[]{:S(2)}, u32[]{:S(2)}) async-start(f32[64,32,256]{2,1,0:T(8,128)} %reshape.104), calls=%async_computation | async-start | bytes 4194304 | tf_op jit(solution)/shard_map/inner/all_to_all | solution.py:65
  81.2 0.7 collective-permute-start.7
  81.9 11.0 %collective-permute-start.8 = (f32[512]{0:T(512)S(1)}, f32[512]{0:T(512)S(1)}, u32[]{:S(2)}, u32[]{:S(2)}) collective-permute-start(f32[512]{0:T(512)S(1)} %get-tuple-element.26), channel_id=1, source_target_pairs={{64,192},{65,193},{66,194},{67,195},{68,196},{69,197},{70,198},{71... | collective-permute-start | bytes 6152 | tf_op jit(solution)/shard_map/close/ppermute | solution.py:68
  92.9 0.7 collective-permute-start.9
  93.6 1.7 %collective-permute-start.10 = (f32[512]{0:T(512)S(1)}, f32[512]{0:T(512)S(1)}, u32[]{:S(2)}, u32[]{:S(2)}) collective-permute-start(f32[512]{0:T(512)S(1)} %get-tuple-element.25), channel_id=1, source_target_pairs={{64,0},{65,1},{66,2},{67,3},{68,4},{69,5},{70,6},{71,7},{72,8},{73... | collective-permute-start | bytes 6152 | tf_op jit(solution)/shard_map/close/ppermute | solution.py:68
  95.3 0.7 collective-permute-start.11
  96.0 0.8 collective-permute-start.12
  97.4 25.6 %all-to-all-done = f32[64,32,256]{2,1,0:T(8,128)S(1)} async-done(((f32[64,32,256]{2,1,0:T(8,128)}), f32[64,32,256]{2,1,0:T(8,128)S(1)}, u32[]{:S(2)}, u32[]{:S(2)}) %all-to-all-start) | async-done | bytes 2097184 | tf_op jit(solution)/shard_map/inner/all_to_all | solution.py:65
  123.3 1.1 reshape.110
  124.4 0.4 copy.75
  124.7 0.7 copy.76
  125.5 9.7 %all-to-all-start.4 = ((f32[64,1,128]{2,1,0:T(1,128)}), f32[64,1,128]{2,1,0:T(1,128)S(1)}, u32[]{:S(2)}, u32[]{:S(2)}) async-start(f32[64,1,128]{2,1,0:T(1,128)} %copy.76), calls=%async_computation.4 | async-start | bytes 65536 | tf_op jit(solution)/shard_map/mirror/all_to_all | solution.py:65
  135.2 9.1 %all-to-all-done.4 = f32[64,1,128]{2,1,0:T(1,128)S(1)} async-done(((f32[64,1,128]{2,1,0:T(1,128)}), f32[64,1,128]{2,1,0:T(1,128)S(1)}, u32[]{:S(2)}, u32[]{:S(2)}) %all-to-all-start.4) | async-done | bytes 32800 | tf_op jit(solution)/shard_map/mirror/all_to_all | solution.py:65
  144.8 18.1 %collective-permute-start.13 = (f32[2,4,256]{2,1,0:T(4,128)S(1)}, f32[2,4,256]{2,1,0:T(4,128)S(1)}, u32[]{:S(2)}, u32[]{:S(2)}) collective-permute-start(f32[2,4,256]{2,1,0:T(4,128)S(1)} %squeeze.11), channel_id=1, source_target_pairs={{0,64},{64,128},{128,192},{1,65},{65,129},{129,193},{2,66},{66,130... | collective-permute-start | bytes 24584 | tf_op jit(solution)/shard_map/close/ppermute | solution.py:68
  162.9 0.6 maximum_bitcast_fusion.4
  163.5 0.3 copy.79
  163.9 0.4 slice.97
  164.4 0.6 maximum_bitcast_fusion.5
  (64 shorter events, 2.6 us)
Async XLA Ops:
  0.6 7.4 %copy-start.1 = (s32[1,256]{1,0:T(1,128)S(1)}, s32[1,256]{1,0:T(1,128)}, u32[]{:S(2)}) copy-start(s32[1,256]{1,0:T(1,128)} %param.5) | copy-start | bytes 3076
  2.1 27.6 %collective-permute-start.4 = (bf16[256,2,256]{2,0,1:T(8,128)(2,1)S(1)}, bf16[256,2,256]{2,0,1:T(8,128)(2,1)S(1)}, u32[]{:S(2)}, u32[]{:S(2)}) collective-permute-start(bf16[256,2,256]{2,0,1:T(8,128)(2,1)S(1)} %bitcast.123), channel_id=1, source_target_pairs={{192,128},{193,129},{194,130},{195,131},{196,132},{197,133},{198,1... | collective-permute-start | bytes 786440 | tf_op jit(solution)/shard_map/edge/ppermute | solution.py:68
  2.8 26.9 %collective-permute-start.5 = (bf16[256,2,256]{2,0,1:T(8,128)(2,1)S(1)}, bf16[256,2,256]{2,0,1:T(8,128)(2,1)S(1)}, u32[]{:S(2)}, u32[]{:S(2)}) collective-permute-start(bf16[256,2,256]{2,0,1:T(8,128)(2,1)S(1)} %bitcast.124), channel_id=1, source_target_pairs={{192,64},{193,65},{194,66},{195,67},{196,68},{197,69},{198,70},{19... | collective-permute-start | bytes 786440 | tf_op jit(solution)/shard_map/edge/ppermute | solution.py:68
  4.1 25.5 %slice-start = ((bf16[4,1,256,2,256]{4,3,2,1,0:T(2,128)(2,1)}), bf16[3,1,256,2,256]{4,3,2,1,0:T(2,128)(2,1)S(1)}, s32[]{:S(2)}) async-start(bf16[4,1,256,2,256]{4,3,2,1,0:T(2,128)(2,1)} %param.4), calls=%async_computation.5 | async-start | bytes 1572864 | tf_op jit(solution)/shard_map/inner/slice | solution.py:92
  5.3 4.7 %collective-permute-start.1 = (bf16[64,2,256]{2,0,1:T(8,128)(2,1)S(1)}, bf16[64,2,256]{2,0,1:T(8,128)(2,1)S(1)}, u32[]{:S(2)}, u32[]{:S(2)}) collective-permute-start(bf16[64,2,256]{2,0,1:T(8,128)(2,1)S(1)} %get-tuple-element.14), channel_id=1, source_target_pairs={{0,64},{1,65},{2,66},{3,67},{4,68},{5,69},{6,70},{7,71},{8,72},{9,... | collective-permute-start | bytes 196616 | tf_op jit(solution)/shard_map/deal/ppermute | solution.py:68
  6.6 4.7 %collective-permute-start.2 = (bf16[64,2,256]{2,0,1:T(8,128)(2,1)S(1)}, bf16[64,2,256]{2,0,1:T(8,128)(2,1)S(1)}, u32[]{:S(2)}, u32[]{:S(2)}) collective-permute-start(bf16[64,2,256]{2,0,1:T(8,128)(2,1)S(1)} %get-tuple-element.16), channel_id=1, source_target_pairs={{0,128},{1,129},{2,130},{3,131},{4,132},{5,133},{6,134},{7,135},{8... | collective-permute-start | bytes 196616 | tf_op jit(solution)/shard_map/deal/ppermute | solution.py:68
  7.3 4.0 %collective-permute-start.3 = (bf16[64,2,256]{2,0,1:T(8,128)(2,1)S(1)}, bf16[64,2,256]{2,0,1:T(8,128)(2,1)S(1)}, u32[]{:S(2)}, u32[]{:S(2)}) collective-permute-start(bf16[64,2,256]{2,0,1:T(8,128)(2,1)S(1)} %get-tuple-element.15), channel_id=1, source_target_pairs={{0,192},{1,193},{2,194},{3,195},{4,196},{5,197},{6,198},{7,199},{8... | collective-permute-start | bytes 196616 | tf_op jit(solution)/shard_map/deal/ppermute | solution.py:68
  10.0 19.7 %collective-permute-start.6 = (bf16[256,2,256]{2,0,1:T(8,128)(2,1)S(1)}, bf16[256,2,256]{2,0,1:T(8,128)(2,1)}, u32[]{:S(2)}, u32[]{:S(2)}) collective-permute-start(bf16[256,2,256]{2,0,1:T(8,128)(2,1)S(1)} %bitcast.125), channel_id=1, source_target_pairs={{192,0},{193,1},{194,2},{195,3},{196,4},{197,5},{198,6},{199,7},{2... | collective-permute-start | bytes 786440 | tf_op jit(solution)/shard_map/edge/ppermute | solution.py:68
  12.2 22.0 %all-to-all-start.1 = ((bf16[64,4,256]{2,1,0:T(4,128)(2,1)}), bf16[64,4,256]{2,1,0:T(4,128)(2,1)S(1)}, u32[]{:S(2)}, u32[]{:S(2)}) async-start(bf16[64,4,256]{2,1,0:T(4,128)(2,1)} %copy.61), calls=%async_computation.1 | async-start | bytes 262144 | tf_op jit(solution)/shard_map/deal/all_to_all | solution.py:65
  24.2 39.9 %collective-permute-start = (bf16[256,2,256]{2,0,1:T(8,128)(2,1)S(1)}, bf16[256,2,256]{2,0,1:T(8,128)(2,1)S(1)}, u32[]{:S(2)}, u32[]{:S(2)}) collective-permute-start(bf16[256,2,256]{2,0,1:T(8,128)(2,1)S(1)} %bitcast.122), channel_id=1, source_target_pairs={{64,0},{128,64},{192,128},{0,192},{65,1},{129,65},{193,129},{1,193... | collective-permute-start | bytes 786440 | tf_op jit(solution)/shard_map/inner/ppermute | solution.py:68
  41.5 16.1 %all-to-all-start.2 = ((bf16[64,2,256]{2,1,0:T(2,128)(2,1)}), bf16[64,2,256]{2,1,0:T(2,128)(2,1)S(1)}, u32[]{:S(2)}, u32[]{:S(2)}) async-start(bf16[64,2,256]{2,1,0:T(2,128)(2,1)} %copy.65), calls=%async_computation.2 | async-start | bytes 131072 | tf_op jit(solution)/shard_map/pick/all_to_all | solution.py:65
  59.5 15.6 %all-to-all-start.3 = ((f32[64,1,1024]{2,1,0:T(1,128)}), f32[64,1,1024]{2,1,0:T(1,128)S(1)}, u32[]{:S(2)}, u32[]{:S(2)}) async-start(f32[64,1,1024]{2,1,0:T(1,128)} %copy.73), calls=%async_computation.3 | async-start | bytes 524288 | tf_op jit(solution)/shard_map/edge/all_to_all | solution.py:65
  64.2 1.2 copy-start
  75.1 47.9 %all-to-all-start = ((f32[64,32,256]{2,1,0:T(8,128)}), f32[64,32,256]{2,1,0:T(8,128)S(1)}, u32[]{:S(2)}, u32[]{:S(2)}) async-start(f32[64,32,256]{2,1,0:T(8,128)} %reshape.104), calls=%async_computation | async-start | bytes 4194304 | tf_op jit(solution)/shard_map/inner/all_to_all | solution.py:65
  81.0 42.2 %copy-start.2 = (f32[2]{0:T(128)S(1)}, f32[2]{0:T(128)}, u32[]{:S(2)}) copy-start(f32[2]{0:T(128)} %constant.49.clone) | copy-start | bytes 28
  81.2 14.8 %collective-permute-start.7 = (f32[512]{0:T(512)S(1)}, f32[512]{0:T(512)S(1)}, u32[]{:S(2)}, u32[]{:S(2)}) collective-permute-start(f32[512]{0:T(512)S(1)} %get-tuple-element.26), channel_id=1, source_target_pairs={{0,192},{1,193},{2,194},{3,195},{4,196},{5,197},{6,198},{7,199},{8... | collective-permute-start | bytes 6152 | tf_op jit(solution)/shard_map/close/ppermute | solution.py:68
  81.9 15.1 %collective-permute-start.8 = (f32[512]{0:T(512)S(1)}, f32[512]{0:T(512)S(1)}, u32[]{:S(2)}, u32[]{:S(2)}) collective-permute-start(f32[512]{0:T(512)S(1)} %get-tuple-element.26), channel_id=1, source_target_pairs={{64,192},{65,193},{66,194},{67,195},{68,196},{69,197},{70,198},{71... | collective-permute-start | bytes 6152 | tf_op jit(solution)/shard_map/close/ppermute | solution.py:68
  92.9 4.1 %collective-permute-start.9 = (f32[512]{0:T(512)S(1)}, f32[512]{0:T(512)S(1)}, u32[]{:S(2)}, u32[]{:S(2)}) collective-permute-start(f32[512]{0:T(512)S(1)} %get-tuple-element.26), channel_id=1, source_target_pairs={{128,192},{129,193},{130,194},{131,195},{132,196},{133,197},{134,1... | collective-permute-start | bytes 6152 | tf_op jit(solution)/shard_map/close/ppermute | solution.py:68
  93.6 70.7 %collective-permute-start.10 = (f32[512]{0:T(512)S(1)}, f32[512]{0:T(512)S(1)}, u32[]{:S(2)}, u32[]{:S(2)}) collective-permute-start(f32[512]{0:T(512)S(1)} %get-tuple-element.25), channel_id=1, source_target_pairs={{64,0},{65,1},{66,2},{67,3},{68,4},{69,5},{70,6},{71,7},{72,8},{73... | collective-permute-start | bytes 6152 | tf_op jit(solution)/shard_map/close/ppermute | solution.py:68
  95.3 69.1 %collective-permute-start.11 = (f32[512]{0:T(512)S(1)}, f32[512]{0:T(512)S(1)}, u32[]{:S(2)}, u32[]{:S(2)}) collective-permute-start(f32[512]{0:T(512)S(1)} %get-tuple-element.25), channel_id=1, source_target_pairs={{128,0},{129,1},{130,2},{131,3},{132,4},{133,5},{134,6},{135,7},{1... | collective-permute-start | bytes 6152 | tf_op jit(solution)/shard_map/close/ppermute | solution.py:68
  96.0 68.3 %collective-permute-start.12 = (f32[512]{0:T(512)S(1)}, f32[512]{0:T(512)S(1)}, u32[]{:S(2)}, u32[]{:S(2)}) collective-permute-start(f32[512]{0:T(512)S(1)} %get-tuple-element.25), channel_id=1, source_target_pairs={{192,0},{193,1},{194,2},{195,3},{196,4},{197,5},{198,6},{199,7},{2... | collective-permute-start | bytes 6152 | tf_op jit(solution)/shard_map/close/ppermute | solution.py:68
  125.5 18.9 %all-to-all-start.4 = ((f32[64,1,128]{2,1,0:T(1,128)}), f32[64,1,128]{2,1,0:T(1,128)S(1)}, u32[]{:S(2)}, u32[]{:S(2)}) async-start(f32[64,1,128]{2,1,0:T(1,128)} %copy.76), calls=%async_computation.4 | async-start | bytes 65536 | tf_op jit(solution)/shard_map/mirror/all_to_all | solution.py:65
  144.8 19.5 %collective-permute-start.13 = (f32[2,4,256]{2,1,0:T(4,128)S(1)}, f32[2,4,256]{2,1,0:T(4,128)S(1)}, u32[]{:S(2)}, u32[]{:S(2)}) collective-permute-start(f32[2,4,256]{2,1,0:T(4,128)S(1)} %squeeze.11), channel_id=1, source_target_pairs={{0,64},{64,128},{128,192},{1,65},{65,129},{129,193},{2,66},{66,130... | collective-permute-start | bytes 24584 | tf_op jit(solution)/shard_map/close/ppermute | solution.py:68

commit v2 on v0

v2 whole, which is shorter than its diff:
```python
import jax
import jax.numpy as jnp
from jax import lax
from jax.experimental import pallas as pl
from jax.experimental.pallas import tpu as pltpu
from jax.sharding import Mesh, PartitionSpec as P

KZ = ("y_hi", "core")
PW = ("x", "y_lo", "z")
F32, BF16 = jnp.float32, jnp.bfloat16
VMEM = pl.BlockSpec(memory_space=pltpu.VMEM)
AFTER = pl.BlockSpec(memory_space=pl.ANY)
LANES = 128


def iota(shape, axis):
    return lax.broadcasted_iota(jnp.int32, shape, axis)


def across(left, right, dims, precision=None):
    return lax.dot_general(left, right, (dims, ((), ())), precision=precision, preferred_element_type=F32)


def placed(left, right, dims):
    return across(left, right, dims, lax.Precision.HIGHEST)


def wide(real, imag):
    return jnp.concatenate(
        [jnp.concatenate([real, imag], axis=1), jnp.concatenate([imag, -real], axis=1)], axis=0
    )


def call(kernel, name, outs, operands, after=(), flops=0, scratch=(), far=()):
    outs = [jax.ShapeDtypeStruct(*o) if i in far else pltpu.VMEM(*o) for i, o in enumerate(outs)]
    size = sum(x.size * x.dtype.itemsize for x in operands)
    return pl.pallas_call(
        kernel,
        out_shape=outs,
        in_specs=[AFTER] * len(after) + [VMEM] * len(operands),
        out_specs=[VMEM] * len(outs),
        scratch_shapes=list(scratch),
        cost_estimate=pl.CostEstimate(flops=flops, bytes_accessed=2 * size, transcendentals=0),
        compiler_params=pltpu.CompilerParams(vmem_limit_bytes=16 << 20),
        name=name,
    )(*after, *(pltpu.with_memory_space_constraint(x, pltpu.VMEM) for x in operands))


def deal_kernel(planes_ref, *out_refs):
    groups = len(out_refs) - 1
    plane_ref = planes_ref.at[0]
    bands = plane_ref.shape[2]
    blocks = bands // groups
    place, band = iota((bands, bands), 0), iota((bands, bands), 1)
    order = jnp.where(band == (place % blocks) * groups + place // blocks, 1.0, 0.0).astype(BF16)
    for part in range(2):
        dealt = across(order, plane_ref[part], ((1,), (1,))).astype(BF16)
        for j in range(groups):
            out_refs[j][pl.ds(part * blocks, blocks), :] = dealt[j * blocks : (j + 1) * blocks]
    out_refs[groups][...] = plane_ref[...]


def terms_kernel(planes_ref, arriving_ref, *refs):
    out_refs, last_ref, prod_ref = refs[:-2], refs[-2], refs[-1]
    count, _, rows, bands = planes_ref.shape
    blocks, share = out_refs[0].shape[0], out_refs[0].shape[1] * LANES // (count * 2 * bands)
    per = 2 * bands // LANES
    here = lax.axis_index("x")
    for k in range(count):
        left = planes_ref[k].reshape(2 * rows, bands)
        after = arriving_ref if k == count - 1 else planes_ref.at[k + 1]
        prod_ref[...] = across(left, wide(after[0], after[1]), ((0,), (0,)))
        for d, out_ref in enumerate(out_refs):
            to = lax.rem(here + d, len(out_refs))
            base = pl.multiple_of(to * blocks * share, blocks * share)
            mine = prod_ref.at[pl.ds(base, blocks * share)]
            for b in range(blocks):
                for c in range(per):
                    piece = mine[pl.ds(b * share, share), pl.ds(c * LANES, LANES)]
                    out_ref[b, pl.ds((k * per + c) * share, share), :] = piece
    last_ref[...] = planes_ref[count - 1]


def load_kernel(after_ref, map_ref, own_ref, *refs):
    out_ref = refs[-1]
    blocks = out_ref.shape[0]
    first = jnp.where(lax.axis_index(KZ) == 0, 1.0, 0.0)
    mine = own_ref[...].astype(F32) * first
    for ref in refs[:-1]:
        mine = mine + ref[...].astype(F32)
    width = mine.shape[1]
    index = map_ref[...]
    digits = [(index // width).astype(F32), (index % width).astype(F32)]
    parts = [mine[:blocks], mine[blocks:]] + [jnp.broadcast_to(d, (blocks, width)) for d in digits]
    per = width // LANES
    for i, part in enumerate(parts):
        for c in range(per):
            out_ref[:, i * per + c, :] = part[:, c * LANES : (c + 1) * LANES]


def pick_kernel(spread_ref, out_ref, hi_ref, lo_ref):
    blocks, width = hi_ref.shape
    per = width // LANES

    def part(i):
        return jnp.concatenate([spread_ref[:, i * per + c, :] for c in range(per)], axis=1)

    table = jnp.concatenate([part(0), part(1)], axis=0).astype(BF16)
    hi_ref[...] = part(2).astype(jnp.int32)
    lo_ref[...] = part(3).astype(jnp.int32)
    rows, owners = iota((width, width), 0), iota((blocks, width), 0)

    def step(t, carry):
        base = pl.multiple_of(t * 8, 8)
        his, los = hi_ref[pl.ds(base, 8), :], lo_ref[pl.ds(base, 8), :]
        real_rows, imag_rows = [], []
        for r in range(8):
            hot = jnp.where(rows == los[r : r + 1, :], 1.0, 0.0).astype(BF16)
            found = jnp.dot(table, hot, preferred_element_type=F32)
            mine = owners == his[r : r + 1, :]
            real_rows.append(jnp.sum(jnp.where(mine, found[:blocks], 0.0), axis=0, keepdims=True))
            imag_rows.append(jnp.sum(jnp.where(mine, found[blocks:], 0.0), axis=0, keepdims=True))
        for i, picked in enumerate((real_rows, imag_rows)):
            picked = jnp.concatenate(picked, axis=0)
            for c in range(per):
                out_ref[pl.ds(base, 8), i * per + c, :] = picked[:, c * LANES : (c + 1) * LANES]
        return carry

    lax.fori_loop(0, blocks // 8, step, 0)


def halve_kernel(after_ref, *refs):
    sums_refs, (keep_ref, give_ref) = refs[:-2], refs[-2:]
    half = keep_ref.shape[0]
    here = lax.axis_index("y_lo")
    for out_ref, side in ((keep_ref, here), (give_ref, 1 - here)):
        total = sums_refs[0][pl.ds(side * half, half)]
        for ref in sums_refs[1:]:
            total = total + ref[pl.ds(side * half, half)]
        out_ref[...] = total


def merge_kernel(*refs):
    picked_ref, keep_ref, got_ref, out_ref = refs[-4:]
    far = keep_ref.shape[0]
    near, chunks = picked_ref.shape[0] // far, picked_ref.shape[1]
    for p in range(near):
        for z in range(far):
            out_ref[z, pl.ds(p * chunks, chunks), :] = picked_ref[p * far + z]
    out_ref[:, pl.ds(near * chunks, keep_ref.shape[1]), :] = keep_ref[...] + got_ref[...]


def edge_kernel(got_ref, own_ref, *refs):
    sent_refs, (plus_ref, out_ref, moved_ref, turn_ref, rows_ref) = refs[:-5], refs[-5:]
    count, _, share, bands = plus_ref.shape
    blocks, width = moved_ref.shape
    far = got_ref.shape[0]
    chunks, near, per = width // LANES, blocks // far, bands // LANES
    here = lax.axis_index(KZ)

    total = got_ref[0, pl.ds(near * chunks, count * 2 * per * share), :]
    for z in range(1, far):
        total = total + got_ref[z, pl.ds(near * chunks, count * 2 * per * share), :]
    for k in range(count):
        for o in range(2):
            for c in range(per):
                first = ((k * 2 + o) * per + c) * share
                piece = total[first : first + share]
                plus_ref[k, o, :, pl.ds(c * LANES, LANES)] = piece
                rows_ref[pl.ds((k * 2 + o) * share, share), pl.ds(c * LANES, LANES)] = piece
    place, band = iota((bands, bands), 0), iota((bands, bands), 1)
    order = jnp.where(band == (place % blocks) * share + place // blocks, 1.0, 0.0)
    tiles = placed(order, rows_ref[...], ((1,), (1,)))
    tiles = jnp.concatenate([tiles[i * blocks : (i + 1) * blocks] for i in range(share)], axis=1)
    out_ref[pl.ds(8, blocks, stride=9), :] = tiles

    final = own_ref[...]
    for j, ref in enumerate(sent_refs):
        final = jnp.where(here == j, ref[...], final)
    for p in range(near):
        for c in range(chunks):
            moved_ref[pl.ds(p * far, far), pl.ds(c * LANES, LANES)] = got_ref[:, p * chunks + c, :]
    moved = moved_ref[...].astype(BF16)
    prods = jnp.dot(moved, wide(final[0], final[1]), preferred_element_type=F32)
    turn_ref[...] = jnp.concatenate([prods[:, :bands].T, -prods[:, bands:].T], axis=1)
    for c in range(4):
        out_ref[pl.ds(c, blocks, stride=9), :] = turn_ref[pl.ds(c, blocks, stride=4), :]
        out_ref[pl.ds(4 + c, blocks, stride=9), :] = prods[:, LANES * c : LANES * (c + 1)]


def gather_kernel(back_ref, minus_ref, *pay_refs):
    count, _, share, bands = minus_ref.shape
    blocks = back_ref.shape[0] // 9
    groups = len(pay_refs)
    sums = [jnp.sum(back_ref[pl.ds(c, blocks, stride=9), :], axis=0, keepdims=True) for c in range(8)]
    edge_n, edge_m = jnp.concatenate(sums[:4], axis=0), jnp.concatenate(sums[4:], axis=0)
    tiles = back_ref[pl.ds(8, blocks, stride=9), :]
    lane = iota((blocks, bands), 1)
    spread = placed(tiles, jnp.where(lane // share == iota((blocks, bands), 0), 1.0, 0.0), ((0,), (0,)))
    spread = jnp.where(iota(spread.shape, 0) % share == iota(spread.shape, 1) % share, spread, 0.0)
    shape = (count * 2 * share, spread.shape[0])
    row, col = iota(shape, 0), iota(shape, 1)
    same = (row % share == col // (count * 2 * share)) & (row // share == (col // share) % (count * 2))
    sign = jnp.where((row // share) % 2 == 0, 1.0, -1.0)
    mirror = placed(jnp.where(same, sign, 0.0), spread, ((1,), (0,)))
    for k in range(count):
        for o in range(2):
            minus_ref[k, o] = mirror[(2 * k + o) * share : (2 * k + o + 1) * share]
    for d, ref in enumerate(pay_refs):
        piece = jnp.where(lax.rem(lax.axis_index(KZ) + d, groups) == groups - 1, edge_n, edge_m)
        if d == 1:
            ref[...] = jnp.zeros_like(ref)
            ref[pl.ds(0, 2 * share), :] = mirror[(count - 1) * 2 * share :]
            ref[pl.ds(2 * share, share), pl.ds(0, LANES)] = piece
        else:
            ref[...] = piece


def close_kernel(plus_ref, minus_ref, *refs):
    got_refs, plus_out, minus_out = refs[:-2], refs[-2], refs[-1]
    count, _, share, bands = plus_ref.shape
    groups = len(got_refs)
    here = lax.axis_index(KZ)
    got = [
        ref[pl.ds(2 * share, share), pl.ds(0, LANES)] if d == 1 else ref[...]
        for d, ref in enumerate(got_refs)
    ]
    plus_out[...] = plus_ref[...]
    for k in range(1, count):
        minus_out[k] = minus_ref[k - 1]
    for o in range(2):
        minus_out[0, o] = got_refs[1][pl.ds(o * share, share), :]

    @pl.when(here == groups - 1)
    def _():
        shape = (LANES, 2 * bands)
        row, col = iota(shape, 0), iota(shape, 1)
        half = LANES // 2
        rows = jnp.zeros((share, 2 * bands), F32)
        for j in range(groups):
            spot = (row // half == col // bands) & ((row % half) * groups + j == col % bands)
            rows = rows + placed(got[groups - 1 - j], jnp.where(spot, 1.0, 0.0), ((1,), (0,)))
        for o in range(2):
            plus_out[count - 1, o] = rows[:, o * bands : (o + 1) * bands]

    @pl.when(here == 0)
    def _():
        per = bands // LANES
        for j in range(groups):
            piece = got[(groups - j) % groups]
            for r in range(2 * per):
                minus_out[0, r // per, pl.ds(j, 1), pl.ds((r % per) * LANES, LANES)] = piece[r : r + 1]


def body(waves, pw_map):
    kz_dev, _, rows, _, bands = waves.shape
    n_kz, n_pw, n_x, n_z = (lax.axis_size(a) for a in (KZ, PW, "x", "z"))
    share, group = bands // n_pw, n_pw // n_x
    planes = waves[:, 0].transpose(0, 2, 1, 3)

    def swap(x, axes):
        return lax.all_to_all(x, axes, 0, 0, tiled=True)

    def sent(x, pairs):
        return lax.ppermute(x, KZ, pairs)

    def around(x, d):
        return sent(x, [(i, (i + d) % n_kz) for i in range(n_kz)])

    def along(x, d):
        return lax.ppermute(x, "x", [(i, (i + d) % n_x) for i in range(n_x)])

    plane = (planes.shape[1:], BF16)
    with jax.named_scope("deal"):
        *dealt, first = call(
            deal_kernel, "deal", [((2 * n_pw, rows), BF16)] * share + [plane], (planes,),
            flops=4 * rows * bands * bands,
        )
        dealt = [dealt[0]] + [sent(dealt[j], [(0, j)]) for j in range(1, n_kz)]

    with jax.named_scope("inner"):
        arriving = around(first, n_kz - 1)
        chunks = kz_dev * 2 * bands * share // LANES
        *terms, final = call(
            terms_kernel, "terms", [((group, chunks, LANES), F32)] * n_x + [plane], (planes, arriving),
            flops=kz_dev * 8 * rows * bands * bands, scratch=[pltpu.VMEM((bands, 2 * bands), F32)],
        )
        sums = [terms[0]] + [along(terms[d], d) for d in range(1, n_x)]
        finals = [sent(final, [(n_kz - 1, j)]) for j in range(n_kz - 1)]

    with jax.named_scope("deal"):
        (load,) = call(
            load_kernel, "load", [((n_pw, 4 * rows // LANES, LANES), F32)], (pw_map, *dealt),
            after=(terms[0],), far=(0,),
        )
        spread = swap(load, PW)
    with jax.named_scope("pick"):
        (picked,) = call(
            pick_kernel, "pick", [((n_pw, 2 * rows // LANES, LANES), F32)], (spread,),
            flops=4 * n_pw * n_pw * rows * rows, scratch=[pltpu.VMEM((n_pw, rows), jnp.int32)] * 2, far=(0,),
        )

    with jax.named_scope("inner"):
        keep, give = call(
            halve_kernel, "halve", [((n_z, chunks, LANES), F32)] * 2, sums, after=(picked,)
        )
        halves = (keep, lax.ppermute(give, "y_lo", [(0, 1), (1, 0)]))
    with jax.named_scope("pick"):
        picked = swap(picked, ("x", "y_lo"))
    with jax.named_scope("inner"):
        (merged,) = call(
            merge_kernel, "merge", [((n_z, n_pw // n_z * 2 * rows // LANES + chunks, LANES), F32)],
            (picked, *halves), after=finals, far=(0,),
        )
        got = swap(merged, "z")

    with jax.named_scope("edge"):
        rows_out = ((kz_dev, 2, share, bands), F32)
        plus, out = call(
            edge_kernel, "edge", [rows_out, ((n_pw * 9, LANES), F32)], (got, final, *finals),
            flops=8 * n_pw * rows * bands, far=(1,),
            scratch=[
                pltpu.VMEM((n_pw, 2 * rows), F32),
                pltpu.VMEM((bands, 2 * n_pw), F32),
                pltpu.VMEM((kz_dev * 2 * share, bands), F32),
            ],
        )
        back = swap(out.reshape(n_pw, 1, 9 * LANES), PW).reshape(n_pw * 9, LANES)

    with jax.named_scope("close"):
        piece = ((share, LANES), F32)
        long = ((4 * share, bands), F32)
        minus, *pieces = call(gather_kernel, "gather", [rows_out, piece, long] + [piece] * (n_kz - 2), (back,))
        pieces = [pieces[0]] + [around(pieces[d], d) for d in range(1, n_kz)]
        plus, minus = call(close_kernel, "close", [rows_out] * 2, (plus, minus, *pieces), far=(0, 1))
    return plus[:, None], minus[:, None]


def solution(mesh):
    fine = Mesh(mesh.devices.reshape(2, 2, 4, 2, 8), KZ + PW)
    out = P(KZ, None, None, PW, None)
    return jax.shard_map(
        body,
        mesh=fine,
        in_specs=(P(KZ, None, PW, None, None), P(None, PW)),
        out_specs=(out, out),
        check_vma=False,
    )
```

time: 1020 us -> 117 us (0.11)
  the two profiles are of different devices: /device:TPU:16 before, /device:TPU:1 now
where the time goes in v2:
time: 117 us; the launch traced here: 116 us
  starting transfers between devices  40.9 us (35%)
  blocking collectives  33.1 us (28%)
  waiting for transfers between devices  29.9 us (26%)
  Pallas kernels  9.55 us (8%)
  local copies, waits for them, and re-layouts  2.04 us (2%)
    all_to_all x2, blocking collectives, swap(): return lax.all_to_all(x, axes, 0, 0, tiled=True)  33.1 us
    ppermute x10, starting transfers between devices, sent(): return lax.ppermute(x, KZ, pairs)  18.7 us
    all_to_all x2, starting transfers between devices, swap(): return lax.all_to_all(x, axes, 0, 0, tiled=True)  16.3 us
    ppermute x3, waiting for transfers between devices, along(): return lax.ppermute(x, 'x', [(i, (i + d) % n_x) for i in range(n_x)])  12.7 us
    all_to_all x2, waiting for transfers between devices, swap(): return lax.all_to_all(x, axes, 0, 0, tiled=True)  10.7 us
    pallas_call x9, Pallas kernels, call(): pl.pallas_call(kernel, out_shape=outs, in_specs=[AFTER] * len(after) + [V...  9.55 us
    ppermute x10, waiting for transfers between devices, sent(): return lax.ppermute(x, KZ, pairs)  6.56 us
    ppermute x3, starting transfers between devices, along(): return lax.ppermute(x, 'x', [(i, (i + d) % n_x) for i in range(n_x)])  4.76 us
  transfers between devices with their start and end apart: 16, of which 7 were waited for; matrix products, arithmetic and copies ran while one was open for 0% of the time, Pallas kernels for 6%

profile of v2, /device:TPU:1, one launch (start us, length us, event | category | flops | bytes accessed | tf_op | source)
XLA Modules:
  0.0 116.2 jit_solution(10725621413772010859)
XLA Ops:
  0.6 1.4 %copy.12 = bf16[4,1,256,2,256]{4,2,3,0,1:T(8,128)(2,1)S(1)} copy(bf16[4,1,256,2,256]{4,3,2,1,0:T(2,128)(2,1)} %param.2) | data formatting | bytes 2097152 | tf_op args[0]
  2.0 0.3 deal.1
  2.3 3.3 %collective-permute-start = (bf16[2,256,256]{2,1,0:T(8,128)(2,1)S(1)}, bf16[2,256,256]{2,1,0:T(8,128)(2,1)S(1)}, u32[]{:S(2)}, u32[]{:S(2)}) collective-permute-start(bf16[2,256,256]{2,1,0:T(8,128)(2,1)S(1)} %get-tuple-element.23), channel_id=1, source_target_pairs={{0,192},{64,0},{128,64},{192,128},{1,193},{65,1},{129,65},{193,129... | collective-permute-start | bytes 786440 | tf_op jit(solution)/shard_map/inner/ppermute | solution.py:265
  5.6 1.3 %collective-permute-start.4 = (bf16[128,256]{1,0:T(8,128)(2,1)S(1)}, bf16[128,256]{1,0:T(8,128)(2,1)S(1)}, u32[]{:S(2)}, u32[]{:S(2)}) collective-permute-start(bf16[128,256]{1,0:T(8,128)(2,1)S(1)} %get-tuple-element.27), channel_id=1, source_target_pairs={{0,64},{1,65},{2,66},{3,67},{4,68},{5,69},{6,70},{7,71},{8,72},{9,... | collective-permute-start | bytes 196616 | tf_op jit(solution)/shard_map/deal/ppermute | solution.py:265
  6.9 0.7 collective-permute-start.5
  7.5 0.7 collective-permute-start.6
  8.2 2.5 %collective-permute-done.arriving_ref = bf16[2,256,256]{2,1,0:T(8,128)(2,1)S(1)} collective-permute-done((bf16[2,256,256]{2,1,0:T(8,128)(2,1)S(1)}, bf16[2,256,256]{2,1,0:T(8,128)(2,1)S(1)}, u32[]{:S(2)}, u32[]{:S(2)}) %collective-permute-start) | collective-permute-done | bytes 262176 | tf_op jit(solution)/shard_map/inner/ppermute | solution.py:265
  10.7 2.1 %terms.1 = (f32[16,64,128]{2,1,0:T(8,128)S(1)}, f32[16,64,128]{2,1,0:T(8,128)}, f32[16,64,128]{2,1,0:T(8,128)}, f32[16,64,128]{2,1,0:T(8,128)}, bf16[2,256,256]{2,1,0:T(8,128)(2,1)S(1)}) custom-call(bf16[4,2,256,256]{3,2,1,0:T(8,128)(2,1)S(1)} %bitcast.14, bf16[2,256,256]{2,1,0:T(8,128)(2,1)S(1)} %collective-permute-done.arriving_ref), custom_call_target="tpu_custom_call" | custom-call | flops 536870912 | bytes 2621440 | tf_op jit(solution)/shard_map/inner/terms/pallas_call | solution.py:37
  12.8 0.0 collective-permute-done.4.refs_0_
  12.8 0.0 collective-permute-done.5.refs_1_
  12.8 0.0 collective-permute-done.6.refs_2_
  12.8 0.0 copy-start
  12.9 0.7 copy-done
  13.5 0.9 load.1
  14.4 12.4 %all-to-all-start = ((f32[64,8,128]{2,1,0:T(8,128)}), f32[64,8,128]{2,1,0:T(8,128)S(1)}, u32[]{:S(2)}, u32[]{:S(2)}) async-start(f32[64,8,128]{2,1,0:T(8,128)} %load.1), calls=%async_computation | async-start | bytes 524288 | tf_op jit(solution)/shard_map/deal/all_to_all | solution.py:262
  26.9 1.1 collective-permute-start.7
  28.0 2.6 %collective-permute-start.8 = (f32[16,64,128]{2,1,0:T(8,128)}, f32[16,64,128]{2,1,0:T(8,128)S(1)}, u32[]{:S(2)}, u32[]{:S(2)}) collective-permute-start(f32[16,64,128]{2,1,0:T(8,128)} %get-tuple-element.31), channel_id=1, source_target_pairs={{0,32},{16,48},{32,0},{48,16},{1,33},{17,49},{33,1},{49,17},{2,34}... | collective-permute-start | bytes 1572872 | tf_op jit(solution)/shard_map/inner/ppermute | solution.py:271
  30.6 1.1 collective-permute-start.9
  31.6 0.7 collective-permute-start.1
  32.3 1.3 %collective-permute-start.2 = (bf16[2,256,256]{2,1,0:T(8,128)(2,1)S(1)}, bf16[2,256,256]{2,1,0:T(8,128)(2,1)S(1)}, u32[]{:S(2)}, u32[]{:S(2)}) collective-permute-start(bf16[2,256,256]{2,1,0:T(8,128)(2,1)S(1)} %get-tuple-element.24.own_ref), channel_id=1, source_target_pairs={{192,64},{193,65},{194,66},{195,67},{196,68},{197,69},{198,70},{19... | collective-permute-start | bytes 786440 | tf_op jit(solution)/shard_map/inner/ppermute | solution.py:265
  33.6 5.5 %all-to-all-done.spread_ref = f32[64,8,128]{2,1,0:T(8,128)S(1)} async-done(((f32[64,8,128]{2,1,0:T(8,128)}), f32[64,8,128]{2,1,0:T(8,128)S(1)}, u32[]{:S(2)}, u32[]{:S(2)}) %all-to-all-start) | async-done | bytes 262176 | tf_op jit(solution)/shard_map/deal/all_to_all | solution.py:262
  39.1 3.5 %pick.1.after_ref = f32[64,4,128]{2,1,0:T(4,128)} custom-call(f32[64,8,128]{2,1,0:T(8,128)S(1)} %all-to-all-done.spread_ref), custom_call_target="tpu_custom_call" | custom-call | flops 1073741824 | bytes 524288 | tf_op jit(solution)/shard_map/pick/pick/pallas_call | solution.py:37
  42.6 1.6 %collective-permute-done.7.refs_1_ = f32[16,64,128]{2,1,0:T(8,128)S(1)} collective-permute-done((f32[16,64,128]{2,1,0:T(8,128)}, f32[16,64,128]{2,1,0:T(8,128)S(1)}, u32[]{:S(2)}, u32[]{:S(2)}) %collective-permute-start.7) | collective-permute-done | bytes 524320 | tf_op jit(solution)/shard_map/inner/ppermute | solution.py:271
  44.2 0.7 collective-permute-start.3
  44.9 11.1 %collective-permute-done.8.refs_2_ = f32[16,64,128]{2,1,0:T(8,128)S(1)} collective-permute-done((f32[16,64,128]{2,1,0:T(8,128)}, f32[16,64,128]{2,1,0:T(8,128)S(1)}, u32[]{:S(2)}, u32[]{:S(2)}) %collective-permute-start.8) | collective-permute-done | bytes 524320 | tf_op jit(solution)/shard_map/inner/ppermute | solution.py:271
  56.0 0.0 collective-permute-done.9.refs_3_
  56.0 0.8 halve.1
  56.8 1.1 collective-permute-start.10
  57.9 3.8 %all-to-all-start.1 = ((f32[64,4,128]{2,1,0:T(4,128)}), f32[64,4,128]{2,1,0:T(4,128)S(1)}, u32[]{:S(2)}, u32[]{:S(2)}) async-start(f32[64,4,128]{2,1,0:T(4,128)} %pick.1.after_ref), calls=%async_computation.1 | async-start | bytes 262144 | tf_op jit(solution)/shard_map/pick/all_to_all | solution.py:262
  61.7 0.0 collective-permute-done.1.refs_0_
  61.7 0.0 collective-permute-done.2.refs_1_
  61.7 0.0 collective-permute-done.3.refs_2_
  61.7 5.2 %all-to-all-done.1.refs_3_ = f32[64,4,128]{2,1,0:T(4,128)S(1)} async-done(((f32[64,4,128]{2,1,0:T(4,128)}), f32[64,4,128]{2,1,0:T(4,128)S(1)}, u32[]{:S(2)}, u32[]{:S(2)}) %all-to-all-start.1) | async-done | bytes 131104 | tf_op jit(solution)/shard_map/pick/all_to_all | solution.py:262
  67.0 0.0 collective-permute-done.10.refs_5_
  67.0 0.1 merge.1
  67.0 16.5 %all_to_all.20.got_ref = f32[8,96,128]{2,1,0:T(8,128)S(1)} all-to-all(f32[8,96,128]{2,1,0:T(8,128)S(1)} %merge.1), channel_id=1, replica_groups=mesh['y_hi'=2,'core'=2,'x'=4,'y_lo'=2,'z'=8] {'z'}, dimensions={0} | all-to-all | bytes 786432 | tf_op jit(solution)/shard_map/inner/all_to_all | solution.py:262
  83.5 0.7 edge.1
  84.2 16.6 %all_to_all.21 = f32[64,1,1152]{2,1,0:T(1,128)S(1)} all-to-all(f32[64,1,1152]{2,1,0:T(1,128)S(1)} %bitcast.16), channel_id=1, replica_groups=mesh['y_hi'=2,'core'=2,'x'=4,'y_lo'=2,'z'=8] {'x','y_lo','z'}, dimensions={0} | all-to-all | bytes 589824 | tf_op jit(solution)/shard_map/edge/all_to_all | solution.py:262
  100.8 0.6 gather.1
  101.3 9.7 %collective-permute-start.11 = (f32[16,256]{1,0:T(8,128)S(1)}, f32[16,256]{1,0:T(8,128)S(1)}, u32[]{:S(2)}, u32[]{:S(2)}) collective-permute-start(f32[16,256]{1,0:T(8,128)S(1)} %get-tuple-element.39), channel_id=1, source_target_pairs={{0,64},{64,128},{128,192},{192,0},{1,65},{65,129},{129,193},{193,1... | collective-permute-start | bytes 49160 | tf_op jit(solution)/shard_map/close/ppermute | solution.py:265
  111.0 0.0 collective-permute-start.12
  111.0 0.5 collective-permute-start.13
  111.5 3.5 %collective-permute-done.12.refs_2_ = f32[4,128]{1,0:T(4,128)S(1)} collective-permute-done((f32[4,128]{1,0:T(4,128)S(1)}, f32[4,128]{1,0:T(4,128)S(1)}, u32[]{:S(2)}, u32[]{:S(2)}) %collective-permute-start.12) | collective-permute-done | bytes 2080 | tf_op jit(solution)/shard_map/close/ppermute | solution.py:265
  115.0 0.6 collective-permute-done.13.refs_3_
  115.6 0.0 collective-permute-done.11.refs_1_
  115.6 0.6 close.1
Async XLA Ops:
  2.3 8.4 %collective-permute-start = (bf16[2,256,256]{2,1,0:T(8,128)(2,1)S(1)}, bf16[2,256,256]{2,1,0:T(8,128)(2,1)S(1)}, u32[]{:S(2)}, u32[]{:S(2)}) collective-permute-start(bf16[2,256,256]{2,1,0:T(8,128)(2,1)S(1)} %get-tuple-element.23), channel_id=1, source_target_pairs={{0,192},{64,0},{128,64},{192,128},{1,193},{65,1},{129,65},{193,129... | collective-permute-start | bytes 786440 | tf_op jit(solution)/shard_map/inner/ppermute | solution.py:265
  5.6 7.2 %collective-permute-start.4 = (bf16[128,256]{1,0:T(8,128)(2,1)S(1)}, bf16[128,256]{1,0:T(8,128)(2,1)S(1)}, u32[]{:S(2)}, u32[]{:S(2)}) collective-permute-start(bf16[128,256]{1,0:T(8,128)(2,1)S(1)} %get-tuple-element.27), channel_id=1, source_target_pairs={{0,64},{1,65},{2,66},{3,67},{4,68},{5,69},{6,70},{7,71},{8,72},{9,... | collective-permute-start | bytes 196616 | tf_op jit(solution)/shard_map/deal/ppermute | solution.py:265
  6.9 6.0 %collective-permute-start.5 = (bf16[128,256]{1,0:T(8,128)(2,1)S(1)}, bf16[128,256]{1,0:T(8,128)(2,1)S(1)}, u32[]{:S(2)}, u32[]{:S(2)}) collective-permute-start(bf16[128,256]{1,0:T(8,128)(2,1)S(1)} %get-tuple-element.28), channel_id=1, source_target_pairs={{0,128},{1,129},{2,130},{3,131},{4,132},{5,133},{6,134},{7,135},{8... | collective-permute-start | bytes 196616 | tf_op jit(solution)/shard_map/deal/ppermute | solution.py:265
  7.5 5.3 %collective-permute-start.6 = (bf16[128,256]{1,0:T(8,128)(2,1)S(1)}, bf16[128,256]{1,0:T(8,128)(2,1)S(1)}, u32[]{:S(2)}, u32[]{:S(2)}) collective-permute-start(bf16[128,256]{1,0:T(8,128)(2,1)S(1)} %get-tuple-element.29), channel_id=1, source_target_pairs={{0,192},{1,193},{2,194},{3,195},{4,196},{5,197},{6,198},{7,199},{8... | collective-permute-start | bytes 196616 | tf_op jit(solution)/shard_map/deal/ppermute | solution.py:265
  12.8 0.7 copy-start
  14.4 24.7 %all-to-all-start = ((f32[64,8,128]{2,1,0:T(8,128)}), f32[64,8,128]{2,1,0:T(8,128)S(1)}, u32[]{:S(2)}, u32[]{:S(2)}) async-start(f32[64,8,128]{2,1,0:T(8,128)} %load.1), calls=%async_computation | async-start | bytes 524288 | tf_op jit(solution)/shard_map/deal/all_to_all | solution.py:262
  26.9 17.3 %collective-permute-start.7 = (f32[16,64,128]{2,1,0:T(8,128)}, f32[16,64,128]{2,1,0:T(8,128)S(1)}, u32[]{:S(2)}, u32[]{:S(2)}) collective-permute-start(f32[16,64,128]{2,1,0:T(8,128)} %get-tuple-element.30), channel_id=1, source_target_pairs={{0,16},{16,32},{32,48},{48,0},{1,17},{17,33},{33,49},{49,1},{2,18}... | collective-permute-start | bytes 1572872 | tf_op jit(solution)/shard_map/inner/ppermute | solution.py:271
  28.0 28.0 %collective-permute-start.8 = (f32[16,64,128]{2,1,0:T(8,128)}, f32[16,64,128]{2,1,0:T(8,128)S(1)}, u32[]{:S(2)}, u32[]{:S(2)}) collective-permute-start(f32[16,64,128]{2,1,0:T(8,128)} %get-tuple-element.31), channel_id=1, source_target_pairs={{0,32},{16,48},{32,0},{48,16},{1,33},{17,49},{33,1},{49,17},{2,34}... | collective-permute-start | bytes 1572872 | tf_op jit(solution)/shard_map/inner/ppermute | solution.py:271
  30.6 25.4 %collective-permute-start.9 = (f32[16,64,128]{2,1,0:T(8,128)}, f32[16,64,128]{2,1,0:T(8,128)S(1)}, u32[]{:S(2)}, u32[]{:S(2)}) collective-permute-start(f32[16,64,128]{2,1,0:T(8,128)} %get-tuple-element.32), channel_id=1, source_target_pairs={{0,48},{16,0},{32,16},{48,32},{1,49},{17,1},{33,17},{49,33},{2,50}... | collective-permute-start | bytes 1572872 | tf_op jit(solution)/shard_map/inner/ppermute | solution.py:271
  31.6 30.1 %collective-permute-start.1 = (bf16[2,256,256]{2,1,0:T(8,128)(2,1)S(1)}, bf16[2,256,256]{2,1,0:T(8,128)(2,1)S(1)}, u32[]{:S(2)}, u32[]{:S(2)}) collective-permute-start(bf16[2,256,256]{2,1,0:T(8,128)(2,1)S(1)} %get-tuple-element.24.own_ref), channel_id=1, source_target_pairs={{192,0},{193,1},{194,2},{195,3},{196,4},{197,5},{198,6},{199,7},{2... | collective-permute-start | bytes 786440 | tf_op jit(solution)/shard_map/inner/ppermute | solution.py:265
  32.3 29.4 %collective-permute-start.2 = (bf16[2,256,256]{2,1,0:T(8,128)(2,1)S(1)}, bf16[2,256,256]{2,1,0:T(8,128)(2,1)S(1)}, u32[]{:S(2)}, u32[]{:S(2)}) collective-permute-start(bf16[2,256,256]{2,1,0:T(8,128)(2,1)S(1)} %get-tuple-element.24.own_ref), channel_id=1, source_target_pairs={{192,64},{193,65},{194,66},{195,67},{196,68},{197,69},{198,70},{19... | collective-permute-start | bytes 786440 | tf_op jit(solution)/shard_map/inner/ppermute | solution.py:265
  44.2 17.5 %collective-permute-start.3 = (bf16[2,256,256]{2,1,0:T(8,128)(2,1)S(1)}, bf16[2,256,256]{2,1,0:T(8,128)(2,1)S(1)}, u32[]{:S(2)}, u32[]{:S(2)}) collective-permute-start(bf16[2,256,256]{2,1,0:T(8,128)(2,1)S(1)} %get-tuple-element.24.own_ref), channel_id=1, source_target_pairs={{192,128},{193,129},{194,130},{195,131},{196,132},{197,133},{198,1... | collective-permute-start | bytes 786440 | tf_op jit(solution)/shard_map/inner/ppermute | solution.py:265
  56.8 10.2 %collective-permute-start.10 = (f32[8,64,128]{2,1,0:T(8,128)}, f32[8,64,128]{2,1,0:T(8,128)S(1)}, u32[]{:S(2)}, u32[]{:S(2)}) collective-permute-start(f32[8,64,128]{2,1,0:T(8,128)} %get-tuple-element.34), channel_id=1, source_target_pairs={{0,8},{8,0},{1,9},{9,1},{2,10},{10,2},{3,11},{11,3},{4,12},{12,4},... | collective-permute-start | bytes 786440 | tf_op jit(solution)/shard_map/inner/ppermute | solution.py:307
  57.9 9.1 %all-to-all-start.1 = ((f32[64,4,128]{2,1,0:T(4,128)}), f32[64,4,128]{2,1,0:T(4,128)S(1)}, u32[]{:S(2)}, u32[]{:S(2)}) async-start(f32[64,4,128]{2,1,0:T(4,128)} %pick.1.after_ref), calls=%async_computation.1 | async-start | bytes 262144 | tf_op jit(solution)/shard_map/pick/all_to_all | solution.py:262
  101.3 14.3 %collective-permute-start.11 = (f32[16,256]{1,0:T(8,128)S(1)}, f32[16,256]{1,0:T(8,128)S(1)}, u32[]{:S(2)}, u32[]{:S(2)}) collective-permute-start(f32[16,256]{1,0:T(8,128)S(1)} %get-tuple-element.39), channel_id=1, source_target_pairs={{0,64},{64,128},{128,192},{192,0},{1,65},{65,129},{129,193},{193,1... | collective-permute-start | bytes 49160 | tf_op jit(solution)/shard_map/close/ppermute | solution.py:265
  111.0 3.9 %collective-permute-start.12 = (f32[4,128]{1,0:T(4,128)S(1)}, f32[4,128]{1,0:T(4,128)S(1)}, u32[]{:S(2)}, u32[]{:S(2)}) collective-permute-start(f32[4,128]{1,0:T(4,128)S(1)} %get-tuple-element.40), channel_id=1, source_target_pairs={{0,128},{64,192},{128,0},{192,64},{1,129},{65,193},{129,1},{193,65... | collective-permute-start | bytes 6152 | tf_op jit(solution)/shard_map/close/ppermute | solution.py:265
  111.0 4.5 %collective-permute-start.13 = (f32[4,128]{1,0:T(4,128)S(1)}, f32[4,128]{1,0:T(4,128)S(1)}, u32[]{:S(2)}, u32[]{:S(2)}) collective-permute-start(f32[4,128]{1,0:T(4,128)S(1)} %get-tuple-element.41), channel_id=1, source_target_pairs={{0,192},{64,0},{128,64},{192,128},{1,193},{65,1},{129,65},{193,129... | collective-permute-start | bytes 6152 | tf_op jit(solution)/shard_map/close/ppermute | solution.py:265

commit v3 on v2

--- a/solution.py
+++ b/solution.py
@@ -46,56 +46,73 @@
     )(*after, *(pltpu.with_memory_space_constraint(x, pltpu.VMEM) for x in operands))
 
 
-def deal_kernel(planes_ref, *out_refs):
-    groups = len(out_refs) - 1
-    plane_ref = planes_ref.at[0]
-    bands = plane_ref.shape[2]
+def dealt_to(group, groups, bands):
+    shape = (bands // groups, bands)
+    return jnp.where(iota(shape, 1) == iota(shape, 0) * groups + group, 1.0, 0.0).astype(BF16)
+
+
+def deal_kernel(planes_ref, map_ref, *out_refs):
+    digits_ref, first_ref, out_refs = out_refs[-1], out_refs[-2], out_refs[:-2]
+    groups, width, bands = len(out_refs) + 1, planes_ref.shape[2], planes_ref.shape[3]
     blocks = bands // groups
-    place, band = iota((bands, bands), 0), iota((bands, bands), 1)
-    order = jnp.where(band == (place % blocks) * groups + place // blocks, 1.0, 0.0).astype(BF16)
-    for part in range(2):
-        dealt = across(order, plane_ref[part], ((1,), (1,))).astype(BF16)
-        for j in range(groups):
-            out_refs[j][pl.ds(part * blocks, blocks), :] = dealt[j * blocks : (j + 1) * blocks]
-    out_refs[groups][...] = plane_ref[...]
-
-
-def terms_kernel(planes_ref, arriving_ref, *refs):
-    out_refs, last_ref, prod_ref = refs[:-2], refs[-2], refs[-1]
+    for j, out_ref in enumerate(out_refs):
+        for part in range(2):
+            dealt = across(dealt_to(j, groups, bands), planes_ref[0, part], ((1,), (1,)))
+            out_ref[pl.ds(part * blocks, blocks), :] = dealt.astype(BF16)
+    first_ref[...] = planes_ref[0]
+    index = map_ref[...]
+    per = width // LANES
+    for i, digit in enumerate((index // width, index % width)):
+        for c in range(per):
+            digits_ref[pl.ds(i * per + c, 1), :] = digit[:, c * LANES : (c + 1) * LANES].astype(F32)
+
+
+def terms_kernel(*refs):
+    planes_ref, arriving_ref, *along_refs = refs[-8:-4]
+    beside_refs, last_ref, prod_ref = refs[-4:-2], refs[-2], refs[-1]
     count, _, rows, bands = planes_ref.shape
-    blocks, share = out_refs[0].shape[0], out_refs[0].shape[1] * LANES // (count * 2 * bands)
-    per = 2 * bands // LANES
-    here = lax.axis_index("x")
+    half, per = count // 2, 2 * bands // LANES
+    size = along_refs[0].shape[0] // 4
+    share = bands // (8 * size)
+    here, side = lax.axis_index("x"), lax.axis_index("y_lo")
+    near = here + 1 - 2 * lax.rem(here, 2)
+    sides = (side, 1 - side)
     for k in range(count):
         left = planes_ref[k].reshape(2 * rows, bands)
         after = arriving_ref if k == count - 1 else planes_ref.at[k + 1]
         prod_ref[...] = across(left, wide(after[0], after[1]), ((0,), (0,)))
-        for d, out_ref in enumerate(out_refs):
-            to = lax.rem(here + d, len(out_refs))
-            base = pl.multiple_of(to * blocks * share, blocks * share)
-            mine = prod_ref.at[pl.ds(base, blocks * share)]
-            for b in range(blocks):
-                for c in range(per):
-                    piece = mine[pl.ds(b * share, share), pl.ds(c * LANES, LANES)]
-                    out_ref[b, pl.ds((k * per + c) * share, share), :] = piece
+        if k < half:
+            order = [[(x, s) for x in xs for s in sides] for xs in ((here, 3 - here), (near, 3 - near))]
+        else:
+            order = [[(x, s) for x in (here, 3 - here, near, 3 - near)] for s in sides]
+        for out_ref, places in zip(along_refs if k < half else beside_refs, order):
+            for p, (x, s) in enumerate(places):
+                first = pl.multiple_of((2 * x + s) * size * share, size * share)
+                mine = prod_ref.at[pl.ds(first, size * share)]
+                for i in range(size):
+                    for c in range(per):
+                        piece = mine[pl.ds(i * share, share), pl.ds(c * LANES, LANES)]
+                        out_ref[p * size + i, pl.ds(((k % half) * per + c) * share, share), :] = piece
     last_ref[...] = planes_ref[count - 1]
 
 
-def load_kernel(after_ref, map_ref, own_ref, *refs):
+def load_kernel(after_ref, digits_ref, own_ref, arriving_ref, *refs):
     out_ref = refs[-1]
     blocks = out_ref.shape[0]
-    first = jnp.where(lax.axis_index(KZ) == 0, 1.0, 0.0)
-    mine = own_ref[...].astype(F32) * first
+    here, groups = lax.axis_index(KZ), len(refs) + 1
+    mine = jnp.where(here == 0, own_ref[...].astype(F32), 0.0)
     for ref in refs[:-1]:
         mine = mine + ref[...].astype(F32)
-    width = mine.shape[1]
-    index = map_ref[...]
-    digits = [(index // width).astype(F32), (index % width).astype(F32)]
-    parts = [mine[:blocks], mine[blocks:]] + [jnp.broadcast_to(d, (blocks, width)) for d in digits]
-    per = width // LANES
-    for i, part in enumerate(parts):
+    order = dealt_to(groups - 1, groups, arriving_ref.shape[2])
+    last = [across(order, arriving_ref[part], ((1,), (1,))) for part in range(2)]
+    mine = jnp.where(here == groups - 1, jnp.concatenate(last, axis=0), mine)
+    per = mine.shape[1] // LANES
+    for i, part in enumerate((mine[:blocks], mine[blocks:])):
         for c in range(per):
             out_ref[:, i * per + c, :] = part[:, c * LANES : (c + 1) * LANES]
+    digits = digits_ref[...]
+    for c in range(2 * per):
+        out_ref[:, 2 * per + c, :] = jnp.broadcast_to(digits[c : c + 1], (blocks, LANES))
 
 
 def pick_kernel(spread_ref, out_ref, hi_ref, lo_ref):
@@ -129,25 +146,24 @@
     lax.fori_loop(0, blocks // 8, step, 0)
 
 
-def halve_kernel(after_ref, *refs):
-    sums_refs, (keep_ref, give_ref) = refs[:-2], refs[-2:]
-    half = keep_ref.shape[0]
-    here = lax.axis_index("y_lo")
-    for out_ref, side in ((keep_ref, here), (give_ref, 1 - here)):
-        total = sums_refs[0][pl.ds(side * half, half)]
-        for ref in sums_refs[1:]:
-            total = total + ref[pl.ds(side * half, half)]
-        out_ref[...] = total
+def fold_kernel(*refs):
+    in_refs, out_refs = refs[:4], refs[4:]
+    half = out_refs[0].shape[0]
+    for i in range(4):
+        kept, got = in_refs[i // 2 * 2], in_refs[i // 2 * 2 + 1]
+        part = pl.ds(i % 2 * half, half)
+        out_refs[i][...] = kept[part] + got[part]
 
 
 def merge_kernel(*refs):
-    picked_ref, keep_ref, got_ref, out_ref = refs[-4:]
-    far = keep_ref.shape[0]
+    picked_ref, sums_refs, out_ref = refs[-6], refs[-5:-1], refs[-1]
+    far, rows = out_ref.shape[0], sums_refs[0].shape[1]
     near, chunks = picked_ref.shape[0] // far, picked_ref.shape[1]
     for p in range(near):
         for z in range(far):
             out_ref[z, pl.ds(p * chunks, chunks), :] = picked_ref[p * far + z]
-    out_ref[:, pl.ds(near * chunks, keep_ref.shape[1]), :] = keep_ref[...] + got_ref[...]
+    for i in range(2):
+        out_ref[:, pl.ds(near * chunks + i * rows, rows), :] = sums_refs[2 * i][...] + sums_refs[2 * i + 1][...]
 
 
 def edge_kernel(got_ref, own_ref, *refs):
@@ -255,7 +271,7 @@
 def body(waves, pw_map):
     kz_dev, _, rows, _, bands = waves.shape
     n_kz, n_pw, n_x, n_z = (lax.axis_size(a) for a in (KZ, PW, "x", "z"))
-    share, group = bands // n_pw, n_pw // n_x
+    share = bands // n_pw
     planes = waves[:, 0].transpose(0, 2, 1, 3)
 
     def swap(x, axes):
@@ -264,53 +280,63 @@
     def sent(x, pairs):
         return lax.ppermute(x, KZ, pairs)
 
-    def around(x, d):
-        return sent(x, [(i, (i + d) % n_kz) for i in range(n_kz)])
-
-    def along(x, d):
-        return lax.ppermute(x, "x", [(i, (i + d) % n_x) for i in range(n_x)])
+    def around(x, d, ends=None):
+        pairs = [(i, (i + d) % n_kz) for i in range(n_kz)]
+        return sent(x, [p for p in pairs if ends is None or p[1] in ends])
+
+    def beside(x):
+        return lax.ppermute(x, "y_lo", [(0, 1), (1, 0)])
+
+    def near(x):
+        return lax.ppermute(x, "x", [(i, i ^ 1) for i in range(n_x)])
+
+    def mirrored(x):
+        return lax.ppermute(x, "x", [(i, n_x - 1 - i) for i in range(n_x)])
 
     plane = (planes.shape[1:], BF16)
     with jax.named_scope("deal"):
-        *dealt, first = call(
-            deal_kernel, "deal", [((2 * n_pw, rows), BF16)] * share + [plane], (planes,),
+        digits = ((2 * rows // LANES, LANES), F32)
+        *dealt, first, digits = call(
+            deal_kernel, "deal", [((2 * n_pw, rows), BF16)] * (share - 1) + [plane, digits], (planes, pw_map),
             flops=4 * rows * bands * bands,
         )
-        dealt = [dealt[0]] + [sent(dealt[j], [(0, j)]) for j in range(1, n_kz)]
+        dealt = [dealt[0]] + [sent(dealt[j], [(0, j)]) for j in range(1, n_kz - 1)]
 
     with jax.named_scope("inner"):
         arriving = around(first, n_kz - 1)
-        chunks = kz_dev * 2 * bands * share // LANES
-        *terms, final = call(
-            terms_kernel, "terms", [((group, chunks, LANES), F32)] * n_x + [plane], (planes, arriving),
+        chunks = kz_dev * bands * share // LANES
+        part = ((n_pw // 2, chunks, LANES), F32)
+        *sums, final = call(
+            terms_kernel, "terms", [part] * 4 + [plane], (planes, arriving), after=dealt[1:],
             flops=kz_dev * 8 * rows * bands * bands, scratch=[pltpu.VMEM((bands, 2 * bands), F32)],
         )
-        sums = [terms[0]] + [along(terms[d], d) for d in range(1, n_x)]
+        terms = sums[0]
+        sums = (sums[0], near(sums[1]), sums[2], beside(sums[3]))
         finals = [sent(final, [(n_kz - 1, j)]) for j in range(n_kz - 1)]
 
     with jax.named_scope("deal"):
         (load,) = call(
-            load_kernel, "load", [((n_pw, 4 * rows // LANES, LANES), F32)], (pw_map, *dealt),
-            after=(terms[0],), far=(0,),
+            load_kernel, "load", [((n_pw, 4 * rows // LANES, LANES), F32)], (digits, dealt[0], arriving, *dealt[1:]),
+            after=(terms,),
         )
         spread = swap(load, PW)
     with jax.named_scope("pick"):
         (picked,) = call(
             pick_kernel, "pick", [((n_pw, 2 * rows // LANES, LANES), F32)], (spread,),
-            flops=4 * n_pw * n_pw * rows * rows, scratch=[pltpu.VMEM((n_pw, rows), jnp.int32)] * 2, far=(0,),
+            flops=4 * n_pw * n_pw * rows * rows, scratch=[pltpu.VMEM((n_pw, rows), jnp.int32)] * 2,
         )
 
     with jax.named_scope("inner"):
-        keep, give = call(
-            halve_kernel, "halve", [((n_z, chunks, LANES), F32)] * 2, sums, after=(picked,)
-        )
-        halves = (keep, lax.ppermute(give, "y_lo", [(0, 1), (1, 0)]))
+        sums = call(fold_kernel, "fold", [((n_pw // 4, chunks, LANES), F32)] * 4, sums)
+        sums = (sums[0], mirrored(sums[1]), sums[2], near(sums[3]))
+        sums = call(fold_kernel, "fold", [((n_pw // 8, chunks, LANES), F32)] * 4, sums)
+        sums = (sums[0], beside(sums[1]), sums[2], mirrored(sums[3]))
     with jax.named_scope("pick"):
         picked = swap(picked, ("x", "y_lo"))
     with jax.named_scope("inner"):
         (merged,) = call(
-            merge_kernel, "merge", [((n_z, n_pw // n_z * 2 * rows // LANES + chunks, LANES), F32)],
-            (picked, *halves), after=finals, far=(0,),
+            merge_kernel, "merge", [((n_z, n_pw // n_z * 2 * rows // LANES + 2 * chunks, LANES), F32)],
+            (picked, *sums), after=finals,
         )
         got = swap(merged, "z")
 
@@ -318,7 +344,7 @@
         rows_out = ((kz_dev, 2, share, bands), F32)
         plus, out = call(
             edge_kernel, "edge", [rows_out, ((n_pw * 9, LANES), F32)], (got, final, *finals),
-            flops=8 * n_pw * rows * bands, far=(1,),
+            flops=8 * n_pw * rows * bands,
             scratch=[
                 pltpu.VMEM((n_pw, 2 * rows), F32),
                 pltpu.VMEM((bands, 2 * n_pw), F32),
@@ -331,7 +357,9 @@
         piece = ((share, LANES), F32)
         long = ((4 * share, bands), F32)
         minus, *pieces = call(gather_kernel, "gather", [rows_out, piece, long] + [piece] * (n_kz - 2), (back,))
-        pieces = [pieces[0]] + [around(pieces[d], d) for d in range(1, n_kz)]
+        pieces = [pieces[0]] + [
+            around(pieces[d], d, None if d == 1 else (0, n_kz - 1)) for d in range(1, n_kz)
+        ]
         plus, minus = call(close_kernel, "close", [rows_out] * 2, (plus, minus, *pieces), far=(0, 1))
     return plus[:, None], minus[:, None]
 

time: 117 us -> 101 us (0.86)
  waiting for transfers between devices: 29.9 us -> 14.8 us
  starting transfers between devices: 40.9 us -> 43.1 us
  blocking collectives: 33.1 us -> 31.4 us
  Pallas kernels: 9.55 us -> 8.36 us
    ppermute x4 -> x6, waiting for transfers between devices: 12.7 us -> 5.69 us  [the longest x2 4.89 us: mirrored(): return lax.ppermute(x, 'x', [(i, n_x - 1 - i) for i in range(n_x)])]
    all_to_all x2, waiting for transfers between devices: 10.7 us -> 5.16 us  [swap(): return lax.all_to_all(x, axes, 0, 0, tiled=True)]
    ppermute x10 -> x9, waiting for transfers between devices: 6.56 us -> 3.96 us  [sent(): return lax.ppermute(x, KZ, pairs)]
    ppermute x4 -> x6, starting transfers between devices: 5.87 us -> 7.91 us  [the longest x2 4.28 us: mirrored(): return lax.ppermute(x, 'x', [(i, n_x - 1 - i) for i in range(n_x)])]
    all_to_all x2, blocking collectives: 33.1 us -> 31.4 us  [swap(): return lax.all_to_all(x, axes, 0, 0, tiled=True)]
    ppermute x10 -> x9, starting transfers between devices: 18.7 us -> 20.3 us  [sent(): return lax.ppermute(x, KZ, pairs)]
    all_to_all x2, starting transfers between devices: 16.3 us -> 14.8 us  [swap(): return lax.all_to_all(x, axes, 0, 0, tiled=True)]
    pallas_call x9 -> x10, Pallas kernels: 9.55 us -> 8.36 us  [call(): pl.pallas_call(kernel, out_shape=outs, in_specs=[AFTER] * len(after) + [V...]
  transfers between devices with their start and end apart: 16 -> 17, of which waited for: 7 -> 6; matrix products, arithmetic and copies ran while one was open for 0% -> 0% of each run, Pallas kernels for 6% -> 5%
where the time goes in v3:
time: 101 us; the launch traced here: 100 us
  starting transfers between devices  43.1 us (43%)
  blocking collectives  31.4 us (31%)
  waiting for transfers between devices  14.8 us (15%)
  Pallas kernels  8.36 us (8%)
  local copies, waits for them, and re-layouts  2.04 us (2%)
    all_to_all x2, blocking collectives, swap(): return lax.all_to_all(x, axes, 0, 0, tiled=True)  31.4 us
    ppermute x9, starting transfers between devices, sent(): return lax.ppermute(x, KZ, pairs)  20.3 us
    all_to_all x2, starting transfers between devices, swap(): return lax.all_to_all(x, axes, 0, 0, tiled=True)  14.8 us
    pallas_call x10, Pallas kernels, call(): pl.pallas_call(kernel, out_shape=outs, in_specs=[AFTER] * len(after) + [V...  8.36 us
    all_to_all x2, waiting for transfers between devices, swap(): return lax.all_to_all(x, axes, 0, 0, tiled=True)  5.16 us
    ppermute x2, waiting for transfers between devices, mirrored(): return lax.ppermute(x, 'x', [(i, n_x - 1 - i) for i in range(n_x)])  4.89 us
    ppermute x2, starting transfers between devices, mirrored(): return lax.ppermute(x, 'x', [(i, n_x - 1 - i) for i in range(n_x)])  4.28 us
    ppermute x9, waiting for transfers between devices, sent(): return lax.ppermute(x, KZ, pairs)  3.96 us
  transfers between devices with their start and end apart: 17, of which 6 were waited for; matrix products, arithmetic and copies ran while one was open for 0% of the time, Pallas kernels for 5%

profile of v3, /device:TPU:1, one launch (start us, length us, event | category | flops | bytes accessed | tf_op | source)
XLA Modules:
  0.0 100.5 jit_solution(3885356390416563620)
XLA Ops:
  0.6 1.4 %copy.12 = bf16[4,1,256,2,256]{4,2,3,0,1:T(8,128)(2,1)S(1)} copy(bf16[4,1,256,2,256]{4,3,2,1,0:T(2,128)(2,1)} %param.2) | data formatting | bytes 2097152 | tf_op args[0]
  2.0 0.0 copy-start
  2.0 0.7 copy-done
  2.7 0.4 deal.1
  3.0 3.3 %collective-permute-start.2 = (bf16[2,256,256]{2,1,0:T(8,128)(2,1)S(1)}, bf16[2,256,256]{2,1,0:T(8,128)(2,1)S(1)}, u32[]{:S(2)}, u32[]{:S(2)}) collective-permute-start(bf16[2,256,256]{2,1,0:T(8,128)(2,1)S(1)} %get-tuple-element.31), channel_id=1, source_target_pairs={{0,192},{64,0},{128,64},{192,128},{1,193},{65,1},{129,65},{193,129... | collective-permute-start | bytes 786440 | tf_op jit(solution)/shard_map/inner/ppermute | solution.py:281
  6.4 1.3 %collective-permute-start = (bf16[128,256]{1,0:T(8,128)(2,1)S(1)}, bf16[128,256]{1,0:T(8,128)(2,1)S(1)}, u32[]{:S(2)}, u32[]{:S(2)}) collective-permute-start(bf16[128,256]{1,0:T(8,128)(2,1)S(1)} %get-tuple-element.29), channel_id=1, source_target_pairs={{0,64},{1,65},{2,66},{3,67},{4,68},{5,69},{6,70},{7,71},{8,72},{9,... | collective-permute-start | bytes 196616 | tf_op jit(solution)/shard_map/deal/ppermute | solution.py:281
  7.6 0.7 collective-permute-start.1
  8.3 1.2 %collective-permute-done.refs_0_ = bf16[128,256]{1,0:T(8,128)(2,1)S(1)} collective-permute-done((bf16[128,256]{1,0:T(8,128)(2,1)S(1)}, bf16[128,256]{1,0:T(8,128)(2,1)S(1)}, u32[]{:S(2)}, u32[]{:S(2)}) %collective-permute-start) | collective-permute-done | bytes 65568 | tf_op jit(solution)/shard_map/deal/ppermute | solution.py:281
  9.5 0.0 collective-permute-done.1.refs_1_
  9.5 2.0 %collective-permute-done.2.refs_3_.arriving_ref = bf16[2,256,256]{2,1,0:T(8,128)(2,1)S(1)} collective-permute-done((bf16[2,256,256]{2,1,0:T(8,128)(2,1)S(1)}, bf16[2,256,256]{2,1,0:T(8,128)(2,1)S(1)}, u32[]{:S(2)}, u32[]{:S(2)}) %collective-permute-start.2) | collective-permute-done | bytes 262176 | tf_op jit(solution)/shard_map/inner/ppermute | solution.py:281
  11.5 1.4 %terms.1 = (f32[32,32,128]{2,1,0:T(8,128)S(1)}, f32[32,32,128]{2,1,0:T(8,128)}, f32[32,32,128]{2,1,0:T(8,128)S(1)}, f32[32,32,128]{2,1,0:T(8,128)S(1)}, bf16[2,256,256]{2,1,0:T(8,128)(2,1)S(1)}) custom-call(bf16[128,256]{1,0:T(8,128)(2,1)S(1)} %collective-permute-done.refs_0_, bf16[128,256]{1,0:T(8,128)(2,1)S(1)} %collective-permute-done.1.refs_1_, ...), custom_call_target="tpu_custom_call" | custom-call | flops 536870912 | bytes 2621440 | tf_op jit(solution)/shard_map/inner/terms/pallas_call | solution.py:37
  12.9 1.2 %collective-permute-start.6 = (f32[32,32,128]{2,1,0:T(8,128)}, f32[32,32,128]{2,1,0:T(8,128)S(1)}, u32[]{:S(2)}, u32[]{:S(2)}) collective-permute-start(f32[32,32,128]{2,1,0:T(8,128)} %get-tuple-element.36), channel_id=1, source_target_pairs={{0,16},{16,0},{32,48},{48,32},{1,17},{17,1},{33,49},{49,33},{2,18}... | collective-permute-start | bytes 1572872 | tf_op jit(solution)/shard_map/inner/ppermute | solution.py:291
  14.1 1.1 %collective-permute-start.7 = (f32[32,32,128]{2,1,0:T(8,128)S(1)}, f32[32,32,128]{2,1,0:T(8,128)S(1)}, u32[]{:S(2)}, u32[]{:S(2)}) collective-permute-start(f32[32,32,128]{2,1,0:T(8,128)S(1)} %get-tuple-element.38), channel_id=1, source_target_pairs={{0,8},{8,0},{1,9},{9,1},{2,10},{10,2},{3,11},{11,3},{4,12},{12,4},... | collective-permute-start | bytes 1572872 | tf_op jit(solution)/shard_map/inner/ppermute | solution.py:288
  15.2 1.0 load.1
  16.1 11.5 %all-to-all-start = ((f32[64,8,128]{2,1,0:T(8,128)}), f32[64,8,128]{2,1,0:T(8,128)S(1)}, u32[]{:S(2)}, u32[]{:S(2)}) async-start(f32[64,8,128]{2,1,0:T(8,128)} %load.1), calls=%async_computation | async-start | bytes 524288 | tf_op jit(solution)/shard_map/deal/all_to_all | solution.py:278
  27.6 0.0 collective-permute-done.6.refs_1_
  27.6 0.0 collective-permute-done.7.refs_3_
  27.6 0.1 fold.2
  27.8 2.5 %collective-permute-start.8 = (f32[16,32,128]{2,1,0:T(8,128)S(1)}, f32[16,32,128]{2,1,0:T(8,128)S(1)}, u32[]{:S(2)}, u32[]{:S(2)}) collective-permute-start(f32[16,32,128]{2,1,0:T(8,128)S(1)} %get-tuple-element.40), channel_id=1, source_target_pairs={{0,48},{16,32},{32,16},{48,0},{1,49},{17,33},{33,17},{49,1},{2,50}... | collective-permute-start | bytes 786440 | tf_op jit(solution)/shard_map/inner/ppermute | solution.py:294
  30.3 0.0 collective-permute-start.9
  30.3 0.7 collective-permute-start.3
  31.0 1.3 %collective-permute-start.4 = (bf16[2,256,256]{2,1,0:T(8,128)(2,1)S(1)}, bf16[2,256,256]{2,1,0:T(8,128)(2,1)S(1)}, u32[]{:S(2)}, u32[]{:S(2)}) collective-permute-start(bf16[2,256,256]{2,1,0:T(8,128)(2,1)S(1)} %get-tuple-element.32.own_ref), channel_id=1, source_target_pairs={{192,64},{193,65},{194,66},{195,67},{196,68},{197,69},{198,70},{19... | collective-permute-start | bytes 786440 | tf_op jit(solution)/shard_map/inner/ppermute | solution.py:281
  32.3 0.7 collective-permute-start.5
  32.9 4.9 %collective-permute-done.8.refs_1_ = f32[16,32,128]{2,1,0:T(8,128)S(1)} collective-permute-done((f32[16,32,128]{2,1,0:T(8,128)S(1)}, f32[16,32,128]{2,1,0:T(8,128)S(1)}, u32[]{:S(2)}, u32[]{:S(2)}) %collective-permute-start.8) | collective-permute-done | bytes 262176 | tf_op jit(solution)/shard_map/inner/ppermute | solution.py:294
  37.8 0.8 collective-permute-done.9.refs_3_
  38.6 0.1 fold.3
  38.7 1.3 %collective-permute-start.10 = (f32[8,32,128]{2,1,0:T(8,128)S(1)}, f32[8,32,128]{2,1,0:T(8,128)S(1)}, u32[]{:S(2)}, u32[]{:S(2)}) collective-permute-start(f32[8,32,128]{2,1,0:T(8,128)S(1)} %get-tuple-element.44), channel_id=1, source_target_pairs={{0,8},{8,0},{1,9},{9,1},{2,10},{10,2},{3,11},{11,3},{4,12},{12,4},... | collective-permute-start | bytes 393224 | tf_op jit(solution)/shard_map/inner/ppermute | solution.py:288
  40.0 1.8 %collective-permute-start.11 = (f32[8,32,128]{2,1,0:T(8,128)S(1)}, f32[8,32,128]{2,1,0:T(8,128)S(1)}, u32[]{:S(2)}, u32[]{:S(2)}) collective-permute-start(f32[8,32,128]{2,1,0:T(8,128)S(1)} %get-tuple-element.46), channel_id=1, source_target_pairs={{0,48},{16,32},{32,16},{48,0},{1,49},{17,33},{33,17},{49,1},{2,50}... | collective-permute-start | bytes 393224 | tf_op jit(solution)/shard_map/inner/ppermute | solution.py:294
  41.8 0.0 all-to-all-done.spread_ref
  41.8 3.5 %pick.1 = f32[64,4,128]{2,1,0:T(4,128)} custom-call(f32[64,8,128]{2,1,0:T(8,128)S(1)} %all-to-all-done.spread_ref), custom_call_target="tpu_custom_call" | custom-call | flops 1073741824 | bytes 524288 | tf_op jit(solution)/shard_map/pick/pick/pallas_call | solution.py:37
  45.3 3.4 %all-to-all-start.1 = ((f32[64,4,128]{2,1,0:T(4,128)}), f32[64,4,128]{2,1,0:T(4,128)S(1)}, u32[]{:S(2)}, u32[]{:S(2)}) async-start(f32[64,4,128]{2,1,0:T(4,128)} %pick.1), calls=%async_computation.1 | async-start | bytes 262144 | tf_op jit(solution)/shard_map/pick/all_to_all | solution.py:278
  48.7 0.0 collective-permute-done.3.refs_0_
  48.7 0.0 collective-permute-done.4.refs_1_
  48.7 0.0 collective-permute-done.5.refs_2_
  48.7 5.2 %all-to-all-done.1.refs_3_ = f32[64,4,128]{2,1,0:T(4,128)S(1)} async-done(((f32[64,4,128]{2,1,0:T(4,128)}), f32[64,4,128]{2,1,0:T(4,128)S(1)}, u32[]{:S(2)}, u32[]{:S(2)}) %all-to-all-start.1) | async-done | bytes 131104 | tf_op jit(solution)/shard_map/pick/all_to_all | solution.py:278
  53.9 0.0 collective-permute-done.10.refs_5_
  53.9 0.1 merge.1
  54.0 16.3 %all_to_all.20.got_ref = f32[8,96,128]{2,1,0:T(8,128)S(1)} all-to-all(f32[8,96,128]{2,1,0:T(8,128)S(1)} %merge.1), channel_id=1, replica_groups=mesh['y_hi'=2,'core'=2,'x'=4,'y_lo'=2,'z'=8] {'z'}, dimensions={0} | all-to-all | bytes 786432 | tf_op jit(solution)/shard_map/inner/all_to_all | solution.py:278
  70.3 0.7 edge.1
  70.9 15.1 %all_to_all.21 = f32[64,1,1152]{2,1,0:T(1,128)S(1)} all-to-all(f32[64,1,1152]{2,1,0:T(1,128)S(1)} %bitcast.16), channel_id=1, replica_groups=mesh['y_hi'=2,'core'=2,'x'=4,'y_lo'=2,'z'=8] {'x','y_lo','z'}, dimensions={0} | all-to-all | bytes 589824 | tf_op jit(solution)/shard_map/edge/all_to_all | solution.py:278
  86.0 0.6 gather.1
  86.6 9.0 %collective-permute-start.12 = (f32[16,256]{1,0:T(8,128)S(1)}, f32[16,256]{1,0:T(8,128)S(1)}, u32[]{:S(2)}, u32[]{:S(2)}) collective-permute-start(f32[16,256]{1,0:T(8,128)S(1)} %get-tuple-element.51), channel_id=1, source_target_pairs={{0,64},{64,128},{128,192},{192,0},{1,65},{65,129},{129,193},{193,1... | collective-permute-start | bytes 49160 | tf_op jit(solution)/shard_map/close/ppermute | solution.py:281
  95.6 2.1 %collective-permute-start.13 = (f32[4,128]{1,0:T(4,128)S(1)}, f32[4,128]{1,0:T(4,128)S(1)}, u32[]{:S(2)}, u32[]{:S(2)}) collective-permute-start(f32[4,128]{1,0:T(4,128)S(1)} %get-tuple-element.52), channel_id=1, source_target_pairs={{64,192},{128,0},{65,193},{129,1},{66,194},{130,2},{67,195},{131,3... | collective-permute-start | bytes 6152 | tf_op jit(solution)/shard_map/close/ppermute | solution.py:281
  97.7 1.3 %collective-permute-start.14 = (f32[4,128]{1,0:T(4,128)S(1)}, f32[4,128]{1,0:T(4,128)S(1)}, u32[]{:S(2)}, u32[]{:S(2)}) collective-permute-start(f32[4,128]{1,0:T(4,128)S(1)} %get-tuple-element.53), channel_id=1, source_target_pairs={{0,192},{64,0},{1,193},{65,1},{2,194},{66,2},{3,195},{67,3},{4,196... | collective-permute-start | bytes 6152 | tf_op jit(solution)/shard_map/close/ppermute | solution.py:281
  99.0 0.0 collective-permute-done.13.refs_2_
  99.0 0.8 collective-permute-done.14.refs_3_
  99.8 0.0 collective-permute-done.12.refs_1_
  99.8 0.6 close.1
  (1 shorter events, 0.0 us)
Async XLA Ops:
  2.0 0.7 copy-start
  3.0 8.4 %collective-permute-start.2 = (bf16[2,256,256]{2,1,0:T(8,128)(2,1)S(1)}, bf16[2,256,256]{2,1,0:T(8,128)(2,1)S(1)}, u32[]{:S(2)}, u32[]{:S(2)}) collective-permute-start(bf16[2,256,256]{2,1,0:T(8,128)(2,1)S(1)} %get-tuple-element.31), channel_id=1, source_target_pairs={{0,192},{64,0},{128,64},{192,128},{1,193},{65,1},{129,65},{193,129... | collective-permute-start | bytes 786440 | tf_op jit(solution)/shard_map/inner/ppermute | solution.py:281
  6.4 3.1 %collective-permute-start = (bf16[128,256]{1,0:T(8,128)(2,1)S(1)}, bf16[128,256]{1,0:T(8,128)(2,1)S(1)}, u32[]{:S(2)}, u32[]{:S(2)}) collective-permute-start(bf16[128,256]{1,0:T(8,128)(2,1)S(1)} %get-tuple-element.29), channel_id=1, source_target_pairs={{0,64},{1,65},{2,66},{3,67},{4,68},{5,69},{6,70},{7,71},{8,72},{9,... | collective-permute-start | bytes 196616 | tf_op jit(solution)/shard_map/deal/ppermute | solution.py:281
  7.6 1.9 %collective-permute-start.1 = (bf16[128,256]{1,0:T(8,128)(2,1)S(1)}, bf16[128,256]{1,0:T(8,128)(2,1)S(1)}, u32[]{:S(2)}, u32[]{:S(2)}) collective-permute-start(bf16[128,256]{1,0:T(8,128)(2,1)S(1)} %get-tuple-element.30), channel_id=1, source_target_pairs={{0,128},{1,129},{2,130},{3,131},{4,132},{5,133},{6,134},{7,135},{8... | collective-permute-start | bytes 196616 | tf_op jit(solution)/shard_map/deal/ppermute | solution.py:281
  12.9 14.7 %collective-permute-start.6 = (f32[32,32,128]{2,1,0:T(8,128)}, f32[32,32,128]{2,1,0:T(8,128)S(1)}, u32[]{:S(2)}, u32[]{:S(2)}) collective-permute-start(f32[32,32,128]{2,1,0:T(8,128)} %get-tuple-element.36), channel_id=1, source_target_pairs={{0,16},{16,0},{32,48},{48,32},{1,17},{17,1},{33,49},{49,33},{2,18}... | collective-permute-start | bytes 1572872 | tf_op jit(solution)/shard_map/inner/ppermute | solution.py:291
  14.1 13.5 %collective-permute-start.7 = (f32[32,32,128]{2,1,0:T(8,128)S(1)}, f32[32,32,128]{2,1,0:T(8,128)S(1)}, u32[]{:S(2)}, u32[]{:S(2)}) collective-permute-start(f32[32,32,128]{2,1,0:T(8,128)S(1)} %get-tuple-element.38), channel_id=1, source_target_pairs={{0,8},{8,0},{1,9},{9,1},{2,10},{10,2},{3,11},{11,3},{4,12},{12,4},... | collective-permute-start | bytes 1572872 | tf_op jit(solution)/shard_map/inner/ppermute | solution.py:288
  16.1 25.7 %all-to-all-start = ((f32[64,8,128]{2,1,0:T(8,128)}), f32[64,8,128]{2,1,0:T(8,128)S(1)}, u32[]{:S(2)}, u32[]{:S(2)}) async-start(f32[64,8,128]{2,1,0:T(8,128)} %load.1), calls=%async_computation | async-start | bytes 524288 | tf_op jit(solution)/shard_map/deal/all_to_all | solution.py:278
  27.8 10.1 %collective-permute-start.8 = (f32[16,32,128]{2,1,0:T(8,128)S(1)}, f32[16,32,128]{2,1,0:T(8,128)S(1)}, u32[]{:S(2)}, u32[]{:S(2)}) collective-permute-start(f32[16,32,128]{2,1,0:T(8,128)S(1)} %get-tuple-element.40), channel_id=1, source_target_pairs={{0,48},{16,32},{32,16},{48,0},{1,49},{17,33},{33,17},{49,1},{2,50}... | collective-permute-start | bytes 786440 | tf_op jit(solution)/shard_map/inner/ppermute | solution.py:294
  30.3 8.3 %collective-permute-start.9 = (f32[16,32,128]{2,1,0:T(8,128)S(1)}, f32[16,32,128]{2,1,0:T(8,128)S(1)}, u32[]{:S(2)}, u32[]{:S(2)}) collective-permute-start(f32[16,32,128]{2,1,0:T(8,128)S(1)} %get-tuple-element.42), channel_id=1, source_target_pairs={{0,16},{16,0},{32,48},{48,32},{1,17},{17,1},{33,49},{49,33},{2,18}... | collective-permute-start | bytes 786440 | tf_op jit(solution)/shard_map/inner/ppermute | solution.py:291
  30.3 18.4 %collective-permute-start.3 = (bf16[2,256,256]{2,1,0:T(8,128)(2,1)S(1)}, bf16[2,256,256]{2,1,0:T(8,128)(2,1)S(1)}, u32[]{:S(2)}, u32[]{:S(2)}) collective-permute-start(bf16[2,256,256]{2,1,0:T(8,128)(2,1)S(1)} %get-tuple-element.32.own_ref), channel_id=1, source_target_pairs={{192,0},{193,1},{194,2},{195,3},{196,4},{197,5},{198,6},{199,7},{2... | collective-permute-start | bytes 786440 | tf_op jit(solution)/shard_map/inner/ppermute | solution.py:281
  31.0 17.8 %collective-permute-start.4 = (bf16[2,256,256]{2,1,0:T(8,128)(2,1)S(1)}, bf16[2,256,256]{2,1,0:T(8,128)(2,1)S(1)}, u32[]{:S(2)}, u32[]{:S(2)}) collective-permute-start(bf16[2,256,256]{2,1,0:T(8,128)(2,1)S(1)} %get-tuple-element.32.own_ref), channel_id=1, source_target_pairs={{192,64},{193,65},{194,66},{195,67},{196,68},{197,69},{198,70},{19... | collective-permute-start | bytes 786440 | tf_op jit(solution)/shard_map/inner/ppermute | solution.py:281
  32.3 16.5 %collective-permute-start.5 = (bf16[2,256,256]{2,1,0:T(8,128)(2,1)S(1)}, bf16[2,256,256]{2,1,0:T(8,128)(2,1)S(1)}, u32[]{:S(2)}, u32[]{:S(2)}) collective-permute-start(bf16[2,256,256]{2,1,0:T(8,128)(2,1)S(1)} %get-tuple-element.32.own_ref), channel_id=1, source_target_pairs={{192,128},{193,129},{194,130},{195,131},{196,132},{197,133},{198,1... | collective-permute-start | bytes 786440 | tf_op jit(solution)/shard_map/inner/ppermute | solution.py:281
  38.7 15.2 %collective-permute-start.10 = (f32[8,32,128]{2,1,0:T(8,128)S(1)}, f32[8,32,128]{2,1,0:T(8,128)S(1)}, u32[]{:S(2)}, u32[]{:S(2)}) collective-permute-start(f32[8,32,128]{2,1,0:T(8,128)S(1)} %get-tuple-element.44), channel_id=1, source_target_pairs={{0,8},{8,0},{1,9},{9,1},{2,10},{10,2},{3,11},{11,3},{4,12},{12,4},... | collective-permute-start | bytes 393224 | tf_op jit(solution)/shard_map/inner/ppermute | solution.py:288
  40.0 13.9 %collective-permute-start.11 = (f32[8,32,128]{2,1,0:T(8,128)S(1)}, f32[8,32,128]{2,1,0:T(8,128)S(1)}, u32[]{:S(2)}, u32[]{:S(2)}) collective-permute-start(f32[8,32,128]{2,1,0:T(8,128)S(1)} %get-tuple-element.46), channel_id=1, source_target_pairs={{0,48},{16,32},{32,16},{48,0},{1,49},{17,33},{33,17},{49,1},{2,50}... | collective-permute-start | bytes 393224 | tf_op jit(solution)/shard_map/inner/ppermute | solution.py:294
  45.3 8.6 %all-to-all-start.1 = ((f32[64,4,128]{2,1,0:T(4,128)}), f32[64,4,128]{2,1,0:T(4,128)S(1)}, u32[]{:S(2)}, u32[]{:S(2)}) async-start(f32[64,4,128]{2,1,0:T(4,128)} %pick.1), calls=%async_computation.1 | async-start | bytes 262144 | tf_op jit(solution)/shard_map/pick/all_to_all | solution.py:278
  86.6 13.2 %collective-permute-start.12 = (f32[16,256]{1,0:T(8,128)S(1)}, f32[16,256]{1,0:T(8,128)S(1)}, u32[]{:S(2)}, u32[]{:S(2)}) collective-permute-start(f32[16,256]{1,0:T(8,128)S(1)} %get-tuple-element.51), channel_id=1, source_target_pairs={{0,64},{64,128},{128,192},{192,0},{1,65},{65,129},{129,193},{193,1... | collective-permute-start | bytes 49160 | tf_op jit(solution)/shard_map/close/ppermute | solution.py:281
  95.6 3.4 %collective-permute-start.13 = (f32[4,128]{1,0:T(4,128)S(1)}, f32[4,128]{1,0:T(4,128)S(1)}, u32[]{:S(2)}, u32[]{:S(2)}) collective-permute-start(f32[4,128]{1,0:T(4,128)S(1)} %get-tuple-element.52), channel_id=1, source_target_pairs={{64,192},{128,0},{65,193},{129,1},{66,194},{130,2},{67,195},{131,3... | collective-permute-start | bytes 6152 | tf_op jit(solution)/shard_map/close/ppermute | solution.py:281
  97.7 2.1 %collective-permute-start.14 = (f32[4,128]{1,0:T(4,128)S(1)}, f32[4,128]{1,0:T(4,128)S(1)}, u32[]{:S(2)}, u32[]{:S(2)}) collective-permute-start(f32[4,128]{1,0:T(4,128)S(1)} %get-tuple-element.53), channel_id=1, source_target_pairs={{0,192},{64,0},{1,193},{65,1},{2,194},{66,2},{3,195},{67,3},{4,196... | collective-permute-start | bytes 6152 | tf_op jit(solution)/shard_map/close/ppermute | solution.py:281

commit v4 on v3

--- a/solution.py
+++ b/solution.py
@@ -1,3 +1,5 @@
+import functools
+
 import jax
 import jax.numpy as jnp
 from jax import lax
@@ -51,52 +53,52 @@
     return jnp.where(iota(shape, 1) == iota(shape, 0) * groups + group, 1.0, 0.0).astype(BF16)
 
 
-def deal_kernel(planes_ref, map_ref, *out_refs):
-    digits_ref, first_ref, out_refs = out_refs[-1], out_refs[-2], out_refs[:-2]
-    groups, width, bands = len(out_refs) + 1, planes_ref.shape[2], planes_ref.shape[3]
+def deal_kernel(planes_ref, *out_refs):
+    plane_ref, first_ref, out_refs = planes_ref.at[0], out_refs[-1], out_refs[:-1]
+    groups, bands = len(out_refs) + 1, plane_ref.shape[2]
     blocks = bands // groups
     for j, out_ref in enumerate(out_refs):
         for part in range(2):
-            dealt = across(dealt_to(j, groups, bands), planes_ref[0, part], ((1,), (1,)))
+            dealt = across(dealt_to(j, groups, bands), plane_ref[part], ((1,), (1,)))
             out_ref[pl.ds(part * blocks, blocks), :] = dealt.astype(BF16)
-    first_ref[...] = planes_ref[0]
-    index = map_ref[...]
-    per = width // LANES
-    for i, digit in enumerate((index // width, index % width)):
-        for c in range(per):
-            digits_ref[pl.ds(i * per + c, 1), :] = digit[:, c * LANES : (c + 1) * LANES].astype(F32)
-
-
-def terms_kernel(*refs):
-    planes_ref, arriving_ref, *along_refs = refs[-8:-4]
-    beside_refs, last_ref, prod_ref = refs[-4:-2], refs[-2], refs[-1]
-    count, _, rows, bands = planes_ref.shape
-    half, per = count // 2, 2 * bands // LANES
-    size = along_refs[0].shape[0] // 4
+    first_ref[...] = plane_ref[...]
+
+
+def terms_kernel(late, *refs):
+    if late:
+        planes_ref, arriving_ref, *out_refs, prod_ref = refs[-5:]
+        count = planes_ref.shape[0]
+        planes = [planes_ref.at[k] for k in range(count // 2, count)] + [arriving_ref]
+    else:
+        planes_ref, *out_refs, last_ref, prod_ref = refs[-5:]
+        count = planes_ref.shape[0]
+        planes = [planes_ref.at[k] for k in range(count // 2 + 1)]
+        last_ref[...] = planes_ref[count - 1]
+    _, rows, bands = planes[0].shape
+    per, size = 2 * bands // LANES, out_refs[0].shape[0] // 4
     share = bands // (8 * size)
     here, side = lax.axis_index("x"), lax.axis_index("y_lo")
     near = here + 1 - 2 * lax.rem(here, 2)
     sides = (side, 1 - side)
-    for k in range(count):
-        left = planes_ref[k].reshape(2 * rows, bands)
-        after = arriving_ref if k == count - 1 else planes_ref.at[k + 1]
-        prod_ref[...] = across(left, wide(after[0], after[1]), ((0,), (0,)))
-        if k < half:
-            order = [[(x, s) for x in xs for s in sides] for xs in ((here, 3 - here), (near, 3 - near))]
-        else:
-            order = [[(x, s) for x in (here, 3 - here, near, 3 - near)] for s in sides]
-        for out_ref, places in zip(along_refs if k < half else beside_refs, order):
+    if late:
+        order = [[(x, s) for x in (here, 3 - here, near, 3 - near)] for s in sides]
+    else:
+        order = [[(x, s) for x in xs for s in sides] for xs in ((here, 3 - here), (near, 3 - near))]
+    for k in range(2):
+        left, after = planes[k], planes[k + 1]
+        prod_ref[...] = across(left[...].reshape(2 * rows, bands), wide(after[0], after[1]), ((0,), (0,)))
+        for out_ref, places in zip(out_refs, order):
             for p, (x, s) in enumerate(places):
                 first = pl.multiple_of((2 * x + s) * size * share, size * share)
                 mine = prod_ref.at[pl.ds(first, size * share)]
                 for i in range(size):
                     for c in range(per):
                         piece = mine[pl.ds(i * share, share), pl.ds(c * LANES, LANES)]
-                        out_ref[p * size + i, pl.ds(((k % half) * per + c) * share, share), :] = piece
-    last_ref[...] = planes_ref[count - 1]
-
-
-def load_kernel(after_ref, digits_ref, own_ref, arriving_ref, *refs):
+                        out_ref[p * size + i, pl.ds((k * per + c) * share, share), :] = piece
+
+
+def load_kernel(*refs):
+    digits_ref, own_ref, arriving_ref, *refs = refs[2:]
     out_ref = refs[-1]
     blocks = out_ref.shape[0]
     here, groups = lax.axis_index(KZ), len(refs) + 1
@@ -124,15 +126,16 @@
 
     table = jnp.concatenate([part(0), part(1)], axis=0).astype(BF16)
     hi_ref[...] = part(2).astype(jnp.int32)
-    lo_ref[...] = part(3).astype(jnp.int32)
-    rows, owners = iota((width, width), 0), iota((blocks, width), 0)
+    lo_ref[...] = part(3)
+    rows, owners = iota((width, width), 0).astype(F32).astype(BF16), iota((blocks, width), 0)
+    one, zero = jnp.ones((), BF16), jnp.zeros((), BF16)
 
     def step(t, carry):
         base = pl.multiple_of(t * 8, 8)
-        his, los = hi_ref[pl.ds(base, 8), :], lo_ref[pl.ds(base, 8), :]
+        his, los = hi_ref[pl.ds(base, 8), :], lo_ref[pl.ds(base, 8), :].astype(BF16)
         real_rows, imag_rows = [], []
         for r in range(8):
-            hot = jnp.where(rows == los[r : r + 1, :], 1.0, 0.0).astype(BF16)
+            hot = jnp.where(rows == los[r : r + 1, :], one, zero)
             found = jnp.dot(table, hot, preferred_element_type=F32)
             mine = owners == his[r : r + 1, :]
             real_rows.append(jnp.sum(jnp.where(mine, found[:blocks], 0.0), axis=0, keepdims=True))
@@ -147,7 +150,7 @@
 
 
 def fold_kernel(*refs):
-    in_refs, out_refs = refs[:4], refs[4:]
+    in_refs, out_refs = refs[-8:-4], refs[-4:]
     half = out_refs[0].shape[0]
     for i in range(4):
         kept, got = in_refs[i // 2 * 2], in_refs[i // 2 * 2 + 1]
@@ -155,8 +158,14 @@
         out_refs[i][...] = kept[part] + got[part]
 
 
-def merge_kernel(*refs):
-    picked_ref, sums_refs, out_ref = refs[-6], refs[-5:-1], refs[-1]
+def pass_kernel(final_ref, *refs):
+    fold_kernel(*refs[:-1])
+    refs[-1][...] = final_ref[...]
+
+
+def merge_kernel(final_ref, over_ref, picked_ref, *refs):
+    sums_refs, out_ref, hand_ref = refs[:-2], refs[-2], refs[-1]
+    hand_ref[...] = jnp.where(lax.axis_index(KZ) == 0, over_ref[...], final_ref[...])
     far, rows = out_ref.shape[0], sums_refs[0].shape[1]
     near, chunks = picked_ref.shape[0] // far, picked_ref.shape[1]
     for p in range(near):
@@ -166,8 +175,8 @@
         out_ref[:, pl.ds(near * chunks + i * rows, rows), :] = sums_refs[2 * i][...] + sums_refs[2 * i + 1][...]
 
 
-def edge_kernel(got_ref, own_ref, *refs):
-    sent_refs, (plus_ref, out_ref, moved_ref, turn_ref, rows_ref) = refs[:-5], refs[-5:]
+def edge_kernel(got_ref, own_ref, other_ref, *refs):
+    (plus_ref, out_ref, moved_ref, turn_ref, rows_ref) = refs
     count, _, share, bands = plus_ref.shape
     blocks, width = moved_ref.shape
     far = got_ref.shape[0]
@@ -190,9 +199,7 @@
     tiles = jnp.concatenate([tiles[i * blocks : (i + 1) * blocks] for i in range(share)], axis=1)
     out_ref[pl.ds(8, blocks, stride=9), :] = tiles
 
-    final = own_ref[...]
-    for j, ref in enumerate(sent_refs):
-        final = jnp.where(here == j, ref[...], final)
+    final = jnp.where((here == 0) | (here == lax.axis_size(KZ) - 1), own_ref[...], other_ref[...])
     for p in range(near):
         for c in range(chunks):
             moved_ref[pl.ds(p * far, far), pl.ds(c * LANES, LANES)] = got_ref[:, p * chunks + c, :]
@@ -224,12 +231,10 @@
             minus_ref[k, o] = mirror[(2 * k + o) * share : (2 * k + o + 1) * share]
     for d, ref in enumerate(pay_refs):
         piece = jnp.where(lax.rem(lax.axis_index(KZ) + d, groups) == groups - 1, edge_n, edge_m)
+        ref[...] = jnp.zeros_like(ref)
         if d == 1:
-            ref[...] = jnp.zeros_like(ref)
             ref[pl.ds(0, 2 * share), :] = mirror[(count - 1) * 2 * share :]
-            ref[pl.ds(2 * share, share), pl.ds(0, LANES)] = piece
-        else:
-            ref[...] = piece
+        ref[pl.ds(2 * share, share), pl.ds(0, LANES)] = piece
 
 
 def close_kernel(plus_ref, minus_ref, *refs):
@@ -237,10 +242,7 @@
     count, _, share, bands = plus_ref.shape
     groups = len(got_refs)
     here = lax.axis_index(KZ)
-    got = [
-        ref[pl.ds(2 * share, share), pl.ds(0, LANES)] if d == 1 else ref[...]
-        for d, ref in enumerate(got_refs)
-    ]
+    got = [ref[pl.ds(2 * share, share), pl.ds(0, LANES)] for ref in got_refs]
     plus_out[...] = plus_ref[...]
     for k in range(1, count):
         minus_out[k] = minus_ref[k - 1]
@@ -295,55 +297,62 @@
 
     plane = (planes.shape[1:], BF16)
     with jax.named_scope("deal"):
-        digits = ((2 * rows // LANES, LANES), F32)
-        *dealt, first, digits = call(
-            deal_kernel, "deal", [((2 * n_pw, rows), BF16)] * (share - 1) + [plane, digits], (planes, pw_map),
+        *dealt, first = call(
+            deal_kernel, "deal", [((2 * n_pw, rows), BF16)] * (share - 1) + [plane], (planes,),
             flops=4 * rows * bands * bands,
         )
-        dealt = [dealt[0]] + [sent(dealt[j], [(0, j)]) for j in range(1, n_kz - 1)]
+        dealt = [dealt[0]] + [sent(dealt[j], [(0, j)]) for j in range(n_kz - 2, 0, -1)]
+        digits = jnp.stack([pw_map[0] // rows, pw_map[0] % rows]).astype(F32).reshape(-1, LANES)
 
     with jax.named_scope("inner"):
         arriving = around(first, n_kz - 1)
         chunks = kz_dev * bands * share // LANES
-        part = ((n_pw // 2, chunks, LANES), F32)
-        *sums, final = call(
-            terms_kernel, "terms", [part] * 4 + [plane], (planes, arriving), after=dealt[1:],
-            flops=kz_dev * 8 * rows * bands * bands, scratch=[pltpu.VMEM((bands, 2 * bands), F32)],
-        )
-        terms = sums[0]
-        sums = (sums[0], near(sums[1]), sums[2], beside(sums[3]))
-        finals = [sent(final, [(n_kz - 1, j)]) for j in range(n_kz - 1)]
+
+        def make_terms(late, operands, after, more):
+            return call(
+                functools.partial(terms_kernel, late), "terms", [((n_pw // 2, chunks, LANES), F32)] * 2 + more,
+                operands, after=after, flops=16 * rows * bands * bands, scratch=[pltpu.VMEM((bands, 2 * bands), F32)],
+            )
+
+        *early, final = make_terms(False, (planes,), (), [plane])
+        late = make_terms(True, (planes, arriving), dealt[1:], [])
+        sums = (early[0], near(early[1]), late[0], beside(late[1]))
 
     with jax.named_scope("deal"):
         (load,) = call(
             load_kernel, "load", [((n_pw, 4 * rows // LANES, LANES), F32)], (digits, dealt[0], arriving, *dealt[1:]),
-            after=(terms,),
+            after=(early[0], late[0]),
         )
         spread = swap(load, PW)
     with jax.named_scope("pick"):
         (picked,) = call(
             pick_kernel, "pick", [((n_pw, 2 * rows // LANES, LANES), F32)], (spread,),
-            flops=4 * n_pw * n_pw * rows * rows, scratch=[pltpu.VMEM((n_pw, rows), jnp.int32)] * 2,
+            flops=4 * n_pw * n_pw * rows * rows,
+            scratch=[pltpu.VMEM((n_pw, rows), jnp.int32), pltpu.VMEM((n_pw, rows), F32)],
         )
 
     with jax.named_scope("inner"):
-        sums = call(fold_kernel, "fold", [((n_pw // 4, chunks, LANES), F32)] * 4, sums)
+        *sums, final = call(
+            pass_kernel, "fold", [((n_pw // 4, chunks, LANES), F32)] * 4 + [plane], (final, *sums)
+        )
+        over = sent(final, [(n_kz - 1, 0)])
         sums = (sums[0], mirrored(sums[1]), sums[2], near(sums[3]))
-        sums = call(fold_kernel, "fold", [((n_pw // 8, chunks, LANES), F32)] * 4, sums)
+        sums = call(fold_kernel, "fold", [((n_pw // 8, chunks, LANES), F32)] * 4, sums, after=(picked,))
         sums = (sums[0], beside(sums[1]), sums[2], mirrored(sums[3]))
     with jax.named_scope("pick"):
         picked = swap(picked, ("x", "y_lo"))
     with jax.named_scope("inner"):
-        (merged,) = call(
-            merge_kernel, "merge", [((n_z, n_pw // n_z * 2 * rows // LANES + 2 * chunks, LANES), F32)],
-            (picked, *sums), after=finals,
-        )
+        merged, hand = call(
+            merge_kernel, "merge", [((n_z, n_pw // n_z * 2 * rows // LANES + 2 * chunks, LANES), F32), plane],
+            (final, over, picked, *sums),
+        )
+        across_chip = sent(hand, [(0, 1), (n_kz - 1, n_kz - 2)])
         got = swap(merged, "z")
 
     with jax.named_scope("edge"):
         rows_out = ((kz_dev, 2, share, bands), F32)
         plus, out = call(
-            edge_kernel, "edge", [rows_out, ((n_pw * 9, LANES), F32)], (got, final, *finals),
+            edge_kernel, "edge", [rows_out, ((n_pw * 9, LANES), F32)], (got, hand, across_chip),
             flops=8 * n_pw * rows * bands,
             scratch=[
                 pltpu.VMEM((n_pw, 2 * rows), F32),
@@ -354,12 +363,10 @@
         back = swap(out.reshape(n_pw, 1, 9 * LANES), PW).reshape(n_pw * 9, LANES)
 
     with jax.named_scope("close"):
-        piece = ((share, LANES), F32)
-        long = ((4 * share, bands), F32)
-        minus, *pieces = call(gather_kernel, "gather", [rows_out, piece, long] + [piece] * (n_kz - 2), (back,))
-        pieces = [pieces[0]] + [
-            around(pieces[d], d, None if d == 1 else (0, n_kz - 1)) for d in range(1, n_kz)
-        ]
+        pieces = [((4 * share, bands), F32)] * 2 + [((6 * share, bands), F32)] * (n_kz - 2)
+        minus, *pieces = call(gather_kernel, "gather", [rows_out] + pieces, (back,))
+        for d in (2, 3, 1):
+            pieces[d] = around(pieces[d], d, None if d == 1 else (0, n_kz - 1))
         plus, minus = call(close_kernel, "close", [rows_out] * 2, (plus, minus, *pieces), far=(0, 1))
     return plus[:, None], minus[:, None]
 

time: 101 us -> 97.5 us (0.965)
  blocking collectives: 31.4 us -> 25.8 us
  waiting for transfers between devices: 14.8 us -> 19.6 us
  starting transfers between devices: 43.1 us -> 39 us
  Pallas kernels: 8.36 us -> 9.88 us
    all_to_all x2, blocking collectives: 31.4 us -> 25.8 us  [swap(): return lax.all_to_all(x, axes, 0, 0, tiled=True)]
    all_to_all x2, waiting for transfers between devices: 5.16 us -> 10.6 us  [swap(): return lax.all_to_all(x, axes, 0, 0, tiled=True)]
    ppermute x9 -> x8, waiting for transfers between devices: 3.96 us -> 8.94 us  [sent(): return lax.ppermute(x, KZ, pairs)]
    ppermute x2, waiting for transfers between devices: 4.89 us -> 0.01 us  [mirrored(): return lax.ppermute(x, 'x', [(i, n_x - 1 - i) for i in range(n_x)])]
    ppermute x9 -> x8, starting transfers between devices: 20.3 us -> 18.7 us  [sent(): return lax.ppermute(x, KZ, pairs)]
    pallas_call x10 -> x11, Pallas kernels: 8.36 us -> 9.88 us  [call(): pl.pallas_call(kernel, out_shape=outs, in_specs=[AFTER] * len(after) + [V...]
    ppermute x2, starting transfers between devices: 1.22 us -> 0.1 us  [near(): return lax.ppermute(x, 'x', [(i, i ^ 1) for i in range(n_x)])]
    ppermute x2, starting transfers between devices: 4.28 us -> 3.16 us  [mirrored(): return lax.ppermute(x, 'x', [(i, n_x - 1 - i) for i in range(n_x)])]
  transfers between devices with their start and end apart: 17 -> 16, of which waited for: 6 -> 5; matrix products, arithmetic and copies ran while one was open for 0% -> 0% of each run, Pallas kernels for 5% -> 7%
where the time goes in v4:
time: 97.5 us; the launch traced here: 97 us
  starting transfers between devices  39 us (40%)
  blocking collectives  25.8 us (26%)
  waiting for transfers between devices  19.6 us (20%)
  Pallas kernels  9.88 us (10%)
  local copies, waits for them, and re-layouts  1.95 us (2%)
    all_to_all x2, blocking collectives, swap(): return lax.all_to_all(x, axes, 0, 0, tiled=True)  25.8 us
    ppermute x8, starting transfers between devices, sent(): return lax.ppermute(x, KZ, pairs)  18.7 us
    all_to_all x2, starting transfers between devices, swap(): return lax.all_to_all(x, axes, 0, 0, tiled=True)  15.6 us
    all_to_all x2, waiting for transfers between devices, swap(): return lax.all_to_all(x, axes, 0, 0, tiled=True)  10.6 us
    pallas_call x11, Pallas kernels, call(): pl.pallas_call(kernel, out_shape=outs, in_specs=[AFTER] * len(after) + [V...  9.88 us
    ppermute x8, waiting for transfers between devices, sent(): return lax.ppermute(x, KZ, pairs)  8.94 us
    ppermute x2, starting transfers between devices, mirrored(): return lax.ppermute(x, 'x', [(i, n_x - 1 - i) for i in range(n_x)])  3.16 us
  transfers between devices with their start and end apart: 16, of which 5 were waited for; matrix products, arithmetic and copies ran while one was open for 0% of the time, Pallas kernels for 7%

profile of v4, /device:TPU:1, one launch (start us, length us, event | category | flops | bytes accessed | tf_op | source)
XLA Modules:
  0.0 97.0 jit_solution(13861657734150957194)
XLA Ops:
  0.6 1.4 %copy.12 = bf16[4,1,256,2,256]{4,2,3,0,1:T(8,128)(2,1)S(1)} copy(bf16[4,1,256,2,256]{4,3,2,1,0:T(2,128)(2,1)} %param.2) | data formatting | bytes 2097152 | tf_op args[0]
  2.0 0.4 deal.1
  2.4 3.3 %collective-permute-start.3 = (bf16[2,256,256]{2,1,0:T(8,128)(2,1)S(1)}, bf16[2,256,256]{2,1,0:T(8,128)(2,1)S(1)}, u32[]{:S(2)}, u32[]{:S(2)}) collective-permute-start(bf16[2,256,256]{2,1,0:T(8,128)(2,1)S(1)} %get-tuple-element.36), channel_id=1, source_target_pairs={{0,192},{64,0},{128,64},{192,128},{1,193},{65,1},{129,65},{193,129... | collective-permute-start | bytes 786440 | tf_op jit(solution)/shard_map/inner/ppermute | solution.py:283
  5.7 0.7 collective-permute-start.1
  6.3 1.3 %collective-permute-start.2 = (bf16[128,256]{1,0:T(8,128)(2,1)S(1)}, bf16[128,256]{1,0:T(8,128)(2,1)S(1)}, u32[]{:S(2)}, u32[]{:S(2)}) collective-permute-start(bf16[128,256]{1,0:T(8,128)(2,1)S(1)} %get-tuple-element.35), channel_id=1, source_target_pairs={{0,64},{1,65},{2,66},{3,67},{4,68},{5,69},{6,70},{7,71},{8,72},{9,... | collective-permute-start | bytes 196616 | tf_op jit(solution)/shard_map/deal/ppermute | solution.py:283
  7.6 0.6 terms.2
  8.2 0.0 copy-start
  8.2 0.1 collective-permute-start
  8.3 0.6 copy-done
  8.9 0.0 collective-permute-done.1.refs_0_.refs_5_
  8.9 2.2 %collective-permute-done.2.refs_1_.refs_6_ = bf16[128,256]{1,0:T(8,128)(2,1)S(1)} collective-permute-done((bf16[128,256]{1,0:T(8,128)(2,1)S(1)}, bf16[128,256]{1,0:T(8,128)(2,1)S(1)}, u32[]{:S(2)}, u32[]{:S(2)}) %collective-permute-start.2) | collective-permute-done | bytes 65568 | tf_op jit(solution)/shard_map/deal/ppermute | solution.py:283
  11.1 0.0 collective-permute-done.3.refs_3_.refs_4_
  11.1 1.4 %terms.3 = (f32[32,32,128]{2,1,0:T(8,128)S(1)}, f32[32,32,128]{2,1,0:T(8,128)}) custom-call(bf16[128,256]{1,0:T(8,128)(2,1)S(1)} %collective-permute-done.1.refs_0_.refs_5_, bf16[128,256]{1,0:T(8,128)(2,1)S(1)} %collective-permute-done.2.refs_1_.refs_6_, bf16[4,2,256,256]{3,2,1,0:T(8,128)(2,1)S(1)} %bitcast.15, ...), custom_call_target="tpu_custom_call" | custom-call | flops 268435456 | bytes 2621440 | tf_op jit(solution)/shard_map/inner/terms/pallas_call | solution.py:39
  12.5 1.0 %collective-permute-start.4 = (f32[32,32,128]{2,1,0:T(8,128)}, f32[32,32,128]{2,1,0:T(8,128)S(1)}, u32[]{:S(2)}, u32[]{:S(2)}) collective-permute-start(f32[32,32,128]{2,1,0:T(8,128)} %get-tuple-element.38), channel_id=1, source_target_pairs={{0,8},{8,0},{1,9},{9,1},{2,10},{10,2},{3,11},{11,3},{4,12},{12,4},... | collective-permute-start | bytes 1572872 | tf_op jit(solution)/shard_map/inner/ppermute | solution.py:290
  13.5 1.0 %load.1 = f32[64,8,128]{2,1,0:T(8,128)} custom-call(f32[32,32,128]{2,1,0:T(8,128)S(1)} %get-tuple-element.32.refs_0_, f32[32,32,128]{2,1,0:T(8,128)S(1)} %get-tuple-element.37.refs_2_.refs_1_, f32[4,128]{1,0:T(4,128)S(1)} %convert_element_type.8.refs_2_, bf16[128,256]{1,0:T(8,128)(2,1)S(1)} %get-tuple-element.40.refs_3_, ...), custom_call_target="tpu_custom_call" | custom-call | bytes 921600 | tf_op jit(solution)/shard_map/deal/load/pallas_call | solution.py:39
  14.5 11.8 %all-to-all-start = ((f32[64,8,128]{2,1,0:T(8,128)}), f32[64,8,128]{2,1,0:T(8,128)S(1)}, u32[]{:S(2)}, u32[]{:S(2)}) async-start(f32[64,8,128]{2,1,0:T(8,128)} %load.1), calls=%async_computation | async-start | bytes 524288 | tf_op jit(solution)/shard_map/deal/all_to_all | solution.py:280
  26.3 0.0 collective-permute-done.refs_1_
  26.3 0.0 collective-permute-done.4.refs_3_
  26.3 0.9 fold.2
  27.3 2.4 %collective-permute-start.6 = (f32[16,32,128]{2,1,0:T(8,128)}, f32[16,32,128]{2,1,0:T(8,128)S(1)}, u32[]{:S(2)}, u32[]{:S(2)}) collective-permute-start(f32[16,32,128]{2,1,0:T(8,128)} %get-tuple-element.42), channel_id=1, source_target_pairs={{0,48},{16,32},{32,16},{48,0},{1,49},{17,33},{33,17},{49,1},{2,50}... | collective-permute-start | bytes 786440 | tf_op jit(solution)/shard_map/inner/ppermute | solution.py:296
  29.7 0.0 collective-permute-start.7
  29.7 0.7 collective-permute-start.5
  30.4 7.0 %all-to-all-done.spread_ref = f32[64,8,128]{2,1,0:T(8,128)S(1)} async-done(((f32[64,8,128]{2,1,0:T(8,128)}), f32[64,8,128]{2,1,0:T(8,128)S(1)}, u32[]{:S(2)}, u32[]{:S(2)}) %all-to-all-start) | async-done | bytes 262176 | tf_op jit(solution)/shard_map/deal/all_to_all | solution.py:280
  37.4 2.9 %pick.1.refs_0_ = f32[64,4,128]{2,1,0:T(4,128)S(1)} custom-call(f32[64,8,128]{2,1,0:T(8,128)S(1)} %all-to-all-done.spread_ref), custom_call_target="tpu_custom_call" | custom-call | flops 1073741824 | bytes 524288 | tf_op jit(solution)/shard_map/pick/pick/pallas_call | solution.py:39
  40.3 0.0 collective-permute-done.6.refs_2_
  40.3 0.0 collective-permute-done.7.refs_4_
  40.3 0.1 fold.3
  40.4 0.4 collective-permute-start.8
  40.8 0.7 collective-permute-start.9
  41.5 9.4 %all_to_all.20.picked_ref = f32[64,4,128]{2,1,0:T(4,128)S(1)} all-to-all(f32[64,4,128]{2,1,0:T(4,128)S(1)} %pick.1.refs_0_), channel_id=1, replica_groups=mesh['y_hi'=2,'core'=2,'x'=4,'y_lo'=2,'z'=8] {'x','y_lo'}, dimensions={0} | all-to-all | bytes 262144 | tf_op jit(solution)/shard_map/pick/all_to_all | solution.py:280
  50.9 0.0 collective-permute-done.5.over_ref
  50.9 0.0 collective-permute-done.8.refs_1_
  50.9 0.0 collective-permute-done.9.refs_3_
  50.9 0.8 merge.1
  51.8 3.8 %all-to-all-start.2 = ((f32[8,96,128]{2,1,0:T(8,128)}), f32[8,96,128]{2,1,0:T(8,128)S(1)}, u32[]{:S(2)}, u32[]{:S(2)}) async-start(f32[8,96,128]{2,1,0:T(8,128)} %get-tuple-element.49), calls=%async_computation.2 | async-start | bytes 786432 | tf_op jit(solution)/shard_map/inner/all_to_all | solution.py:280
  55.6 1.3 %collective-permute-start.10 = (bf16[2,256,256]{2,1,0:T(8,128)(2,1)S(1)}, bf16[2,256,256]{2,1,0:T(8,128)(2,1)S(1)}, u32[]{:S(2)}, u32[]{:S(2)}) collective-permute-start(bf16[2,256,256]{2,1,0:T(8,128)(2,1)S(1)} %get-tuple-element.50.own_ref), channel_id=1, source_target_pairs={{0,64},{192,128},{1,65},{193,129},{2,66},{194,130},{3,67},{195,131... | collective-permute-start | bytes 786440 | tf_op jit(solution)/shard_map/inner/ppermute | solution.py:283
  56.9 5.9 %collective-permute-done.10.other_ref = bf16[2,256,256]{2,1,0:T(8,128)(2,1)S(1)} collective-permute-done((bf16[2,256,256]{2,1,0:T(8,128)(2,1)S(1)}, bf16[2,256,256]{2,1,0:T(8,128)(2,1)S(1)}, u32[]{:S(2)}, u32[]{:S(2)}) %collective-permute-start.10) | collective-permute-done | bytes 262176 | tf_op jit(solution)/shard_map/inner/ppermute | solution.py:283
  62.7 3.7 %all-to-all-done.2.got_ref = f32[8,96,128]{2,1,0:T(8,128)S(1)} async-done(((f32[8,96,128]{2,1,0:T(8,128)}), f32[8,96,128]{2,1,0:T(8,128)S(1)}, u32[]{:S(2)}, u32[]{:S(2)}) %all-to-all-start.2) | async-done | bytes 393248 | tf_op jit(solution)/shard_map/inner/all_to_all | solution.py:280
  66.4 0.7 edge.1
  67.1 16.3 %all_to_all.21 = f32[64,1,1152]{2,1,0:T(1,128)S(1)} all-to-all(f32[64,1,1152]{2,1,0:T(1,128)S(1)} %bitcast.17), channel_id=1, replica_groups=mesh['y_hi'=2,'core'=2,'x'=4,'y_lo'=2,'z'=8] {'x','y_lo','z'}, dimensions={0} | all-to-all | bytes 589824 | tf_op jit(solution)/shard_map/edge/all_to_all | solution.py:280
  83.4 0.6 gather.1
  84.0 6.7 %collective-permute-start.12 = (f32[24,256]{1,0:T(8,128)S(1)}, f32[24,256]{1,0:T(8,128)S(1)}, u32[]{:S(2)}, u32[]{:S(2)}) collective-permute-start(f32[24,256]{1,0:T(8,128)S(1)} %get-tuple-element.56), channel_id=1, source_target_pairs={{64,192},{128,0},{65,193},{129,1},{66,194},{130,2},{67,195},{131,3... | collective-permute-start | bytes 73736 | tf_op jit(solution)/shard_map/close/ppermute | solution.py:283
  90.7 2.2 %collective-permute-start.13 = (f32[24,256]{1,0:T(8,128)S(1)}, f32[24,256]{1,0:T(8,128)S(1)}, u32[]{:S(2)}, u32[]{:S(2)}) collective-permute-start(f32[24,256]{1,0:T(8,128)S(1)} %get-tuple-element.57), channel_id=1, source_target_pairs={{0,192},{64,0},{1,193},{65,1},{2,194},{66,2},{3,195},{67,3},{4,196... | collective-permute-start | bytes 73736 | tf_op jit(solution)/shard_map/close/ppermute | solution.py:283
  92.9 2.6 %collective-permute-start.11 = (f32[16,256]{1,0:T(8,128)S(1)}, f32[16,256]{1,0:T(8,128)S(1)}, u32[]{:S(2)}, u32[]{:S(2)}) collective-permute-start(f32[16,256]{1,0:T(8,128)S(1)} %get-tuple-element.55), channel_id=1, source_target_pairs={{0,64},{64,128},{128,192},{192,0},{1,65},{65,129},{129,193},{193,1... | collective-permute-start | bytes 49160 | tf_op jit(solution)/shard_map/close/ppermute | solution.py:283
  95.5 0.9 collective-permute-done.11.refs_1_
  96.3 0.0 collective-permute-done.12.refs_2_
  96.4 0.0 collective-permute-done.13.refs_3_
  96.4 0.6 close.1
  (4 shorter events, 0.0 us)
Async XLA Ops:
  2.4 8.7 %collective-permute-start.3 = (bf16[2,256,256]{2,1,0:T(8,128)(2,1)S(1)}, bf16[2,256,256]{2,1,0:T(8,128)(2,1)S(1)}, u32[]{:S(2)}, u32[]{:S(2)}) collective-permute-start(bf16[2,256,256]{2,1,0:T(8,128)(2,1)S(1)} %get-tuple-element.36), channel_id=1, source_target_pairs={{0,192},{64,0},{128,64},{192,128},{1,193},{65,1},{129,65},{193,129... | collective-permute-start | bytes 786440 | tf_op jit(solution)/shard_map/inner/ppermute | solution.py:283
  5.7 3.2 %collective-permute-start.1 = (bf16[128,256]{1,0:T(8,128)(2,1)S(1)}, bf16[128,256]{1,0:T(8,128)(2,1)S(1)}, u32[]{:S(2)}, u32[]{:S(2)}) collective-permute-start(bf16[128,256]{1,0:T(8,128)(2,1)S(1)} %get-tuple-element.34), channel_id=1, source_target_pairs={{0,128},{1,129},{2,130},{3,131},{4,132},{5,133},{6,134},{7,135},{8... | collective-permute-start | bytes 196616 | tf_op jit(solution)/shard_map/deal/ppermute | solution.py:283
  6.3 4.7 %collective-permute-start.2 = (bf16[128,256]{1,0:T(8,128)(2,1)S(1)}, bf16[128,256]{1,0:T(8,128)(2,1)S(1)}, u32[]{:S(2)}, u32[]{:S(2)}) collective-permute-start(bf16[128,256]{1,0:T(8,128)(2,1)S(1)} %get-tuple-element.35), channel_id=1, source_target_pairs={{0,64},{1,65},{2,66},{3,67},{4,68},{5,69},{6,70},{7,71},{8,72},{9,... | collective-permute-start | bytes 196616 | tf_op jit(solution)/shard_map/deal/ppermute | solution.py:283
  8.2 0.7 copy-start
  8.2 18.1 %collective-permute-start = (f32[32,32,128]{2,1,0:T(8,128)S(1)}, f32[32,32,128]{2,1,0:T(8,128)S(1)}, u32[]{:S(2)}, u32[]{:S(2)}) collective-permute-start(f32[32,32,128]{2,1,0:T(8,128)S(1)} %get-tuple-element.33), channel_id=1, source_target_pairs={{0,16},{16,0},{32,48},{48,32},{1,17},{17,1},{33,49},{49,33},{2,18}... | collective-permute-start | bytes 1572872 | tf_op jit(solution)/shard_map/inner/ppermute | solution.py:293
  12.5 13.9 %collective-permute-start.4 = (f32[32,32,128]{2,1,0:T(8,128)}, f32[32,32,128]{2,1,0:T(8,128)S(1)}, u32[]{:S(2)}, u32[]{:S(2)}) collective-permute-start(f32[32,32,128]{2,1,0:T(8,128)} %get-tuple-element.38), channel_id=1, source_target_pairs={{0,8},{8,0},{1,9},{9,1},{2,10},{10,2},{3,11},{11,3},{4,12},{12,4},... | collective-permute-start | bytes 1572872 | tf_op jit(solution)/shard_map/inner/ppermute | solution.py:290
  14.5 22.8 %all-to-all-start = ((f32[64,8,128]{2,1,0:T(8,128)}), f32[64,8,128]{2,1,0:T(8,128)S(1)}, u32[]{:S(2)}, u32[]{:S(2)}) async-start(f32[64,8,128]{2,1,0:T(8,128)} %load.1), calls=%async_computation | async-start | bytes 524288 | tf_op jit(solution)/shard_map/deal/all_to_all | solution.py:280
  27.3 13.0 %collective-permute-start.6 = (f32[16,32,128]{2,1,0:T(8,128)}, f32[16,32,128]{2,1,0:T(8,128)S(1)}, u32[]{:S(2)}, u32[]{:S(2)}) collective-permute-start(f32[16,32,128]{2,1,0:T(8,128)} %get-tuple-element.42), channel_id=1, source_target_pairs={{0,48},{16,32},{32,16},{48,0},{1,49},{17,33},{33,17},{49,1},{2,50}... | collective-permute-start | bytes 786440 | tf_op jit(solution)/shard_map/inner/ppermute | solution.py:296
  29.7 10.6 %collective-permute-start.7 = (f32[16,32,128]{2,1,0:T(8,128)}, f32[16,32,128]{2,1,0:T(8,128)S(1)}, u32[]{:S(2)}, u32[]{:S(2)}) collective-permute-start(f32[16,32,128]{2,1,0:T(8,128)} %get-tuple-element.44), channel_id=1, source_target_pairs={{0,16},{16,0},{32,48},{48,32},{1,17},{17,1},{33,49},{49,33},{2,18}... | collective-permute-start | bytes 786440 | tf_op jit(solution)/shard_map/inner/ppermute | solution.py:293
  29.7 21.2 %collective-permute-start.5 = (bf16[2,256,256]{2,1,0:T(8,128)(2,1)S(1)}, bf16[2,256,256]{2,1,0:T(8,128)(2,1)S(1)}, u32[]{:S(2)}, u32[]{:S(2)}) collective-permute-start(bf16[2,256,256]{2,1,0:T(8,128)(2,1)S(1)} %get-tuple-element.39.final_ref), channel_id=1, source_target_pairs={{192,0},{193,1},{194,2},{195,3},{196,4},{197,5},{198,6},{199,7},{2... | collective-permute-start | bytes 786440 | tf_op jit(solution)/shard_map/inner/ppermute | solution.py:283
  40.4 10.6 %collective-permute-start.8 = (f32[8,32,128]{2,1,0:T(8,128)S(1)}, f32[8,32,128]{2,1,0:T(8,128)S(1)}, u32[]{:S(2)}, u32[]{:S(2)}) collective-permute-start(f32[8,32,128]{2,1,0:T(8,128)S(1)} %get-tuple-element.46), channel_id=1, source_target_pairs={{0,8},{8,0},{1,9},{9,1},{2,10},{10,2},{3,11},{11,3},{4,12},{12,4},... | collective-permute-start | bytes 393224 | tf_op jit(solution)/shard_map/inner/ppermute | solution.py:290
  40.8 10.2 %collective-permute-start.9 = (f32[8,32,128]{2,1,0:T(8,128)S(1)}, f32[8,32,128]{2,1,0:T(8,128)S(1)}, u32[]{:S(2)}, u32[]{:S(2)}) collective-permute-start(f32[8,32,128]{2,1,0:T(8,128)S(1)} %get-tuple-element.48), channel_id=1, source_target_pairs={{0,48},{16,32},{32,16},{48,0},{1,49},{17,33},{33,17},{49,1},{2,50}... | collective-permute-start | bytes 393224 | tf_op jit(solution)/shard_map/inner/ppermute | solution.py:296
  51.8 14.6 %all-to-all-start.2 = ((f32[8,96,128]{2,1,0:T(8,128)}), f32[8,96,128]{2,1,0:T(8,128)S(1)}, u32[]{:S(2)}, u32[]{:S(2)}) async-start(f32[8,96,128]{2,1,0:T(8,128)} %get-tuple-element.49), calls=%async_computation.2 | async-start | bytes 786432 | tf_op jit(solution)/shard_map/inner/all_to_all | solution.py:280
  55.6 7.2 %collective-permute-start.10 = (bf16[2,256,256]{2,1,0:T(8,128)(2,1)S(1)}, bf16[2,256,256]{2,1,0:T(8,128)(2,1)S(1)}, u32[]{:S(2)}, u32[]{:S(2)}) collective-permute-start(bf16[2,256,256]{2,1,0:T(8,128)(2,1)S(1)} %get-tuple-element.50.own_ref), channel_id=1, source_target_pairs={{0,64},{192,128},{1,65},{193,129},{2,66},{194,130},{3,67},{195,131... | collective-permute-start | bytes 786440 | tf_op jit(solution)/shard_map/inner/ppermute | solution.py:283
  84.0 12.4 %collective-permute-start.12 = (f32[24,256]{1,0:T(8,128)S(1)}, f32[24,256]{1,0:T(8,128)S(1)}, u32[]{:S(2)}, u32[]{:S(2)}) collective-permute-start(f32[24,256]{1,0:T(8,128)S(1)} %get-tuple-element.56), channel_id=1, source_target_pairs={{64,192},{128,0},{65,193},{129,1},{66,194},{130,2},{67,195},{131,3... | collective-permute-start | bytes 73736 | tf_op jit(solution)/shard_map/close/ppermute | solution.py:283
  90.7 5.6 %collective-permute-start.13 = (f32[24,256]{1,0:T(8,128)S(1)}, f32[24,256]{1,0:T(8,128)S(1)}, u32[]{:S(2)}, u32[]{:S(2)}) collective-permute-start(f32[24,256]{1,0:T(8,128)S(1)} %get-tuple-element.57), channel_id=1, source_target_pairs={{0,192},{64,0},{1,193},{65,1},{2,194},{66,2},{3,195},{67,3},{4,196... | collective-permute-start | bytes 73736 | tf_op jit(solution)/shard_map/close/ppermute | solution.py:283
  92.9 3.5 %collective-permute-start.11 = (f32[16,256]{1,0:T(8,128)S(1)}, f32[16,256]{1,0:T(8,128)S(1)}, u32[]{:S(2)}, u32[]{:S(2)}) collective-permute-start(f32[16,256]{1,0:T(8,128)S(1)} %get-tuple-element.55), channel_id=1, source_target_pairs={{0,64},{64,128},{128,192},{192,0},{1,65},{65,129},{129,193},{193,1... | collective-permute-start | bytes 49160 | tf_op jit(solution)/shard_map/close/ppermute | solution.py:283

commit v5 on v4

--- a/solution.py
+++ b/solution.py
@@ -98,9 +98,9 @@
 
 
 def load_kernel(*refs):
-    digits_ref, own_ref, arriving_ref, *refs = refs[2:]
+    index_ref, own_ref, arriving_ref, *refs = refs[2:]
     out_ref = refs[-1]
-    blocks = out_ref.shape[0]
+    blocks = own_ref.shape[0] // 2
     here, groups = lax.axis_index(KZ), len(refs) + 1
     mine = jnp.where(here == 0, own_ref[...].astype(F32), 0.0)
     for ref in refs[:-1]:
@@ -111,10 +111,11 @@
     per = mine.shape[1] // LANES
     for i, part in enumerate((mine[:blocks], mine[blocks:])):
         for c in range(per):
-            out_ref[:, i * per + c, :] = part[:, c * LANES : (c + 1) * LANES]
-    digits = digits_ref[...]
-    for c in range(2 * per):
-        out_ref[:, 2 * per + c, :] = jnp.broadcast_to(digits[c : c + 1], (blocks, LANES))
+            out_ref[pl.ds(i * per + c, blocks, stride=3 * per), :] = part[:, c * LANES : (c + 1) * LANES]
+    index = index_ref[...]
+    for c in range(per):
+        row = jnp.broadcast_to(index[:, c * LANES : (c + 1) * LANES], (blocks, LANES))
+        out_ref[pl.ds(2 * per + c, blocks, stride=3 * per), :] = row
 
 
 def pick_kernel(spread_ref, out_ref, hi_ref, lo_ref):
@@ -122,19 +123,21 @@
     per = width // LANES
 
     def part(i):
-        return jnp.concatenate([spread_ref[:, i * per + c, :] for c in range(per)], axis=1)
+        rows = [spread_ref[pl.ds(i * per + c, blocks, stride=3 * per), :] for c in range(per)]
+        return jnp.concatenate(rows, axis=1)
 
     table = jnp.concatenate([part(0), part(1)], axis=0).astype(BF16)
-    hi_ref[...] = part(2).astype(jnp.int32)
-    lo_ref[...] = part(3)
+    index = part(2).astype(jnp.int32)
+    hi_ref[...] = index // width
+    lo_ref[...] = (index % width).astype(F32)
     rows, owners = iota((width, width), 0).astype(F32).astype(BF16), iota((blocks, width), 0)
     one, zero = jnp.ones((), BF16), jnp.zeros((), BF16)
 
     def step(t, carry):
-        base = pl.multiple_of(t * 8, 8)
-        his, los = hi_ref[pl.ds(base, 8), :], lo_ref[pl.ds(base, 8), :].astype(BF16)
+        base = pl.multiple_of(t * 16, 16)
+        his, los = hi_ref[pl.ds(base, 16), :], lo_ref[pl.ds(base, 16), :].astype(BF16)
         real_rows, imag_rows = [], []
-        for r in range(8):
+        for r in range(16):
             hot = jnp.where(rows == los[r : r + 1, :], one, zero)
             found = jnp.dot(table, hot, preferred_element_type=F32)
             mine = owners == his[r : r + 1, :]
@@ -143,10 +146,10 @@
         for i, picked in enumerate((real_rows, imag_rows)):
             picked = jnp.concatenate(picked, axis=0)
             for c in range(per):
-                out_ref[pl.ds(base, 8), i * per + c, :] = picked[:, c * LANES : (c + 1) * LANES]
+                out_ref[pl.ds(base, 16), i * per + c, :] = picked[:, c * LANES : (c + 1) * LANES]
         return carry
 
-    lax.fori_loop(0, blocks // 8, step, 0)
+    lax.fori_loop(0, blocks // 16, step, 0)
 
 
 def fold_kernel(*refs):
@@ -302,7 +305,6 @@
             flops=4 * rows * bands * bands,
         )
         dealt = [dealt[0]] + [sent(dealt[j], [(0, j)]) for j in range(n_kz - 2, 0, -1)]
-        digits = jnp.stack([pw_map[0] // rows, pw_map[0] % rows]).astype(F32).reshape(-1, LANES)
 
     with jax.named_scope("inner"):
         arriving = around(first, n_kz - 1)
@@ -320,10 +322,11 @@
 
     with jax.named_scope("deal"):
         (load,) = call(
-            load_kernel, "load", [((n_pw, 4 * rows // LANES, LANES), F32)], (digits, dealt[0], arriving, *dealt[1:]),
+            load_kernel, "load", [((n_pw * 3 * rows // LANES, LANES), F32)],
+            (pw_map.astype(F32), dealt[0], arriving, *dealt[1:]),
             after=(early[0], late[0]),
         )
-        spread = swap(load, PW)
+        spread = swap(load.reshape(n_pw, 1, -1), PW).reshape(load.shape)
     with jax.named_scope("pick"):
         (picked,) = call(
             pick_kernel, "pick", [((n_pw, 2 * rows // LANES, LANES), F32)], (spread,),

time: 97.5 us -> 96.5 us (0.990)
  starting transfers between devices: 39 us -> 40.2 us
  transfers between devices with their start and end apart: 16 -> 16, of which waited for: 5 -> 5; matrix products, arithmetic and copies ran while one was open for 0% -> 0% of each run, Pallas kernels for 7% -> 6%
where the time goes in v5:
time: 96.5 us; the launch traced here: 96.1 us
  starting transfers between devices  40.2 us (42%)
  blocking collectives  25 us (26%)
  waiting for transfers between devices  19.6 us (20%)
  Pallas kernels  9.15 us (9%)
  local copies, waits for them, and re-layouts  1.37 us (1%)
    all_to_all x2, blocking collectives, swap(): return lax.all_to_all(x, axes, 0, 0, tiled=True)  25 us
    ppermute x8, starting transfers between devices, sent(): return lax.ppermute(x, KZ, pairs)  18.8 us
    all_to_all x2, starting transfers between devices, swap(): return lax.all_to_all(x, axes, 0, 0, tiled=True)  16.4 us
    all_to_all x2, waiting for transfers between devices, swap(): return lax.all_to_all(x, axes, 0, 0, tiled=True)  10.6 us
    pallas_call x11, Pallas kernels, call(): pl.pallas_call(kernel, out_shape=outs, in_specs=[AFTER] * len(after) + [V...  9.15 us
    ppermute x8, waiting for transfers between devices, sent(): return lax.ppermute(x, KZ, pairs)  8.99 us
    ppermute x2, starting transfers between devices, mirrored(): return lax.ppermute(x, 'x', [(i, n_x - 1 - i) for i in range(n_x)])  3.43 us
  transfers between devices with their start and end apart: 16, of which 5 were waited for; matrix products, arithmetic and copies ran while one was open for 0% of the time, Pallas kernels for 6%

profile of v5, /device:TPU:1, one launch (start us, length us, event | category | flops | bytes accessed | tf_op | source)
XLA Modules:
  0.0 96.1 jit_solution(12499912729223021312)
XLA Ops:
  0.6 1.4 %copy.13 = bf16[4,1,256,2,256]{4,2,3,0,1:T(8,128)(2,1)S(1)} copy(bf16[4,1,256,2,256]{4,3,2,1,0:T(2,128)(2,1)} %param.2) | data formatting | bytes 2097152 | tf_op args[0]
  2.0 0.4 deal.1
  2.4 3.3 %collective-permute-start.3 = (bf16[2,256,256]{2,1,0:T(8,128)(2,1)S(1)}, bf16[2,256,256]{2,1,0:T(8,128)(2,1)S(1)}, u32[]{:S(2)}, u32[]{:S(2)}) collective-permute-start(bf16[2,256,256]{2,1,0:T(8,128)(2,1)S(1)} %get-tuple-element.36), channel_id=1, source_target_pairs={{0,192},{64,0},{128,64},{192,128},{1,193},{65,1},{129,65},{193,129... | collective-permute-start | bytes 786440 | tf_op jit(solution)/shard_map/inner/ppermute | solution.py:286
  5.7 0.7 collective-permute-start.1
  6.3 1.3 %collective-permute-start.2 = (bf16[128,256]{1,0:T(8,128)(2,1)S(1)}, bf16[128,256]{1,0:T(8,128)(2,1)S(1)}, u32[]{:S(2)}, u32[]{:S(2)}) collective-permute-start(bf16[128,256]{1,0:T(8,128)(2,1)S(1)} %get-tuple-element.35), channel_id=1, source_target_pairs={{0,64},{1,65},{2,66},{3,67},{4,68},{5,69},{6,70},{7,71},{8,72},{9,... | collective-permute-start | bytes 196616 | tf_op jit(solution)/shard_map/deal/ppermute | solution.py:286
  7.6 0.6 terms.2
  8.2 0.1 collective-permute-start
  8.3 0.0 collective-permute-done.1.refs_0_.refs_5_
  8.3 2.8 %collective-permute-done.2.refs_1_.refs_6_ = bf16[128,256]{1,0:T(8,128)(2,1)S(1)} collective-permute-done((bf16[128,256]{1,0:T(8,128)(2,1)S(1)}, bf16[128,256]{1,0:T(8,128)(2,1)S(1)}, u32[]{:S(2)}, u32[]{:S(2)}) %collective-permute-start.2) | collective-permute-done | bytes 65568 | tf_op jit(solution)/shard_map/deal/ppermute | solution.py:286
  11.1 0.0 collective-permute-done.3.refs_3_.refs_4_
  11.1 1.4 %terms.3 = (f32[32,32,128]{2,1,0:T(8,128)S(1)}, f32[32,32,128]{2,1,0:T(8,128)}) custom-call(bf16[128,256]{1,0:T(8,128)(2,1)S(1)} %collective-permute-done.1.refs_0_.refs_5_, bf16[128,256]{1,0:T(8,128)(2,1)S(1)} %collective-permute-done.2.refs_1_.refs_6_, bf16[4,2,256,256]{3,2,1,0:T(8,128)(2,1)S(1)} %bitcast.17, ...), custom_call_target="tpu_custom_call" | custom-call | flops 268435456 | bytes 2621440 | tf_op jit(solution)/shard_map/inner/terms/pallas_call | solution.py:39
  12.5 0.0 copy-start
  12.5 1.0 %collective-permute-start.4 = (f32[32,32,128]{2,1,0:T(8,128)}, f32[32,32,128]{2,1,0:T(8,128)S(1)}, u32[]{:S(2)}, u32[]{:S(2)}) collective-permute-start(f32[32,32,128]{2,1,0:T(8,128)} %get-tuple-element.38), channel_id=1, source_target_pairs={{0,8},{8,0},{1,9},{9,1},{2,10},{10,2},{3,11},{11,3},{4,12},{12,4},... | collective-permute-start | bytes 1572872 | tf_op jit(solution)/shard_map/inner/ppermute | solution.py:293
  13.5 0.0 copy-done
  13.5 0.9 load.1
  14.4 12.0 %all-to-all-start = ((f32[64,1,768]{2,1,0:T(1,128)}), f32[64,1,768]{2,1,0:T(1,128)S(1)}, u32[]{:S(2)}, u32[]{:S(2)}) async-start(f32[64,1,768]{2,1,0:T(1,128)} %bitcast.3), calls=%async_computation | async-start | bytes 393216 | tf_op jit(solution)/shard_map/deal/all_to_all | solution.py:283
  26.4 0.0 collective-permute-done.refs_1_
  26.5 0.0 collective-permute-done.4.refs_3_
  26.5 0.9 fold.2
  27.4 2.4 %collective-permute-start.6 = (f32[16,32,128]{2,1,0:T(8,128)}, f32[16,32,128]{2,1,0:T(8,128)S(1)}, u32[]{:S(2)}, u32[]{:S(2)}) collective-permute-start(f32[16,32,128]{2,1,0:T(8,128)} %get-tuple-element.42), channel_id=1, source_target_pairs={{0,48},{16,32},{32,16},{48,0},{1,49},{17,33},{33,17},{49,1},{2,50}... | collective-permute-start | bytes 786440 | tf_op jit(solution)/shard_map/inner/ppermute | solution.py:299
  29.8 0.0 collective-permute-start.7
  29.8 0.7 collective-permute-start.5
  30.5 6.4 %all-to-all-done = f32[64,1,768]{2,1,0:T(1,128)S(1)} async-done(((f32[64,1,768]{2,1,0:T(1,128)}), f32[64,1,768]{2,1,0:T(1,128)S(1)}, u32[]{:S(2)}, u32[]{:S(2)}) %all-to-all-start) | async-done | bytes 196640 | tf_op jit(solution)/shard_map/deal/all_to_all | solution.py:283
  36.9 2.3 %pick.1.refs_0_ = f32[64,4,128]{2,1,0:T(4,128)S(1)} custom-call(f32[384,128]{1,0:T(8,128)S(1)} %bitcast.20), custom_call_target="tpu_custom_call" | custom-call | flops 1073741824 | bytes 393216 | tf_op jit(solution)/shard_map/pick/pick/pallas_call | solution.py:39
  39.2 0.0 collective-permute-done.6.refs_2_
  39.3 0.0 collective-permute-done.7.refs_4_
  39.3 0.1 fold.3
  39.3 0.5 collective-permute-start.8
  39.8 1.0 %collective-permute-start.9 = (f32[8,32,128]{2,1,0:T(8,128)S(1)}, f32[8,32,128]{2,1,0:T(8,128)S(1)}, u32[]{:S(2)}, u32[]{:S(2)}) collective-permute-start(f32[8,32,128]{2,1,0:T(8,128)S(1)} %get-tuple-element.48), channel_id=1, source_target_pairs={{0,48},{16,32},{32,16},{48,0},{1,49},{17,33},{33,17},{49,1},{2,50}... | collective-permute-start | bytes 393224 | tf_op jit(solution)/shard_map/inner/ppermute | solution.py:299
  40.8 9.0 %all_to_all.20.picked_ref = f32[64,4,128]{2,1,0:T(4,128)S(1)} all-to-all(f32[64,4,128]{2,1,0:T(4,128)S(1)} %pick.1.refs_0_), channel_id=1, replica_groups=mesh['y_hi'=2,'core'=2,'x'=4,'y_lo'=2,'z'=8] {'x','y_lo'}, dimensions={0} | all-to-all | bytes 262144 | tf_op jit(solution)/shard_map/pick/all_to_all | solution.py:283
  49.8 0.0 collective-permute-done.5.over_ref
  49.8 0.0 collective-permute-done.8.refs_1_
  49.8 0.0 collective-permute-done.9.refs_3_
  49.8 0.8 merge.1
  50.7 4.3 %all-to-all-start.2 = ((f32[8,96,128]{2,1,0:T(8,128)}), f32[8,96,128]{2,1,0:T(8,128)S(1)}, u32[]{:S(2)}, u32[]{:S(2)}) async-start(f32[8,96,128]{2,1,0:T(8,128)} %get-tuple-element.49), calls=%async_computation.2 | async-start | bytes 786432 | tf_op jit(solution)/shard_map/inner/all_to_all | solution.py:283
  55.0 1.3 %collective-permute-start.10 = (bf16[2,256,256]{2,1,0:T(8,128)(2,1)S(1)}, bf16[2,256,256]{2,1,0:T(8,128)(2,1)S(1)}, u32[]{:S(2)}, u32[]{:S(2)}) collective-permute-start(bf16[2,256,256]{2,1,0:T(8,128)(2,1)S(1)} %get-tuple-element.50.own_ref), channel_id=1, source_target_pairs={{0,64},{192,128},{1,65},{193,129},{2,66},{194,130},{3,67},{195,131... | collective-permute-start | bytes 786440 | tf_op jit(solution)/shard_map/inner/ppermute | solution.py:286
  56.3 5.3 %collective-permute-done.10.other_ref = bf16[2,256,256]{2,1,0:T(8,128)(2,1)S(1)} collective-permute-done((bf16[2,256,256]{2,1,0:T(8,128)(2,1)S(1)}, bf16[2,256,256]{2,1,0:T(8,128)(2,1)S(1)}, u32[]{:S(2)}, u32[]{:S(2)}) %collective-permute-start.10) | collective-permute-done | bytes 262176 | tf_op jit(solution)/shard_map/inner/ppermute | solution.py:286
  61.6 4.2 %all-to-all-done.2.got_ref = f32[8,96,128]{2,1,0:T(8,128)S(1)} async-done(((f32[8,96,128]{2,1,0:T(8,128)}), f32[8,96,128]{2,1,0:T(8,128)S(1)}, u32[]{:S(2)}, u32[]{:S(2)}) %all-to-all-start.2) | async-done | bytes 393248 | tf_op jit(solution)/shard_map/inner/all_to_all | solution.py:283
  65.8 0.7 edge.1
  66.4 16.0 %all_to_all.21 = f32[64,1,1152]{2,1,0:T(1,128)S(1)} all-to-all(f32[64,1,1152]{2,1,0:T(1,128)S(1)} %bitcast.19), channel_id=1, replica_groups=mesh['y_hi'=2,'core'=2,'x'=4,'y_lo'=2,'z'=8] {'x','y_lo','z'}, dimensions={0} | all-to-all | bytes 589824 | tf_op jit(solution)/shard_map/edge/all_to_all | solution.py:283
  82.4 0.6 gather.1
  83.0 7.4 %collective-permute-start.12 = (f32[24,256]{1,0:T(8,128)S(1)}, f32[24,256]{1,0:T(8,128)S(1)}, u32[]{:S(2)}, u32[]{:S(2)}) collective-permute-start(f32[24,256]{1,0:T(8,128)S(1)} %get-tuple-element.56), channel_id=1, source_target_pairs={{64,192},{128,0},{65,193},{129,1},{66,194},{130,2},{67,195},{131,3... | collective-permute-start | bytes 73736 | tf_op jit(solution)/shard_map/close/ppermute | solution.py:286
  90.3 1.6 %collective-permute-start.13 = (f32[24,256]{1,0:T(8,128)S(1)}, f32[24,256]{1,0:T(8,128)S(1)}, u32[]{:S(2)}, u32[]{:S(2)}) collective-permute-start(f32[24,256]{1,0:T(8,128)S(1)} %get-tuple-element.57), channel_id=1, source_target_pairs={{0,192},{64,0},{1,193},{65,1},{2,194},{66,2},{3,195},{67,3},{4,196... | collective-permute-start | bytes 73736 | tf_op jit(solution)/shard_map/close/ppermute | solution.py:286
  92.0 2.6 %collective-permute-start.11 = (f32[16,256]{1,0:T(8,128)S(1)}, f32[16,256]{1,0:T(8,128)S(1)}, u32[]{:S(2)}, u32[]{:S(2)}) collective-permute-start(f32[16,256]{1,0:T(8,128)S(1)} %get-tuple-element.55), channel_id=1, source_target_pairs={{0,64},{64,128},{128,192},{192,0},{1,65},{65,129},{129,193},{193,1... | collective-permute-start | bytes 49160 | tf_op jit(solution)/shard_map/close/ppermute | solution.py:286
  94.5 0.9 collective-permute-done.11.refs_1_
  95.4 0.0 collective-permute-done.12.refs_2_
  95.4 0.0 collective-permute-done.13.refs_3_
  95.4 0.6 close.1
  (1 shorter events, 0.0 us)
Async XLA Ops:
  2.4 8.7 %collective-permute-start.3 = (bf16[2,256,256]{2,1,0:T(8,128)(2,1)S(1)}, bf16[2,256,256]{2,1,0:T(8,128)(2,1)S(1)}, u32[]{:S(2)}, u32[]{:S(2)}) collective-permute-start(bf16[2,256,256]{2,1,0:T(8,128)(2,1)S(1)} %get-tuple-element.36), channel_id=1, source_target_pairs={{0,192},{64,0},{128,64},{192,128},{1,193},{65,1},{129,65},{193,129... | collective-permute-start | bytes 786440 | tf_op jit(solution)/shard_map/inner/ppermute | solution.py:286
  5.7 2.6 %collective-permute-start.1 = (bf16[128,256]{1,0:T(8,128)(2,1)S(1)}, bf16[128,256]{1,0:T(8,128)(2,1)S(1)}, u32[]{:S(2)}, u32[]{:S(2)}) collective-permute-start(bf16[128,256]{1,0:T(8,128)(2,1)S(1)} %get-tuple-element.34), channel_id=1, source_target_pairs={{0,128},{1,129},{2,130},{3,131},{4,132},{5,133},{6,134},{7,135},{8... | collective-permute-start | bytes 196616 | tf_op jit(solution)/shard_map/deal/ppermute | solution.py:286
  6.3 4.7 %collective-permute-start.2 = (bf16[128,256]{1,0:T(8,128)(2,1)S(1)}, bf16[128,256]{1,0:T(8,128)(2,1)S(1)}, u32[]{:S(2)}, u32[]{:S(2)}) collective-permute-start(bf16[128,256]{1,0:T(8,128)(2,1)S(1)} %get-tuple-element.35), channel_id=1, source_target_pairs={{0,64},{1,65},{2,66},{3,67},{4,68},{5,69},{6,70},{7,71},{8,72},{9,... | collective-permute-start | bytes 196616 | tf_op jit(solution)/shard_map/deal/ppermute | solution.py:286
  8.2 18.2 %collective-permute-start = (f32[32,32,128]{2,1,0:T(8,128)S(1)}, f32[32,32,128]{2,1,0:T(8,128)S(1)}, u32[]{:S(2)}, u32[]{:S(2)}) collective-permute-start(f32[32,32,128]{2,1,0:T(8,128)S(1)} %get-tuple-element.33), channel_id=1, source_target_pairs={{0,16},{16,0},{32,48},{48,32},{1,17},{17,1},{33,49},{49,33},{2,18}... | collective-permute-start | bytes 1572872 | tf_op jit(solution)/shard_map/inner/ppermute | solution.py:296
  12.5 1.0 %copy-start = (s32[1,256]{1,0:T(1,128)S(1)}, s32[1,256]{1,0:T(1,128)}, u32[]{:S(2)}) copy-start(s32[1,256]{1,0:T(1,128)} %param.3) | copy-start | bytes 3076
  12.5 14.0 %collective-permute-start.4 = (f32[32,32,128]{2,1,0:T(8,128)}, f32[32,32,128]{2,1,0:T(8,128)S(1)}, u32[]{:S(2)}, u32[]{:S(2)}) collective-permute-start(f32[32,32,128]{2,1,0:T(8,128)} %get-tuple-element.38), channel_id=1, source_target_pairs={{0,8},{8,0},{1,9},{9,1},{2,10},{10,2},{3,11},{11,3},{4,12},{12,4},... | collective-permute-start | bytes 1572872 | tf_op jit(solution)/shard_map/inner/ppermute | solution.py:293
  14.4 22.6 %all-to-all-start = ((f32[64,1,768]{2,1,0:T(1,128)}), f32[64,1,768]{2,1,0:T(1,128)S(1)}, u32[]{:S(2)}, u32[]{:S(2)}) async-start(f32[64,1,768]{2,1,0:T(1,128)} %bitcast.3), calls=%async_computation | async-start | bytes 393216 | tf_op jit(solution)/shard_map/deal/all_to_all | solution.py:283
  27.4 11.8 %collective-permute-start.6 = (f32[16,32,128]{2,1,0:T(8,128)}, f32[16,32,128]{2,1,0:T(8,128)S(1)}, u32[]{:S(2)}, u32[]{:S(2)}) collective-permute-start(f32[16,32,128]{2,1,0:T(8,128)} %get-tuple-element.42), channel_id=1, source_target_pairs={{0,48},{16,32},{32,16},{48,0},{1,49},{17,33},{33,17},{49,1},{2,50}... | collective-permute-start | bytes 786440 | tf_op jit(solution)/shard_map/inner/ppermute | solution.py:299
  29.8 9.4 %collective-permute-start.7 = (f32[16,32,128]{2,1,0:T(8,128)}, f32[16,32,128]{2,1,0:T(8,128)S(1)}, u32[]{:S(2)}, u32[]{:S(2)}) collective-permute-start(f32[16,32,128]{2,1,0:T(8,128)} %get-tuple-element.44), channel_id=1, source_target_pairs={{0,16},{16,0},{32,48},{48,32},{1,17},{17,1},{33,49},{49,33},{2,18}... | collective-permute-start | bytes 786440 | tf_op jit(solution)/shard_map/inner/ppermute | solution.py:296
  29.8 20.0 %collective-permute-start.5 = (bf16[2,256,256]{2,1,0:T(8,128)(2,1)S(1)}, bf16[2,256,256]{2,1,0:T(8,128)(2,1)S(1)}, u32[]{:S(2)}, u32[]{:S(2)}) collective-permute-start(bf16[2,256,256]{2,1,0:T(8,128)(2,1)S(1)} %get-tuple-element.39.final_ref), channel_id=1, source_target_pairs={{192,0},{193,1},{194,2},{195,3},{196,4},{197,5},{198,6},{199,7},{2... | collective-permute-start | bytes 786440 | tf_op jit(solution)/shard_map/inner/ppermute | solution.py:286
  39.3 10.5 %collective-permute-start.8 = (f32[8,32,128]{2,1,0:T(8,128)S(1)}, f32[8,32,128]{2,1,0:T(8,128)S(1)}, u32[]{:S(2)}, u32[]{:S(2)}) collective-permute-start(f32[8,32,128]{2,1,0:T(8,128)S(1)} %get-tuple-element.46), channel_id=1, source_target_pairs={{0,8},{8,0},{1,9},{9,1},{2,10},{10,2},{3,11},{11,3},{4,12},{12,4},... | collective-permute-start | bytes 393224 | tf_op jit(solution)/shard_map/inner/ppermute | solution.py:293
  39.8 10.0 %collective-permute-start.9 = (f32[8,32,128]{2,1,0:T(8,128)S(1)}, f32[8,32,128]{2,1,0:T(8,128)S(1)}, u32[]{:S(2)}, u32[]{:S(2)}) collective-permute-start(f32[8,32,128]{2,1,0:T(8,128)S(1)} %get-tuple-element.48), channel_id=1, source_target_pairs={{0,48},{16,32},{32,16},{48,0},{1,49},{17,33},{33,17},{49,1},{2,50}... | collective-permute-start | bytes 393224 | tf_op jit(solution)/shard_map/inner/ppermute | solution.py:299
  50.7 15.1 %all-to-all-start.2 = ((f32[8,96,128]{2,1,0:T(8,128)}), f32[8,96,128]{2,1,0:T(8,128)S(1)}, u32[]{:S(2)}, u32[]{:S(2)}) async-start(f32[8,96,128]{2,1,0:T(8,128)} %get-tuple-element.49), calls=%async_computation.2 | async-start | bytes 786432 | tf_op jit(solution)/shard_map/inner/all_to_all | solution.py:283
  55.0 6.6 %collective-permute-start.10 = (bf16[2,256,256]{2,1,0:T(8,128)(2,1)S(1)}, bf16[2,256,256]{2,1,0:T(8,128)(2,1)S(1)}, u32[]{:S(2)}, u32[]{:S(2)}) collective-permute-start(bf16[2,256,256]{2,1,0:T(8,128)(2,1)S(1)} %get-tuple-element.50.own_ref), channel_id=1, source_target_pairs={{0,64},{192,128},{1,65},{193,129},{2,66},{194,130},{3,67},{195,131... | collective-permute-start | bytes 786440 | tf_op jit(solution)/shard_map/inner/ppermute | solution.py:286
  83.0 12.4 %collective-permute-start.12 = (f32[24,256]{1,0:T(8,128)S(1)}, f32[24,256]{1,0:T(8,128)S(1)}, u32[]{:S(2)}, u32[]{:S(2)}) collective-permute-start(f32[24,256]{1,0:T(8,128)S(1)} %get-tuple-element.56), channel_id=1, source_target_pairs={{64,192},{128,0},{65,193},{129,1},{66,194},{130,2},{67,195},{131,3... | collective-permute-start | bytes 73736 | tf_op jit(solution)/shard_map/close/ppermute | solution.py:286
  90.3 5.1 %collective-permute-start.13 = (f32[24,256]{1,0:T(8,128)S(1)}, f32[24,256]{1,0:T(8,128)S(1)}, u32[]{:S(2)}, u32[]{:S(2)}) collective-permute-start(f32[24,256]{1,0:T(8,128)S(1)} %get-tuple-element.57), channel_id=1, source_target_pairs={{0,192},{64,0},{1,193},{65,1},{2,194},{66,2},{3,195},{67,3},{4,196... | collective-permute-start | bytes 73736 | tf_op jit(solution)/shard_map/close/ppermute | solution.py:286
  92.0 3.5 %collective-permute-start.11 = (f32[16,256]{1,0:T(8,128)S(1)}, f32[16,256]{1,0:T(8,128)S(1)}, u32[]{:S(2)}, u32[]{:S(2)}) collective-permute-start(f32[16,256]{1,0:T(8,128)S(1)} %get-tuple-element.55), channel_id=1, source_target_pairs={{0,64},{64,128},{128,192},{192,0},{1,65},{65,129},{129,193},{193,1... | collective-permute-start | bytes 49160 | tf_op jit(solution)/shard_map/close/ppermute | solution.py:286

commit v6 on v5

--- a/solution.py
+++ b/solution.py
@@ -366,7 +366,7 @@
         back = swap(out.reshape(n_pw, 1, 9 * LANES), PW).reshape(n_pw * 9, LANES)
 
     with jax.named_scope("close"):
-        pieces = [((4 * share, bands), F32)] * 2 + [((6 * share, bands), F32)] * (n_kz - 2)
+        pieces = [((3 * share, bands), F32)] * 2 + [((4 * share, bands), F32)] * (n_kz - 2)
         minus, *pieces = call(gather_kernel, "gather", [rows_out] + pieces, (back,))
         for d in (2, 3, 1):
             pieces[d] = around(pieces[d], d, None if d == 1 else (0, n_kz - 1))

time: 96.5 us -> 96.5 us (level)
  no operation moved by 1% of the time
where the time goes in v6:
time: 96.5 us; the launch traced here: 96.1 us
  starting transfers between devices  40.2 us (42%)
  blocking collectives  25 us (26%)
  waiting for transfers between devices  19.6 us (20%)
  Pallas kernels  9.15 us (9%)
  local copies, waits for them, and re-layouts  1.37 us (1%)
    all_to_all x2, blocking collectives, swap(): return lax.all_to_all(x, axes, 0, 0, tiled=True)  25 us
    ppermute x8, starting transfers between devices, sent(): return lax.ppermute(x, KZ, pairs)  18.8 us
    all_to_all x2, starting transfers between devices, swap(): return lax.all_to_all(x, axes, 0, 0, tiled=True)  16.4 us
    all_to_all x2, waiting for transfers between devices, swap(): return lax.all_to_all(x, axes, 0, 0, tiled=True)  10.6 us
    pallas_call x11, Pallas kernels, call(): pl.pallas_call(kernel, out_shape=outs, in_specs=[AFTER] * len(after) + [V...  9.15 us
    ppermute x8, waiting for transfers between devices, sent(): return lax.ppermute(x, KZ, pairs)  8.99 us
    ppermute x2, starting transfers between devices, mirrored(): return lax.ppermute(x, 'x', [(i, n_x - 1 - i) for i in range(n_x)])  3.43 us
  transfers between devices with their start and end apart: 16, of which 5 were waited for; matrix products, arithmetic and copies ran while one was open for 0% of the time, Pallas kernels for 6%

profile of v6, /device:TPU:1, one launch (start us, length us, event | category | flops | bytes accessed | tf_op | source)
XLA Modules:
  0.0 96.1 jit_solution(18050866534898508020)
XLA Ops:
  0.6 1.4 %copy.13 = bf16[4,1,256,2,256]{4,2,3,0,1:T(8,128)(2,1)S(1)} copy(bf16[4,1,256,2,256]{4,3,2,1,0:T(2,128)(2,1)} %param.2) | data formatting | bytes 2097152 | tf_op args[0]
  2.0 0.4 deal.1
  2.4 3.3 %collective-permute-start.3 = (bf16[2,256,256]{2,1,0:T(8,128)(2,1)S(1)}, bf16[2,256,256]{2,1,0:T(8,128)(2,1)S(1)}, u32[]{:S(2)}, u32[]{:S(2)}) collective-permute-start(bf16[2,256,256]{2,1,0:T(8,128)(2,1)S(1)} %get-tuple-element.36), channel_id=1, source_target_pairs={{0,192},{64,0},{128,64},{192,128},{1,193},{65,1},{129,65},{193,129... | collective-permute-start | bytes 786440 | tf_op jit(solution)/shard_map/inner/ppermute | solution.py:286
  5.7 0.7 collective-permute-start.1
  6.3 1.3 %collective-permute-start.2 = (bf16[128,256]{1,0:T(8,128)(2,1)S(1)}, bf16[128,256]{1,0:T(8,128)(2,1)S(1)}, u32[]{:S(2)}, u32[]{:S(2)}) collective-permute-start(bf16[128,256]{1,0:T(8,128)(2,1)S(1)} %get-tuple-element.35), channel_id=1, source_target_pairs={{0,64},{1,65},{2,66},{3,67},{4,68},{5,69},{6,70},{7,71},{8,72},{9,... | collective-permute-start | bytes 196616 | tf_op jit(solution)/shard_map/deal/ppermute | solution.py:286
  7.6 0.6 terms.2
  8.2 0.1 collective-permute-start
  8.3 0.0 collective-permute-done.1.refs_0_.refs_5_
  8.3 2.8 %collective-permute-done.2.refs_1_.refs_6_ = bf16[128,256]{1,0:T(8,128)(2,1)S(1)} collective-permute-done((bf16[128,256]{1,0:T(8,128)(2,1)S(1)}, bf16[128,256]{1,0:T(8,128)(2,1)S(1)}, u32[]{:S(2)}, u32[]{:S(2)}) %collective-permute-start.2) | collective-permute-done | bytes 65568 | tf_op jit(solution)/shard_map/deal/ppermute | solution.py:286
  11.1 0.0 collective-permute-done.3.refs_3_.refs_4_
  11.1 1.4 %terms.3 = (f32[32,32,128]{2,1,0:T(8,128)S(1)}, f32[32,32,128]{2,1,0:T(8,128)}) custom-call(bf16[128,256]{1,0:T(8,128)(2,1)S(1)} %collective-permute-done.1.refs_0_.refs_5_, bf16[128,256]{1,0:T(8,128)(2,1)S(1)} %collective-permute-done.2.refs_1_.refs_6_, bf16[4,2,256,256]{3,2,1,0:T(8,128)(2,1)S(1)} %bitcast.17, ...), custom_call_target="tpu_custom_call" | custom-call | flops 268435456 | bytes 2621440 | tf_op jit(solution)/shard_map/inner/terms/pallas_call | solution.py:39
  12.5 0.0 copy-start
  12.5 1.0 %collective-permute-start.4 = (f32[32,32,128]{2,1,0:T(8,128)}, f32[32,32,128]{2,1,0:T(8,128)S(1)}, u32[]{:S(2)}, u32[]{:S(2)}) collective-permute-start(f32[32,32,128]{2,1,0:T(8,128)} %get-tuple-element.38), channel_id=1, source_target_pairs={{0,8},{8,0},{1,9},{9,1},{2,10},{10,2},{3,11},{11,3},{4,12},{12,4},... | collective-permute-start | bytes 1572872 | tf_op jit(solution)/shard_map/inner/ppermute | solution.py:293
  13.5 0.0 copy-done
  13.5 0.9 load.1
  14.4 12.0 %all-to-all-start = ((f32[64,1,768]{2,1,0:T(1,128)}), f32[64,1,768]{2,1,0:T(1,128)S(1)}, u32[]{:S(2)}, u32[]{:S(2)}) async-start(f32[64,1,768]{2,1,0:T(1,128)} %bitcast.3), calls=%async_computation | async-start | bytes 393216 | tf_op jit(solution)/shard_map/deal/all_to_all | solution.py:283
  26.4 0.0 collective-permute-done.refs_1_
  26.5 0.0 collective-permute-done.4.refs_3_
  26.5 0.9 fold.2
  27.4 2.4 %collective-permute-start.6 = (f32[16,32,128]{2,1,0:T(8,128)}, f32[16,32,128]{2,1,0:T(8,128)S(1)}, u32[]{:S(2)}, u32[]{:S(2)}) collective-permute-start(f32[16,32,128]{2,1,0:T(8,128)} %get-tuple-element.42), channel_id=1, source_target_pairs={{0,48},{16,32},{32,16},{48,0},{1,49},{17,33},{33,17},{49,1},{2,50}... | collective-permute-start | bytes 786440 | tf_op jit(solution)/shard_map/inner/ppermute | solution.py:299
  29.8 0.0 collective-permute-start.7
  29.8 0.7 collective-permute-start.5
  30.5 6.4 %all-to-all-done = f32[64,1,768]{2,1,0:T(1,128)S(1)} async-done(((f32[64,1,768]{2,1,0:T(1,128)}), f32[64,1,768]{2,1,0:T(1,128)S(1)}, u32[]{:S(2)}, u32[]{:S(2)}) %all-to-all-start) | async-done | bytes 196640 | tf_op jit(solution)/shard_map/deal/all_to_all | solution.py:283
  36.9 2.3 %pick.1.refs_0_ = f32[64,4,128]{2,1,0:T(4,128)S(1)} custom-call(f32[384,128]{1,0:T(8,128)S(1)} %bitcast.20), custom_call_target="tpu_custom_call" | custom-call | flops 1073741824 | bytes 393216 | tf_op jit(solution)/shard_map/pick/pick/pallas_call | solution.py:39
  39.2 0.0 collective-permute-done.6.refs_2_
  39.3 0.0 collective-permute-done.7.refs_4_
  39.3 0.1 fold.3
  39.3 0.5 collective-permute-start.8
  39.8 1.0 %collective-permute-start.9 = (f32[8,32,128]{2,1,0:T(8,128)S(1)}, f32[8,32,128]{2,1,0:T(8,128)S(1)}, u32[]{:S(2)}, u32[]{:S(2)}) collective-permute-start(f32[8,32,128]{2,1,0:T(8,128)S(1)} %get-tuple-element.48), channel_id=1, source_target_pairs={{0,48},{16,32},{32,16},{48,0},{1,49},{17,33},{33,17},{49,1},{2,50}... | collective-permute-start | bytes 393224 | tf_op jit(solution)/shard_map/inner/ppermute | solution.py:299
  40.8 9.0 %all_to_all.20.picked_ref = f32[64,4,128]{2,1,0:T(4,128)S(1)} all-to-all(f32[64,4,128]{2,1,0:T(4,128)S(1)} %pick.1.refs_0_), channel_id=1, replica_groups=mesh['y_hi'=2,'core'=2,'x'=4,'y_lo'=2,'z'=8] {'x','y_lo'}, dimensions={0} | all-to-all | bytes 262144 | tf_op jit(solution)/shard_map/pick/all_to_all | solution.py:283
  49.8 0.0 collective-permute-done.5.over_ref
  49.8 0.0 collective-permute-done.8.refs_1_
  49.8 0.0 collective-permute-done.9.refs_3_
  49.8 0.8 merge.1
  50.7 4.3 %all-to-all-start.2 = ((f32[8,96,128]{2,1,0:T(8,128)}), f32[8,96,128]{2,1,0:T(8,128)S(1)}, u32[]{:S(2)}, u32[]{:S(2)}) async-start(f32[8,96,128]{2,1,0:T(8,128)} %get-tuple-element.49), calls=%async_computation.2 | async-start | bytes 786432 | tf_op jit(solution)/shard_map/inner/all_to_all | solution.py:283
  55.0 1.3 %collective-permute-start.10 = (bf16[2,256,256]{2,1,0:T(8,128)(2,1)S(1)}, bf16[2,256,256]{2,1,0:T(8,128)(2,1)S(1)}, u32[]{:S(2)}, u32[]{:S(2)}) collective-permute-start(bf16[2,256,256]{2,1,0:T(8,128)(2,1)S(1)} %get-tuple-element.50.own_ref), channel_id=1, source_target_pairs={{0,64},{192,128},{1,65},{193,129},{2,66},{194,130},{3,67},{195,131... | collective-permute-start | bytes 786440 | tf_op jit(solution)/shard_map/inner/ppermute | solution.py:286
  56.3 5.3 %collective-permute-done.10.other_ref = bf16[2,256,256]{2,1,0:T(8,128)(2,1)S(1)} collective-permute-done((bf16[2,256,256]{2,1,0:T(8,128)(2,1)S(1)}, bf16[2,256,256]{2,1,0:T(8,128)(2,1)S(1)}, u32[]{:S(2)}, u32[]{:S(2)}) %collective-permute-start.10) | collective-permute-done | bytes 262176 | tf_op jit(solution)/shard_map/inner/ppermute | solution.py:286
  61.6 4.2 %all-to-all-done.2.got_ref = f32[8,96,128]{2,1,0:T(8,128)S(1)} async-done(((f32[8,96,128]{2,1,0:T(8,128)}), f32[8,96,128]{2,1,0:T(8,128)S(1)}, u32[]{:S(2)}, u32[]{:S(2)}) %all-to-all-start.2) | async-done | bytes 393248 | tf_op jit(solution)/shard_map/inner/all_to_all | solution.py:283
  65.8 0.7 edge.1
  66.4 16.0 %all_to_all.21 = f32[64,1,1152]{2,1,0:T(1,128)S(1)} all-to-all(f32[64,1,1152]{2,1,0:T(1,128)S(1)} %bitcast.19), channel_id=1, replica_groups=mesh['y_hi'=2,'core'=2,'x'=4,'y_lo'=2,'z'=8] {'x','y_lo','z'}, dimensions={0} | all-to-all | bytes 589824 | tf_op jit(solution)/shard_map/edge/all_to_all | solution.py:283
  82.4 0.6 gather.1
  83.0 7.4 %collective-permute-start.12 = (f32[16,256]{1,0:T(8,128)S(1)}, f32[16,256]{1,0:T(8,128)S(1)}, u32[]{:S(2)}, u32[]{:S(2)}) collective-permute-start(f32[16,256]{1,0:T(8,128)S(1)} %get-tuple-element.56), channel_id=1, source_target_pairs={{64,192},{128,0},{65,193},{129,1},{66,194},{130,2},{67,195},{131,3... | collective-permute-start | bytes 49160 | tf_op jit(solution)/shard_map/close/ppermute | solution.py:286
  90.3 1.6 %collective-permute-start.13 = (f32[16,256]{1,0:T(8,128)S(1)}, f32[16,256]{1,0:T(8,128)S(1)}, u32[]{:S(2)}, u32[]{:S(2)}) collective-permute-start(f32[16,256]{1,0:T(8,128)S(1)} %get-tuple-element.57), channel_id=1, source_target_pairs={{0,192},{64,0},{1,193},{65,1},{2,194},{66,2},{3,195},{67,3},{4,196... | collective-permute-start | bytes 49160 | tf_op jit(solution)/shard_map/close/ppermute | solution.py:286
  92.0 2.6 %collective-permute-start.11 = (f32[12,256]{1,0:T(8,128)S(1)}, f32[12,256]{1,0:T(8,128)S(1)}, u32[]{:S(2)}, u32[]{:S(2)}) collective-permute-start(f32[12,256]{1,0:T(8,128)S(1)} %get-tuple-element.55), channel_id=1, source_target_pairs={{0,64},{64,128},{128,192},{192,0},{1,65},{65,129},{129,193},{193,1... | collective-permute-start | bytes 36872 | tf_op jit(solution)/shard_map/close/ppermute | solution.py:286
  94.5 0.9 collective-permute-done.11.refs_1_
  95.4 0.0 collective-permute-done.12.refs_2_
  95.4 0.0 collective-permute-done.13.refs_3_
  95.4 0.6 close.1
  (1 shorter events, 0.0 us)
Async XLA Ops:
  2.4 8.7 %collective-permute-start.3 = (bf16[2,256,256]{2,1,0:T(8,128)(2,1)S(1)}, bf16[2,256,256]{2,1,0:T(8,128)(2,1)S(1)}, u32[]{:S(2)}, u32[]{:S(2)}) collective-permute-start(bf16[2,256,256]{2,1,0:T(8,128)(2,1)S(1)} %get-tuple-element.36), channel_id=1, source_target_pairs={{0,192},{64,0},{128,64},{192,128},{1,193},{65,1},{129,65},{193,129... | collective-permute-start | bytes 786440 | tf_op jit(solution)/shard_map/inner/ppermute | solution.py:286
  5.7 2.6 %collective-permute-start.1 = (bf16[128,256]{1,0:T(8,128)(2,1)S(1)}, bf16[128,256]{1,0:T(8,128)(2,1)S(1)}, u32[]{:S(2)}, u32[]{:S(2)}) collective-permute-start(bf16[128,256]{1,0:T(8,128)(2,1)S(1)} %get-tuple-element.34), channel_id=1, source_target_pairs={{0,128},{1,129},{2,130},{3,131},{4,132},{5,133},{6,134},{7,135},{8... | collective-permute-start | bytes 196616 | tf_op jit(solution)/shard_map/deal/ppermute | solution.py:286
  6.3 4.7 %collective-permute-start.2 = (bf16[128,256]{1,0:T(8,128)(2,1)S(1)}, bf16[128,256]{1,0:T(8,128)(2,1)S(1)}, u32[]{:S(2)}, u32[]{:S(2)}) collective-permute-start(bf16[128,256]{1,0:T(8,128)(2,1)S(1)} %get-tuple-element.35), channel_id=1, source_target_pairs={{0,64},{1,65},{2,66},{3,67},{4,68},{5,69},{6,70},{7,71},{8,72},{9,... | collective-permute-start | bytes 196616 | tf_op jit(solution)/shard_map/deal/ppermute | solution.py:286
  8.2 18.2 %collective-permute-start = (f32[32,32,128]{2,1,0:T(8,128)S(1)}, f32[32,32,128]{2,1,0:T(8,128)S(1)}, u32[]{:S(2)}, u32[]{:S(2)}) collective-permute-start(f32[32,32,128]{2,1,0:T(8,128)S(1)} %get-tuple-element.33), channel_id=1, source_target_pairs={{0,16},{16,0},{32,48},{48,32},{1,17},{17,1},{33,49},{49,33},{2,18}... | collective-permute-start | bytes 1572872 | tf_op jit(solution)/shard_map/inner/ppermute | solution.py:296
  12.5 1.0 %copy-start = (s32[1,256]{1,0:T(1,128)S(1)}, s32[1,256]{1,0:T(1,128)}, u32[]{:S(2)}) copy-start(s32[1,256]{1,0:T(1,128)} %param.3) | copy-start | bytes 3076
  12.5 14.0 %collective-permute-start.4 = (f32[32,32,128]{2,1,0:T(8,128)}, f32[32,32,128]{2,1,0:T(8,128)S(1)}, u32[]{:S(2)}, u32[]{:S(2)}) collective-permute-start(f32[32,32,128]{2,1,0:T(8,128)} %get-tuple-element.38), channel_id=1, source_target_pairs={{0,8},{8,0},{1,9},{9,1},{2,10},{10,2},{3,11},{11,3},{4,12},{12,4},... | collective-permute-start | bytes 1572872 | tf_op jit(solution)/shard_map/inner/ppermute | solution.py:293
  14.4 22.6 %all-to-all-start = ((f32[64,1,768]{2,1,0:T(1,128)}), f32[64,1,768]{2,1,0:T(1,128)S(1)}, u32[]{:S(2)}, u32[]{:S(2)}) async-start(f32[64,1,768]{2,1,0:T(1,128)} %bitcast.3), calls=%async_computation | async-start | bytes 393216 | tf_op jit(solution)/shard_map/deal/all_to_all | solution.py:283
  27.4 11.8 %collective-permute-start.6 = (f32[16,32,128]{2,1,0:T(8,128)}, f32[16,32,128]{2,1,0:T(8,128)S(1)}, u32[]{:S(2)}, u32[]{:S(2)}) collective-permute-start(f32[16,32,128]{2,1,0:T(8,128)} %get-tuple-element.42), channel_id=1, source_target_pairs={{0,48},{16,32},{32,16},{48,0},{1,49},{17,33},{33,17},{49,1},{2,50}... | collective-permute-start | bytes 786440 | tf_op jit(solution)/shard_map/inner/ppermute | solution.py:299
  29.8 9.4 %collective-permute-start.7 = (f32[16,32,128]{2,1,0:T(8,128)}, f32[16,32,128]{2,1,0:T(8,128)S(1)}, u32[]{:S(2)}, u32[]{:S(2)}) collective-permute-start(f32[16,32,128]{2,1,0:T(8,128)} %get-tuple-element.44), channel_id=1, source_target_pairs={{0,16},{16,0},{32,48},{48,32},{1,17},{17,1},{33,49},{49,33},{2,18}... | collective-permute-start | bytes 786440 | tf_op jit(solution)/shard_map/inner/ppermute | solution.py:296
  29.8 20.0 %collective-permute-start.5 = (bf16[2,256,256]{2,1,0:T(8,128)(2,1)S(1)}, bf16[2,256,256]{2,1,0:T(8,128)(2,1)S(1)}, u32[]{:S(2)}, u32[]{:S(2)}) collective-permute-start(bf16[2,256,256]{2,1,0:T(8,128)(2,1)S(1)} %get-tuple-element.39.final_ref), channel_id=1, source_target_pairs={{192,0},{193,1},{194,2},{195,3},{196,4},{197,5},{198,6},{199,7},{2... | collective-permute-start | bytes 786440 | tf_op jit(solution)/shard_map/inner/ppermute | solution.py:286
  39.3 10.5 %collective-permute-start.8 = (f32[8,32,128]{2,1,0:T(8,128)S(1)}, f32[8,32,128]{2,1,0:T(8,128)S(1)}, u32[]{:S(2)}, u32[]{:S(2)}) collective-permute-start(f32[8,32,128]{2,1,0:T(8,128)S(1)} %get-tuple-element.46), channel_id=1, source_target_pairs={{0,8},{8,0},{1,9},{9,1},{2,10},{10,2},{3,11},{11,3},{4,12},{12,4},... | collective-permute-start | bytes 393224 | tf_op jit(solution)/shard_map/inner/ppermute | solution.py:293
  39.8 10.0 %collective-permute-start.9 = (f32[8,32,128]{2,1,0:T(8,128)S(1)}, f32[8,32,128]{2,1,0:T(8,128)S(1)}, u32[]{:S(2)}, u32[]{:S(2)}) collective-permute-start(f32[8,32,128]{2,1,0:T(8,128)S(1)} %get-tuple-element.48), channel_id=1, source_target_pairs={{0,48},{16,32},{32,16},{48,0},{1,49},{17,33},{33,17},{49,1},{2,50}... | collective-permute-start | bytes 393224 | tf_op jit(solution)/shard_map/inner/ppermute | solution.py:299
  50.7 15.1 %all-to-all-start.2 = ((f32[8,96,128]{2,1,0:T(8,128)}), f32[8,96,128]{2,1,0:T(8,128)S(1)}, u32[]{:S(2)}, u32[]{:S(2)}) async-start(f32[8,96,128]{2,1,0:T(8,128)} %get-tuple-element.49), calls=%async_computation.2 | async-start | bytes 786432 | tf_op jit(solution)/shard_map/inner/all_to_all | solution.py:283
  55.0 6.6 %collective-permute-start.10 = (bf16[2,256,256]{2,1,0:T(8,128)(2,1)S(1)}, bf16[2,256,256]{2,1,0:T(8,128)(2,1)S(1)}, u32[]{:S(2)}, u32[]{:S(2)}) collective-permute-start(bf16[2,256,256]{2,1,0:T(8,128)(2,1)S(1)} %get-tuple-element.50.own_ref), channel_id=1, source_target_pairs={{0,64},{192,128},{1,65},{193,129},{2,66},{194,130},{3,67},{195,131... | collective-permute-start | bytes 786440 | tf_op jit(solution)/shard_map/inner/ppermute | solution.py:286
  83.0 12.4 %collective-permute-start.12 = (f32[16,256]{1,0:T(8,128)S(1)}, f32[16,256]{1,0:T(8,128)S(1)}, u32[]{:S(2)}, u32[]{:S(2)}) collective-permute-start(f32[16,256]{1,0:T(8,128)S(1)} %get-tuple-element.56), channel_id=1, source_target_pairs={{64,192},{128,0},{65,193},{129,1},{66,194},{130,2},{67,195},{131,3... | collective-permute-start | bytes 49160 | tf_op jit(solution)/shard_map/close/ppermute | solution.py:286
  90.3 5.1 %collective-permute-start.13 = (f32[16,256]{1,0:T(8,128)S(1)}, f32[16,256]{1,0:T(8,128)S(1)}, u32[]{:S(2)}, u32[]{:S(2)}) collective-permute-start(f32[16,256]{1,0:T(8,128)S(1)} %get-tuple-element.57), channel_id=1, source_target_pairs={{0,192},{64,0},{1,193},{65,1},{2,194},{66,2},{3,195},{67,3},{4,196... | collective-permute-start | bytes 49160 | tf_op jit(solution)/shard_map/close/ppermute | solution.py:286
  92.0 3.5 %collective-permute-start.11 = (f32[12,256]{1,0:T(8,128)S(1)}, f32[12,256]{1,0:T(8,128)S(1)}, u32[]{:S(2)}, u32[]{:S(2)}) collective-permute-start(f32[12,256]{1,0:T(8,128)S(1)} %get-tuple-element.55), channel_id=1, source_target_pairs={{0,64},{64,128},{128,192},{192,0},{1,65},{65,129},{129,193},{193,1... | collective-permute-start | bytes 36872 | tf_op jit(solution)/shard_map/close/ppermute | solution.py:286
